TPU v7x, 32 devices: a whole 2x2x4 slice. The times are simulated.
32 devices in a mesh: dp: 8 (over y, x, core), tensor: 4 (over z).
Axes of the slice: x: 2, y: 2, z: 4, core: 2. Of those that a mesh axis runs over, the one named last changes fastest.
Arguments:
- tokens: bfloat16 [8192, 768], P(('dp', 'tensor')), may hold values from -6 to 6
- gain_one: float32 [768], replicated, may hold values from 0.25 to 1.75
- shift_one: float32 [768], replicated, may hold values from -1.5 to 1.5
- qkv_weight: bfloat16 [768, 3, 768], P('dp', None, 'tensor'), may hold values from -0.3125 to 0.3125
- qkv_bias: float32 [3, 768], P(None, 'tensor'), may hold values from -1.5 to 1.5
- out_weight: bfloat16 [768, 768], P('tensor', 'dp'), may hold values from -0.875 to 0.875
- out_bias: float32 [768], replicated, may hold values from -1.5 to 1.5
- gain_two: float32 [768], replicated, may hold values from 0.25 to 1.75
- shift_two: float32 [768], replicated, may hold values from -1.5 to 1.5
- up_weight: bfloat16 [768, 3072], P('dp', 'tensor'), may hold values from -0.21875 to 0.21875
- up_bias: float32 [3072], P('tensor'), may hold values from -1.5 to 1.5
- down_weight: bfloat16 [3072, 768], P('tensor', 'dp'), may hold values from -0.15625 to 0.15625
- down_bias: float32 [768], replicated, may hold values from -1.5 to 1.5
- cotangent: bfloat16 [8192, 768], P(('dp', 'tensor')), may hold values from -6 to 6
Outputs:
- output: bfloat16 [8192, 768], P(('dp', 'tensor'))
- grad_tokens: float32 [8192, 768], P(('dp', 'tensor'))
- grad_gain_one: float32 [768], replicated
- grad_shift_one: float32 [768], replicated
- grad_qkv_weight: float32 [768, 3, 768], P('dp', None, 'tensor')
- grad_qkv_bias: float32 [3, 768], P(None, 'tensor')
- grad_out_weight: float32 [768, 768], P('tensor', 'dp')
- grad_out_bias: float32 [768], replicated
- grad_gain_two: float32 [768], replicated
- grad_shift_two: float32 [768], replicated
- grad_up_weight: float32 [768, 3072], P('dp', 'tensor')
- grad_up_bias: float32 [3072], P('tensor')
- grad_down_weight: float32 [3072, 768], P('tensor', 'dp')
- grad_down_bias: float32 [768], replicated
All inputs are finite; a program needn't handle non-finite values.
Results may differ from a plain program's by a relative error of at most 0.018.
Values may be sent and summed in bfloat16 or wider, within the bound.
No kernel may reach another device: no remote copies, remote signals or barrier semaphores. Data moves between devices by JAX's collectives and lax.ppermute only.
A program may use at most 128 MiB of HBM per device.

v0:
```python
import jax
import jax.numpy as jnp
from jax import lax
from jax.experimental import pallas as pl
from jax.experimental.pallas import tpu as pltpu
from jax.sharding import PartitionSpec as P

HEAD_DIM = 64
EPS = 1e-05
BF = jnp.bfloat16
F32 = jnp.float32
AXES = ("dp", "tensor")


def dot_nn(left, right):
    return lax.dot_general(left, right, (((1,), (0,)), ((), ())), preferred_element_type=F32)


def dot_nt(left, right):
    return lax.dot_general(left, right, (((1,), (1,)), ((), ())), preferred_element_type=F32)


def dot_tn(left, right):
    return lax.dot_general(left, right, (((0,), (0,)), ((), ())), preferred_element_type=F32)


class Plan:
    def __init__(self):
        self.n_dp = lax.axis_size("dp")
        self.n_t = lax.axis_size("tensor")
        assert self.n_t == 4 and self.n_dp % 2 == 0
        self.n_k = self.n_dp // 2
        assert self.n_k & (self.n_k - 1) == 0
        self.d = lax.axis_index("dp")
        self.t = lax.axis_index("tensor")
        self.k = self.d // 2
        self.c = self.d % 2
        self.h = self.t // 2
        self.r = jnp.where(self.c == self.h, self.t, self.t ^ 2)
        self.j = self.c + 2 * (self.t % 2)

    def send(self, value, where):
        pairs = []
        for d in range(self.n_dp):
            for t in range(self.n_t):
                to_d, to_t = where(d, t)
                pairs.append((d * self.n_t + t, to_d * self.n_t + to_t))
        return lax.ppermute(value, AXES, pairs)

    def swap_home(self, value):
        return self.send(value, lambda d, t: (d, t) if d % 2 == t // 2 else (d ^ 1, t ^ 2))

    def over_z(self, value):
        return self.send(value, lambda d, t: (d, t ^ 1))

    def over_core(self, value):
        return self.send(value, lambda d, t: (d ^ 1, t))

    def over_plane(self, value, p):
        return self.send(value, lambda d, t: (d ^ (2 * p), t))

    def group_gather(self, value):
        mine = jnp.stack([value, self.over_z(value)])
        return mine, self.over_core(mine)

    def group_sum(self, first, second):
        pair = first + self.over_core(second).astype(F32)
        return pair[0] + self.over_z(pair[1].astype(BF)).astype(F32)

    def spread(self, shard):
        got = []
        for i in (0, 1):
            got.append(
                self.send(
                    shard, lambda d, t, i=i: (2 * (d // 2) + t % 2, t // 2 + 2 * ((d % 2) ^ i))
                )
            )
        return got

    def to_slot(self, value):
        return self.send(value, lambda d, t: (2 * (d // 2) + t % 2, t // 2 + 2 * (d % 2)))

    def unspread(self, chunk):
        total = 0.0
        for i in (0, 1):
            part = lax.dynamic_index_in_dim(chunk, self.h ^ i, 0, keepdims=False)
            got = self.send(
                part, lambda d, t, i=i: (2 * (d // 2) + ((t // 2) ^ i), d % 2 + 2 * (t % 2))
            )
            total = total + got.astype(F32)
        return total

    def plane_gather(self, value):
        if self.n_k == 4:
            return jnp.stack([value] + [self.over_plane(value, p) for p in (1, 2, 3)])
        held = value[None]
        size = 1
        while size < self.n_k:
            held = jnp.concatenate([held, self.over_plane(held, size)])
            size *= 2
        return held

    def plane_sum(self, value):
        pick = lambda p: lax.dynamic_index_in_dim(value, self.k ^ p, 0, keepdims=False)
        if self.n_k == 4:
            total = pick(0).astype(F32)
            for p in (1, 2, 3):
                total = total + self.over_plane(pick(p).astype(BF), p).astype(F32)
            return total
        held = jnp.stack([pick(p) for p in range(self.n_k)]).astype(F32)
        size = self.n_k // 2
        while size:
            held = held[:size] + self.over_plane(held[size:].astype(BF), size).astype(F32)
            size //= 2
        return held[0]

    def ordered_weight(self, held):
        flat = held.reshape((self.n_dp,) + held.shape[2:])
        parts = []
        for d in range(self.n_dp):
            at = ((d // 2) ^ self.k) * 2 + ((d % 2) ^ self.h)
            parts.append(lax.dynamic_index_in_dim(flat, at, 0, keepdims=False))
        return jnp.concatenate(parts, 0)

    def ordered_rows(self, first, second):
        flat = jnp.concatenate([first, second])
        return jnp.concatenate(
            [lax.dynamic_index_in_dim(flat, a ^ self.r, 0, keepdims=False) for a in range(4)], 0
        )

    def relative_rows(self, value):
        rows = value.reshape((4, -1) + value.shape[1:])
        return [lax.dynamic_index_in_dim(rows, i ^ self.r, 0, keepdims=False) for i in range(4)]

    def chip_sum(self, value):
        value = value + self.over_core(value)
        p = 1
        while p < self.n_k:
            value = value + self.over_plane(value, p)
            p *= 2
        return value

    def over_two(self, value):
        return self.send(value, lambda d, t: (d, t ^ 2))


def after(value, *earlier):
    return lax.optimization_barrier((value,) + earlier)[0]


PEAK = 1.15e9


def call(body, outs, args, micros, mib, scratch=()):
    shapes = tuple(jax.ShapeDtypeStruct(shape, dtype) for shape, dtype in outs)
    cost = pl.CostEstimate(
        flops=int(micros * PEAK), bytes_accessed=int(micros * 3.0e6), transcendentals=0
    )

    return pl.pallas_call(
        body,
        out_shape=shapes,
        in_specs=[pl.BlockSpec(memory_space=pltpu.SMEM)]
        + [pl.BlockSpec(memory_space=pltpu.VMEM)] * (len(args) - 1),
        out_specs=tuple(pl.BlockSpec(memory_space=pltpu.VMEM) for _ in shapes),
        scratch_shapes=list(scratch),
        compiler_params=pltpu.CompilerParams(vmem_limit_bytes=mib * 2**20),
        cost_estimate=cost,
    )(*args)


def normalise(values):
    middle = jnp.mean(values, -1, keepdims=True)
    centred = values - middle
    variance = jnp.mean(centred * centred, -1, keepdims=True)
    rate = lax.rsqrt(variance + EPS)
    return centred * rate, rate


def norm_back(grad, hat, rate, gain):
    scaled = grad * gain
    first = jnp.mean(scaled, -1, keepdims=True)
    second = jnp.mean(scaled * hat, -1, keepdims=True)
    return rate * (scaled - first - hat * second)


def col_sum(values):
    return jnp.sum(values, 0, keepdims=True)


def chunk_at(ids, i, rows):
    return pl.ds(pl.multiple_of((ids[2] ^ i) * rows, rows), rows)


def order_weight(ids, pieces, scratch, shard):
    if len(pieces) == 1:
        scratch[...] = pieces[0][0]
        return
    for p, piece in enumerate(pieces):
        for i in range(2):
            at = 2 * (ids[0] ^ p) + (ids[1] ^ i)
            scratch[pl.ds(pl.multiple_of(at * shard, shard), shard), :] = piece[i]


def mixed_kernel(n_w, shard, ids, x0, x1, x2, x3, gain, shift, bias, *refs):
    pieces, (normed, mixed, w_all) = refs[:n_w], refs[n_w:]
    order_weight(ids, pieces, w_all, shard)
    wide = mixed.shape[1]
    for i, x in enumerate((x0, x1, x2, x3)):
        rows = x.shape[0]
        hat, _ = normalise(x[...].astype(F32))
        low = (hat * gain[...] + shift[...]).astype(BF)
        normed[chunk_at(ids, i, rows), :] = low
        out = dot_nn(low, w_all[:, :wide]) + bias[...]
        mixed[chunk_at(ids, i, rows), :] = out.astype(BF)


def attend_kernel(ids, mixed, attended, logs):
    length, wide = attended.shape
    block = min(256, length)
    tri = lax.broadcasted_iota(jnp.int32, (block, block), 0) <= lax.broadcasted_iota(
        jnp.int32, (block, block), 1
    )
    for head in range(wide // HEAD_DIM):
        at = head * HEAD_DIM
        q_t = (mixed[:, at : at + HEAD_DIM].astype(F32) * HEAD_DIM ** (-0.5)).T.astype(BF)
        keys = mixed[:, wide + at : wide + at + HEAD_DIM]
        v_t = mixed[:, 2 * wide + at : 2 * wide + at + HEAD_DIM].astype(F32).T.astype(BF)
        for b in range(length // block):
            low = b * block
            q_b = q_t[:, low : low + block]
            near = jnp.where(tri, dot_nn(keys[low : low + block], q_b), -1e30)
            top = jnp.max(near, 0, keepdims=True)
            if b:
                far = dot_nn(keys[:low], q_b)
                top = jnp.maximum(top, jnp.max(far, 0, keepdims=True))
            near = jnp.exp(near - top)
            total = col_sum(near)
            out = dot_nn(v_t[:, low : low + block], near.astype(BF))
            if b:
                far = jnp.exp(far - top)
                total = total + col_sum(far)
                out = out + dot_nn(v_t[:, :low], far.astype(BF))
            out = out * (1.0 / total)
            attended[low : low + block, at : at + HEAD_DIM] = out.T.astype(BF)
            logs[head : head + 1, low : low + block] = top + jnp.log(total)


def forward_kernel(n_w, shard, ids, *refs):
    att, outs, xs = refs[0:4], refs[4:8], refs[8:12]
    out_bias, gain, shift, up_bias = refs[12:16]
    pieces = refs[16 : 16 + n_w]
    hidden_own, normed_two, act, slope, up_w = refs[16 + n_w : 21 + n_w]
    out_w = refs[21 + n_w]
    order_weight(ids, pieces, up_w, shard)
    for g, out in enumerate(outs):
        if n_w == 1:
            out_w[g] = out[0, 0]
        else:
            for p in range(n_w):
                for i in range(2):
                    at = 2 * (ids[0] ^ p) + (ids[1] ^ i)
                    out_w[g, pl.ds(pl.multiple_of(at * shard, shard), shard), :] = out[p, i]
    for i in range(4):
        rows = xs[0].shape[0]
        hidden = xs[i][...].astype(F32) + out_bias[...]
        for g in range(4):
            hidden = hidden + dot_nt(att[g][chunk_at(ids, i, rows), :], out_w[g])
        if i == 0:
            hidden_own[...] = hidden
        hat, _ = normalise(hidden)
        low = (hat * gain[...] + shift[...]).astype(BF)
        span = slice(i * rows, (i + 1) * rows)
        normed_two[span, :] = low
        up = dot_nn(low, up_w[...]) + up_bias[...]
        whole = 0.5 * (1.0 + lax.erf(up * 0.5**0.5))
        act[span, :] = (up * whole).astype(BF)
        bell = jnp.exp(-0.5 * up * up) * (2.0 * jnp.pi) ** (-0.5)
        slope[span, :] = (whole + up * bell).astype(BF)


def backward_kernel(n_w, shard, ids, *refs):
    pieces = refs[:n_w]
    g0, g1, g2, g3, slope, up_w = refs[n_w : n_w + 6]
    grad_up, own, after_one, second, bias_grad, down_t = refs[n_w + 6 :]
    rows = g0.shape[0]
    units = slope.shape[1]
    order_weight(ids, pieces, down_t, shard)
    bias_sum = jnp.zeros((1, units), F32)
    for i, g in enumerate((g0, g1, g2, g3)):
        span = slice(i * rows, (i + 1) * rows)
        grad = (dot_nn(g[...], down_t[...]) * slope[span, :].astype(F32)).astype(BF)
        grad_up[span, :] = grad
        bias_sum = bias_sum + col_sum(grad.astype(F32))
        put_part(i, dot_nt(grad, up_w[...]), own, after_one, second)
    bias_grad[...] = bias_sum


def put_part(i, value, own, after_one, second):
    if i == 0:
        own[...] = value
    elif i == 1:
        after_one[...] = value
    else:
        second[i - 2] = value.astype(BF)


def mlp_grad_kernel(n_o, shard, ids, normed_two, g0, g1, g2, g3, act, grad_up, *refs):
    outs, scratch = refs[:n_o], refs[n_o]
    units = act.shape[1]
    rows = g0.shape[0]
    scratch[:, :units] = dot_tn(normed_two[...], grad_up[...])
    total = 0.0
    for i, g in enumerate((g0, g1, g2, g3)):
        total = total + dot_tn(g[...], act[i * rows : (i + 1) * rows, :])
    scratch[:, units:] = total
    emit_grad(ids, scratch, outs, shard)


def emit_grad(ids, scratch, outs, shard):
    if len(outs) == 1:
        outs[0][...] = scratch[...]
        return
    for p, out in enumerate(outs):
        at = pl.ds(pl.multiple_of((ids[0] ^ p) * 2 * shard, 2 * shard), 2 * shard)
        out[...] = scratch[at, :].astype(out.dtype)


def mlp_out_kernel(ids, act, down_t, own, after_one, second):
    rows = own.shape[0]
    for i in range(4):
        out = dot_nt(act[i * rows : (i + 1) * rows, :], down_t[...])
        put_part(i, out, own, after_one, second)


def norm_two_kernel(ids, own, got_core, got_z, hidden, g, gain, grad_hidden, low, sums):
    grad = own[...] + got_core[0].astype(F32) + got_z[...].astype(F32)
    hat, rate = normalise(hidden[...])
    g32 = g[...].astype(F32)
    total = g32 + norm_back(grad, hat, rate, gain[...])
    grad_hidden[...] = total
    low[...] = total.astype(BF)
    sums[0:1, :] = col_sum(total)
    sums[1:2, :] = col_sum(grad * hat)
    sums[2:3, :] = col_sum(grad)
    sums[3:4, :] = col_sum(g32)


def norm_one_kernel(ids, own, got_core, got_z, x, gain, grad_hidden, out):
    grad = own[...] + got_core[0].astype(F32) + got_z[...].astype(F32)
    hat, rate = normalise(x[...].astype(F32))
    total = grad_hidden[...] + norm_back(grad, hat, rate, gain[...])
    out[...] = total.astype(BF)


def attend_back_kernel(ids, mixed, logs, w_all, gh0, gh1, gh2, gh3, x0, x1, x2, x3, *refs):
    sums_two, up_bias, grad_mixed, own, after_one, second, small, g_rows, gm32 = refs
    length, wide3 = mixed.shape
    wide = wide3 // 3
    rows = x0.shape[0]
    block = min(256, length)
    for i, gh in enumerate((gh0, gh1, gh2, gh3)):
        g_rows[chunk_at(ids, i, rows), :] = dot_nn(gh[...], w_all[:, wide3:])
    tri = lax.broadcasted_iota(jnp.int32, (block, block), 0) <= lax.broadcasted_iota(
        jnp.int32, (block, block), 1
    )
    for head in range(wide // HEAD_DIM):
        at = head * HEAD_DIM
        scaled = mixed[:, at : at + HEAD_DIM].astype(F32) * HEAD_DIM ** (-0.5)
        q_rows = scaled.astype(BF)
        q_t = scaled.T.astype(BF)
        keys = mixed[:, wide + at : wide + at + HEAD_DIM]
        k_t = keys.astype(F32).T.astype(BF)
        values = mixed[:, 2 * wide + at : 2 * wide + at + HEAD_DIM]
        grad32 = g_rows[:, at : at + HEAD_DIM]
        grad_rows = grad32.astype(BF)
        grad_t = grad32.T.astype(BF)
        for b in range(length // block):
            low, end = b * block, (b + 1) * block
            q_b = q_t[:, low:end]
            g_b = grad_t[:, low:end]
            log = logs[head : head + 1, low:end]
            near = jnp.where(tri, jnp.exp(dot_nn(keys[low:end], q_b) - log), 0.0)
            near_d = dot_nn(values[low:end], g_b)
            inner = col_sum(near * near_d)
            if b:
                far = jnp.exp(dot_nn(keys[:low], q_b) - log)
                far_d = dot_nn(values[:low], g_b)
                inner = inner + col_sum(far * far_d)
            near_s = (near * (near_d - inner)).astype(BF)
            grad_q = dot_nn(k_t[:, low:end], near_s)
            gm32[low:end, HEAD_DIM : 2 * HEAD_DIM] = dot_nn(near_s, q_rows[low:end])
            gm32[low:end, 2 * HEAD_DIM :] = dot_nn(near.astype(BF), grad_rows[low:end])
            if b:
                far_s = (far * (far_d - inner)).astype(BF)
                grad_q = grad_q + dot_nn(k_t[:, :low], far_s)
                gm32[:low, HEAD_DIM : 2 * HEAD_DIM] += dot_nn(far_s, q_rows[low:end])
                gm32[:low, 2 * HEAD_DIM :] += dot_nn(far.astype(BF), grad_rows[low:end])
            gm32[low:end, :HEAD_DIM] = grad_q.T * HEAD_DIM ** (-0.5)
        for part in range(3):
            grad_mixed[:, part * wide + at : part * wide + at + HEAD_DIM] = gm32[
                :, part * HEAD_DIM : (part + 1) * HEAD_DIM
            ].astype(BF)
    bias_grad = col_sum(grad_mixed[...].astype(F32))
    gain_sum = jnp.zeros((1, x0.shape[1]), F32)
    shift_sum = gain_sum
    for i, x in enumerate((x0, x1, x2, x3)):
        back = dot_nt(grad_mixed[chunk_at(ids, i, rows), :], w_all[:, :wide3])
        hat, _ = normalise(x[...].astype(F32))
        gain_sum = gain_sum + col_sum(back * hat)
        shift_sum = shift_sum + col_sum(back)
        put_part(i, back, own, after_one, second)
    small[...] = jnp.zeros(small.shape, F32)
    small[0:1, :] = gain_sum
    small[1:2, :] = shift_sum
    small[2:6, :] = sums_two[0:4, :]
    small[pl.ds(6 + 2 * ids[3], 1), :wide3] = bias_grad
    small[pl.ds(7 + 2 * ids[3], 1), : up_bias.shape[1]] = up_bias[...]


def attn_grad_kernel(n_o, shard, ids, normed, grad_mixed, gh0, gh1, gh2, gh3, attended, *refs):
    outs, scratch = refs[:n_o], refs[n_o]
    wide3 = grad_mixed.shape[1]
    rows = gh0.shape[0]
    scratch[:, :wide3] = dot_tn(normed[...], grad_mixed[...])
    total = 0.0
    for i, gh in enumerate((gh0, gh1, gh2, gh3)):
        total = total + dot_tn(gh[...], attended[chunk_at(ids, i, rows), :])
    scratch[:, wide3:] = total
    emit_grad(ids, scratch, outs, shard)


def local(
    tokens,
    gain_one,
    shift_one,
    qkv_weight,
    qkv_bias,
    out_weight,
    out_bias,
    gain_two,
    shift_two,
    up_weight,
    up_bias,
    down_weight,
    down_bias,
    cotangent,
):
    plan = Plan()
    rows, width = tokens.shape
    shard = qkv_weight.shape[0]
    wide = qkv_weight.shape[2]
    wide3 = 3 * wide
    units = up_weight.shape[1]
    length = 4 * rows
    n_k = plan.n_k
    direct = n_k == 4 and shard % 16 == 0
    n_w = n_k if direct else 1
    n_o = n_k if direct else 1
    ids = jnp.stack([plan.k, plan.h, plan.r, plan.j]).astype(jnp.int32)
    row = lambda v: v.reshape(1, -1)
    row_gain_one, row_shift_one = row(gain_one), row(shift_one)
    row_gain_two, row_shift_two = row(gain_two), row(shift_two)

    def plane_pieces(value):
        if direct:
            return [value] + [plan.over_plane(value, p) for p in (1, 2, 3)]
        return [plan.ordered_weight(plan.plane_gather(value))[None]]

    def plane_got(pieces):
        return [plan.over_plane(pieces[p], p) for p in (1, 2, 3)] if direct else []

    def plane_total(pieces, got, *earlier):
        if direct:
            total = after(pieces[0], *earlier)
            for value in got:
                total = total + value.astype(F32)
            return total
        return plan.plane_sum(pieces[0].reshape((n_k, 2 * shard) + pieces[0].shape[1:]))

    def grad_outs(n):
        if direct:
            return [((2 * shard, n), F32)] + [((2 * shard, n), BF)] * (n_k - 1)
        return [((width, n), F32)]

    def parts():
        return [((rows, width), F32), ((rows, width), F32), ((2, rows, width), BF)]

    def toward_z(after_one, got_core):
        return (after_one + got_core[1].astype(F32)).astype(BF)

    x0 = plan.swap_home(tokens)
    attn_shard = jnp.concatenate([qkv_weight.reshape(shard, wide3), out_weight.T], 1)
    attn_spread = jnp.stack(plan.spread(attn_shard))
    biases = plan.to_slot(jnp.concatenate([qkv_bias.reshape(-1), up_bias]))
    qkv_bias_j, up_bias_j = row(biases[:wide3]), row(biases[wide3:])
    x1 = plan.over_z(x0)
    x2 = plan.over_core(x0)
    x3 = plan.over_core(x1)
    attn_w = plane_pieces(attn_spread)

    mlp_shard = jnp.concatenate([up_weight, down_weight.T], 1)
    mlp_spread = plan.spread(after(mlp_shard, attn_w[-1], x0))
    up_stack = jnp.stack([piece[:, :units] for piece in mlp_spread])
    down_stack = jnp.stack([piece[:, units:] for piece in mlp_spread])

    normed, mixed, w_all = call(
        lambda *refs: mixed_kernel(n_w, shard, *refs),
        [((length, width), BF), ((length, wide3), BF), ((width, width), BF)],
        [ids, x0, x1, x2, x3, row_gain_one, row_shift_one, qkv_bias_j] + attn_w,
        3,
        11,
    )
    out_t = jnp.stack([piece[..., wide3:] for piece in attn_w])
    out_z = plan.over_z(after(out_t, mixed))
    outs = [out_t, out_z, plan.over_core(out_t), plan.over_core(out_z)]
    g0 = plan.swap_home(after(cotangent, x1))
    up_pieces = plane_pieces(up_stack)

    attended, logs = call(
        attend_kernel,
        [((length, wide), BF), ((8, length), F32)],
        [ids, mixed],
        6,
        10,
    )
    att_z = plan.over_z(after(attended, g0, *up_pieces))
    down_pieces = plane_pieces(after(down_stack, attended))
    att_last = after(att_z, *outs, *down_pieces[1:])
    att = [attended, att_z, plan.over_core(attended), plan.over_core(att_last)]
    g1 = plan.over_z(after(g0, att_z))

    hidden_own, normed_two, act, slope, up_j = call(
        lambda *refs: forward_kernel(n_w, shard, *refs),
        [
            ((rows, width), F32),
            ((length, width), BF),
            ((length, units), BF),
            ((length, units), BF),
            ((width, units), BF),
        ],
        [ids]
        + att
        + outs
        + [x0, x1, x2, x3]
        + [row(out_bias), row_gain_two, row_shift_two, up_bias_j]
        + up_pieces,
        7,
        22,
        [pltpu.VMEM((4, width, wide), BF)],
    )
    gs = [g0, g1, plan.over_core(g0), plan.over_core(after(g1, slope))]
    grad_up, gn2_own, gn2_one, gn2_second, up_bias_grad, down_t = call(
        lambda *refs: backward_kernel(n_w, shard, *refs),
        [((length, units), BF)] + parts() + [((1, units), F32), ((width, units), BF)],
        [ids] + down_pieces + gs + [slope, up_j],
        5,
        18,
    )
    gn2_core = plan.over_core(gn2_second)
    gn2_z_in = toward_z(gn2_one, gn2_core)
    gn2_z = plan.over_z(gn2_z_in)
    out_own, out_one, out_second = call(
        mlp_out_kernel,
        parts(),
        [ids, act, down_t],
        2,
        12,
    )
    out_core = plan.over_core(out_second)
    out_z_in = toward_z(out_one, out_core)
    mlp_grad = call(
        lambda *refs: mlp_grad_kernel(n_o, shard, *refs),
        grad_outs(2 * units),
        [ids, after(normed_two, gn2_z_in)] + gs + [act, grad_up],
        5,
        22,
        [pltpu.VMEM((width, 2 * units), F32)],
    )
    grad_hidden, gh0, sums_two = call(
        norm_two_kernel,
        [((rows, width), F32), ((rows, width), BF), ((8, width), F32)],
        [ids, gn2_own, gn2_core, gn2_z, after(hidden_own, mlp_grad[-1]), g0, row_gain_two],
        2,
        8,
    )
    gh1 = plan.over_z(gh0)
    mlp_got = plane_got(mlp_grad)
    ghs = [gh0, gh1, plan.over_core(gh0), plan.over_core(after(gh1, *mlp_got[:2]))]
    out_from_z = plan.over_z(after(out_z_in, gh1))
    out_sum = hidden_own + out_own + out_core[0].astype(F32) + out_from_z.astype(F32)
    output_here = (out_sum + down_bias).astype(BF)

    grad_mixed, gn1_own, gn1_one, gn1_second, small = call(
        attend_back_kernel,
        [((length, wide3), BF)] + parts() + [((16, width), F32)],
        [ids, after(mixed, out_z_in), logs, w_all]
        + ghs
        + [x0, x1, x2, x3, sums_two, up_bias_grad],
        12,
        22,
        [pltpu.VMEM((length, wide), F32), pltpu.VMEM((length, 3 * HEAD_DIM), F32)],
    )
    gn1_core = plan.over_core(after(gn1_second, out_from_z, *mlp_got[2:]))
    gn1_z_in = toward_z(gn1_one, gn1_core)
    gn1_z = plan.over_z(gn1_z_in)
    mlp_part = plane_total(mlp_grad, mlp_got, gn1_z_in).astype(BF).reshape(2, shard, 2 * units)
    mlp_summed = plan.unspread(mlp_part)
    attn_grad = call(
        lambda *refs: attn_grad_kernel(n_o, shard, *refs),
        grad_outs(width),
        [ids, after(normed, gn1_z_in), grad_mixed] + ghs + [attended],
        3,
        14,
        [pltpu.VMEM((width, width), F32)],
    )
    small = plan.chip_sum(after(small, gn1_z_in))
    attn_grad = lax.optimization_barrier(tuple(attn_grad) + (mlp_summed, small))[:-2]
    attn_got = plane_got(attn_grad)
    (grad_low,) = call(
        norm_one_kernel,
        [((rows, width), BF)],
        [ids, gn1_own, gn1_core, gn1_z, x0, row_gain_one, grad_hidden],
        2,
        12,
    )
    grad_tokens = plan.swap_home(grad_low).astype(F32)
    output = plan.swap_home(after(output_here, gn1_z_in))

    small = after(small, grad_low)
    small = small + plan.over_z(small)
    attn_total = plane_total(attn_grad, attn_got, small, output)
    attn_part = attn_total.astype(BF).reshape(2, shard, width)
    attn_summed = plan.unspread(after(attn_part, grad_tokens))
    small = small + plan.over_two(small)
    mine = lax.dynamic_slice_in_dim(small, 6 + 2 * plan.t, 2, 0)
    return (
        output,
        grad_tokens,
        small[0],
        small[1],
        attn_summed[:, :wide3].reshape(shard, 3, wide),
        mine[0, :wide3].reshape(3, wide),
        attn_summed[:, wide3:].T,
        small[2],
        small[3],
        small[4],
        mlp_summed[:, :units],
        mine[1, :units],
        mlp_summed[:, units:].T,
        small[5],
    )


def solution(mesh):
    in_specs = (
        P(("dp", "tensor"), None),
        P(),
        P(),
        P("dp", None, "tensor"),
        P(None, "tensor"),
        P("tensor", "dp"),
        P(),
        P(),
        P(),
        P("dp", "tensor"),
        P("tensor"),
        P("tensor", "dp"),
        P(),
        P(("dp", "tensor"), None),
    )
    out_specs = (
        P(("dp", "tensor"), None),
        P(("dp", "tensor"), None),
        P(),
        P(),
        P("dp", None, "tensor"),
        P(None, "tensor"),
        P("tensor", "dp"),
        P(),
        P(),
        P(),
        P("dp", "tensor"),
        P("tensor"),
        P("tensor", "dp"),
        P(),
    )
    return jax.shard_map(local, mesh=mesh, in_specs=in_specs, out_specs=out_specs, check_vma=False)
```

profile of v0, /device:TPU:0, one launch (start us, length us, event | category | flops | bytes accessed | tf_op | source)
XLA Modules:
  0.0 212.2 jit_solution(9529125885210922340)
XLA Ops:
  0.7 1.1 copy.32
  2.0 0.9 copy.33
  3.6 5.8 %collective-permute-start.6 = (bf16[96,768]{1,0:T(8,128)(2,1)S(1)}, bf16[96,768]{1,0:T(8,128)(2,1)S(1)}, u32[]{:S(2)}, u32[]{:S(2)}) collective-permute-start(bf16[96,768]{1,0:T(8,128)(2,1)S(1)} %pad_maximum_fusion.5), channel_id=1, source_target_pairs={{0,2},{1,6},{2,3},{3,7},{4,0},{5,4},{6,1},{7,5},{8,10},{9,14},{10,... | collective-permute-start | bytes 442376 | tf_op jit(solution)/shard_map/ppermute | solution.py:48
  9.4 1.6 collective-permute-start
  13.3 2.5 %collective-permute-start.9 = (bf16[2,96,768]{2,1,0:T(8,128)(2,1)S(1)}, bf16[2,96,768]{2,1,0:T(8,128)(2,1)S(1)}, u32[]{:S(2)}, u32[]{:S(2)}) collective-permute-start(bf16[2,96,768]{2,1,0:T(8,128)(2,1)S(1)} %pad_maximum_fusion.1.refs_8_), channel_id=1, source_target_pairs={{0,24},{1,25},{2,26},{3,27},{4,28},{5,29},{6,30},{7,31},{8,16},{9,... | collective-permute-start | bytes 884744 | tf_op jit(solution)/shard_map/ppermute | solution.py:48
  17.3 12.3 %collective-permute-start.1 = (bf16[256,768]{1,0:T(8,128)(2,1)S(1)}, bf16[256,768]{1,0:T(8,128)(2,1)S(1)}, u32[]{:S(2)}, u32[]{:S(2)}) collective-permute-start(bf16[256,768]{1,0:T(8,128)(2,1)S(1)} %collective-permute-done.refs_1_.refs_9_.x0.x), channel_id=1, source_target_pairs={{0,1},{1,0},{2,3},{3,2},{4,5},{5,4},{6,7},{7,6},{8,9},{9,8},{10,11... | collective-permute-start | bytes 1179656 | tf_op jit(solution)/shard_map/ppermute | solution.py:48
  30.4 6.4 %collective-permute-start.12 = (bf16[96,1536]{1,0:T(8,128)(2,1)S(1)}, bf16[96,1536]{1,0:T(8,128)(2,1)S(1)}, u32[]{:S(2)}, u32[]{:S(2)}) collective-permute-start(bf16[96,1536]{1,0:T(8,128)(2,1)S(1)} %pad_maximum_fusion.2), channel_id=1, source_target_pairs={{0,2},{1,6},{2,3},{3,7},{4,0},{5,4},{6,1},{7,5},{8,10},{9,14},{10,... | collective-permute-start | bytes 884744 | tf_op jit(solution)/shard_map/ppermute | solution.py:48
  37.2 1.7 collective-permute-done.1.refs_2_.refs_10_.x1
  38.9 3.2 %collective-permute-done.12 = bf16[96,1536]{1,0:T(8,128)(2,1)S(1)} collective-permute-done((bf16[96,1536]{1,0:T(8,128)(2,1)S(1)}, bf16[96,1536]{1,0:T(8,128)(2,1)S(1)}, u32[]{:S(2)}, u32[]{:S(2)}) %collective-permute-start.12) | collective-permute-done | bytes 294944 | tf_op jit(solution)/shard_map/ppermute | solution.py:48
  42.7 1.7 collective-permute-start.14
  44.4 1.3 collective-permute-start.15
  46.5 2.5 %shard_map.245 = (bf16[1024,768]{1,0:T(8,128)(2,1)S(1)}, bf16[1024,576]{1,0:T(8,128)(2,1)S(1)}, bf16[768,768]{1,0:T(8,128)(2,1)S(1)}) custom-call(s32[4]{0:T(128)S(1)} %pad_add_fusion.refs_0_.ids, bf16[256,768]{1,0:T(8,128)(2,1)S(1)} %collective-permute-done.refs_1_.refs_9_.x0.x, bf16[256,768]{1,0:T(8,128)(2,1)S(1)} %collective-permute-done.1.refs_2_.refs_10_.x1, ...), custom_call_target="tpu_custom_call" | custom-call | flops 3449999872 | bytes 9000000 | tf_op jit(solution)/shard_map/pallas_call | solution.py:160
  49.1 1.1 copy-done.19
  50.2 1.8 collective-permute-done.13.refs_18_
  52.0 7.1 %collective-permute-start.18 = (bf16[4,2,96,192]{3,2,1,0:T(8,128)(2,1)S(1)}, bf16[4,2,96,192]{3,2,1,0:T(8,128)(2,1)S(1)}, u32[]{:S(2)}, u32[]{:S(2)}) collective-permute-start(bf16[4,2,96,192]{3,2,1,0:T(8,128)(2,1)S(1)} %pad_maximum_fusion.refs_5_), channel_id=1, source_target_pairs={{0,1},{1,0},{2,3},{3,2},{4,5},{5,4},{6,7},{7,6},{8,9},{9,8},{10,11... | collective-permute-start | bytes 884744 | tf_op jit(solution)/shard_map/ppermute | solution.py:48
  59.1 5.5 %shard_map.246 = (bf16[1024,192]{1,0:T(8,128)(2,1)S(1)}, f32[8,1024]{1,0:T(8,128)S(1)}) custom-call(s32[4]{0:T(128)S(1)} %pad_add_fusion.refs_0_.ids, bf16[1024,576]{1,0:T(8,128)(2,1)S(1)} %get-tuple-element.102.mixed), custom_call_target="tpu_custom_call" | custom-call | flops 6899999744 | bytes 18000000 | tf_op jit(solution)/shard_map/pallas_call | solution.py:160
  64.7 1.5 collective-permute-start.21
  66.2 1.3 collective-permute-start.22
  68.3 2.7 %collective-permute-done.18.refs_6_ = bf16[4,2,96,192]{3,2,1,0:T(8,128)(2,1)S(1)} collective-permute-done((bf16[4,2,96,192]{3,2,1,0:T(8,128)(2,1)S(1)}, bf16[4,2,96,192]{3,2,1,0:T(8,128)(2,1)S(1)}, u32[]{:S(2)}, u32[]{:S(2)}) %collective-permute-start.18) | collective-permute-done | bytes 294944 | tf_op jit(solution)/shard_map/ppermute | solution.py:48
  71.3 2.7 %collective-permute-done.21.refs_2_ = bf16[2,96,768]{2,1,0:T(8,128)(2,1)S(1)} collective-permute-done((bf16[2,96,768]{2,1,0:T(8,128)(2,1)S(1)}, bf16[2,96,768]{2,1,0:T(8,128)(2,1)S(1)}, u32[]{:S(2)}, u32[]{:S(2)}) %collective-permute-start.21) | collective-permute-done | bytes 294944 | tf_op jit(solution)/shard_map/ppermute | solution.py:48
  74.0 1.5 collective-permute-start.17
  75.5 5.2 %collective-permute-done.22.refs_3_ = bf16[2,96,768]{2,1,0:T(8,128)(2,1)S(1)} collective-permute-done((bf16[2,96,768]{2,1,0:T(8,128)(2,1)S(1)}, bf16[2,96,768]{2,1,0:T(8,128)(2,1)S(1)}, u32[]{:S(2)}, u32[]{:S(2)}) %collective-permute-start.22) | collective-permute-done | bytes 294944 | tf_op jit(solution)/shard_map/ppermute | solution.py:48
  80.6 1.1 collective-permute-done.23.refs_4_
  82.9 1.3 collective-permute-start.25
  84.2 6.6 %shard_map.247 = (f32[256,768]{1,0:T(8,128)S(1)}, bf16[1024,768]{1,0:T(8,128)(2,1)S(1)}, bf16[1024,768]{1,0:T(8,128)(2,1)S(1)}, bf16[1024,768]{1,0:T(8,128)(2,1)S(1)}, bf16[768,768]{1,0:T(8,128)(2,1)S(1)}) custom-call(s32[4]{0:T(128)S(1)} %pad_add_fusion.refs_0_.ids, bf16[1024,192]{1,0:T(8,128)(2,1)S(1)} %get-tuple-element.78.refs_1_.refs_7_, ...), custom_call_target="tpu_custom_call" | custom-call | flops 8049999872 | bytes 21000000 | tf_op jit(solution)/shard_map/pallas_call | solution.py:160
  90.8 3.2 %collective-permute-done.25.refs_6_.refs_3_ = bf16[256,768]{1,0:T(8,128)(2,1)S(1)} collective-permute-done((bf16[256,768]{1,0:T(8,128)(2,1)S(1)}, bf16[256,768]{1,0:T(8,128)(2,1)S(1)}, u32[]{:S(2)}, u32[]{:S(2)}) %collective-permute-start.25) | collective-permute-done | bytes 393248 | tf_op jit(solution)/shard_map/ppermute | solution.py:48
  94.0 1.7 collective-permute-done.27.refs_8_.refs_5_
  95.7 3.7 %shard_map.248 = (bf16[1024,768]{1,0:T(8,128)(2,1)S(1)}, f32[256,768]{1,0:T(8,128)S(1)}, f32[256,768]{1,0:T(8,128)S(1)}, bf16[2,256,768]{2,1,0:T(8,128)(2,1)S(1)...) custom-call(s32[4]{0:T(128)S(1)} %pad_add_fusion.refs_0_.ids, bf16[2,96,768]{2,1,0:T(8,128)(2,1)S(1)} %pad_maximum_fusion.4.refs_1_, ...), custom_call_target="tpu_custom_call" | custom-call | flops 5750000128 | bytes 15000000 | tf_op jit(solution)/shard_map/pallas_call | solution.py:160
  99.6 2.0 shard_map.249
  102.1 1.3 collective-permute-start.30
  103.5 3.5 %shard_map.250 = (f32[192,1536]{1,0:T(8,128)S(1)}, bf16[192,1536]{1,0:T(8,128)(2,1)S(1)}, bf16[192,1536]{1,0:T(8,128)(2,1)S(1)}, bf16[192,1536]{1,0:T(8,128)(2,1)S(1)}) custom-call(s32[4]{0:T(128)S(1)} %pad_add_fusion.refs_0_.ids, bf16[1024,768]{1,0:T(8,128)(2,1)S(1)} %get-tuple-element.96.refs_1_, ...), custom_call_target="tpu_custom_call" | custom-call | flops 5750000128 | bytes 15000000 | tf_op jit(solution)/shard_map/pallas_call | solution.py:160
  107.7 1.7 collective-permute-start.35
  109.4 4.0 %collective-permute-done.30.got_z = bf16[256,768]{1,0:T(8,128)(2,1)S(1)} collective-permute-done((bf16[256,768]{1,0:T(8,128)(2,1)S(1)}, bf16[256,768]{1,0:T(8,128)(2,1)S(1)}, u32[]{:S(2)}, u32[]{:S(2)}) %collective-permute-start.30) | collective-permute-done | bytes 393248 | tf_op jit(solution)/shard_map/ppermute | solution.py:48
  113.4 1.3 shard_map.251
  114.7 0.9 copy-done.15
  115.6 1.3 collective-permute-start.31
  116.8 5.3 %collective-permute-done.34 = bf16[192,1536]{1,0:T(8,128)(2,1)S(1)} collective-permute-done((bf16[192,1536]{1,0:T(8,128)(2,1)S(1)}, bf16[192,1536]{1,0:T(8,128)(2,1)S(1)}, u32[]{:S(2)}, u32[]{:S(2)}) %collective-permute-start.34) | collective-permute-done | bytes 589856 | tf_op jit(solution)/shard_map/ppermute | solution.py:48
  123.0 2.9 %collective-permute-done.31.gh1.refs_4_ = bf16[256,768]{1,0:T(8,128)(2,1)S(1)} collective-permute-done((bf16[256,768]{1,0:T(8,128)(2,1)S(1)}, bf16[256,768]{1,0:T(8,128)(2,1)S(1)}, u32[]{:S(2)}, u32[]{:S(2)}) %collective-permute-start.31) | collective-permute-done | bytes 393248 | tf_op jit(solution)/shard_map/ppermute | solution.py:48
  125.9 2.1 collective-permute-start.37
  128.1 1.1 collective-permute-start.32
  129.2 12.1 %shard_map.252 = (bf16[1024,576]{1,0:T(8,128)(2,1)S(1)}, f32[256,768]{1,0:T(8,128)S(1)}, f32[256,768]{1,0:T(8,128)S(1)}, bf16[2,256,768]{2,1,0:T(8,128)(2,1)}, f32[16,768]{1,0:T(8,128)S(1)}) custom-call(s32[4]{0:T(128)S(1)} %pad_add_fusion.refs_0_.ids, bf16[1024,576]{1,0:T(8,128)(2,1)S(1)} %get-tuple-element.102.mixed, ...), custom_call_target="tpu_custom_call" | custom-call | flops 13799999488 | bytes 36000000 | tf_op jit(solution)/shard_map/pallas_call | solution.py:160
  141.9 0.9 copy-done.17
  142.8 1.1 copy-done.21
  143.9 0.9 copy-done.28
  144.8 2.1 fusion.5
  147.4 1.1 fusion
  148.4 1.1 collective-permute-start.40
  152.2 2.5 %collective-permute-start.48 = (bf16[96,1536]{1,0:T(8,128)(2,1)S(1)}, bf16[96,1536]{1,0:T(8,128)(2,1)S(1)}, u32[]{:S(2)}, u32[]{:S(2)}) collective-permute-start(bf16[96,1536]{1,0:T(8,128)(2,1)S(1)} %get-tuple-element.158), channel_id=1, source_target_pairs={{0,4},{1,6},{2,0},{3,2},{4,5},{5,7},{6,1},{7,3},{8,12},{9,14},{10,... | collective-permute-start | bytes 884744 | tf_op jit(solution)/shard_map/ppermute | solution.py:48
  154.7 4.5 %collective-permute-start.39 = (bf16[256,768]{1,0:T(8,128)(2,1)}, bf16[256,768]{1,0:T(8,128)(2,1)}, u32[]{:S(2)}, u32[]{:S(2)}) collective-permute-start(bf16[256,768]{1,0:T(8,128)(2,1)} %fusion.5), channel_id=1, source_target_pairs={{0,0},{1,1},{2,4},{3,5},{4,2},{5,3},{6,6},{7,7},{8,8},{9,9},{10,12... | collective-permute-start | bytes 1179656 | tf_op jit(solution)/shard_map/ppermute | solution.py:48
  159.2 1.1 collective-permute-start.44
  160.3 2.6 %shard_map.254 = (f32[192,768]{1,0:T(8,128)S(1)}, bf16[192,768]{1,0:T(8,128)(2,1)S(1)}, bf16[192,768]{1,0:T(8,128)(2,1)S(1)}, bf16[192,768]{1,0:T(8,128)(2,1)S(1)}) custom-call(s32[4]{0:T(128)S(1)} %pad_add_fusion.refs_0_.ids, bf16[1024,768]{1,0:T(8,128)(2,1)S(1)} %copy-done.20, bf16[1024,576]{1,0:T(8,128)(2,1)S(1)} %copy-done.22, ...), custom_call_target="tpu_custom_call" | custom-call | flops 3449999872 | bytes 9000000 | tf_op jit(solution)/shard_map/pallas_call | solution.py:160
  163.3 10.0 %collective-permute-done.48 = bf16[96,1536]{1,0:T(8,128)(2,1)S(1)} collective-permute-done((bf16[96,1536]{1,0:T(8,128)(2,1)S(1)}, bf16[96,1536]{1,0:T(8,128)(2,1)S(1)}, u32[]{:S(2)}, u32[]{:S(2)}) %collective-permute-start.48) | collective-permute-done | bytes 294944 | tf_op jit(solution)/shard_map/ppermute | solution.py:48
  173.4 1.3 collective-permute-start.49
  175.1 1.8 collective-permute-start.51
  177.0 1.8 shard_map.253
  178.8 4.1 %collective-permute-done.45 = f32[16,768]{1,0:T(8,128)S(1)} collective-permute-done((f32[16,768]{1,0:T(8,128)S(1)}, f32[16,768]{1,0:T(8,128)S(1)}, u32[]{:S(2)}, u32[]{:S(2)}) %collective-permute-start.45) | collective-permute-done | bytes 49184 | tf_op jit(solution)/shard_map/ppermute | solution.py:48
  183.6 1.0 collective-permute-start.46
  184.6 1.3 add_convert_fusion.1
  185.9 0.9 convert_element_type.91
  187.9 11.2 %collective-permute-start.53 = (bf16[96,768]{0,1:T(8,128)(2,1)S(1)}, bf16[96,768]{0,1:T(8,128)(2,1)S(1)}, u32[]{:S(2)}, u32[]{:S(2)}) collective-permute-start(bf16[96,768]{0,1:T(8,128)(2,1)S(1)} %bitcast.68), channel_id=1, source_target_pairs={{0,4},{1,6},{2,0},{3,2},{4,5},{5,7},{6,1},{7,3},{8,12},{9,14},{10,... | collective-permute-start | bytes 442376 | tf_op jit(solution)/shard_map/ppermute | solution.py:48
  199.1 0.8 slice_bitcast_fusion.4
  201.3 7.2 %collective-permute-done.53 = bf16[96,768]{0,1:T(8,128)(2,1)S(1)} collective-permute-done((bf16[96,768]{0,1:T(8,128)(2,1)S(1)}, bf16[96,768]{0,1:T(8,128)(2,1)S(1)}, u32[]{:S(2)}, u32[]{:S(2)}) %collective-permute-start.53) | collective-permute-done | bytes 147488 | tf_op jit(solution)/shard_map/ppermute | solution.py:48
  209.1 0.9 copy.37
  210.0 1.8 copy.39
  (185 shorter events, 20.6 us)
Async XLA Ops:
  0.7 15.3 %copy-start.33 = (f32[768]{0:T(1024)S(1)}, f32[768]{0:T(1024)}, u32[]{:S(2)}) copy-start(f32[768]{0:T(1024)} %param.15) | copy-start | bytes 9220
  3.0 10.3 %collective-permute-start.5 = (bf16[96,768]{1,0:T(8,128)(2,1)S(1)}, bf16[96,768]{1,0:T(8,128)(2,1)S(1)}, u32[]{:S(2)}, u32[]{:S(2)}) collective-permute-start(bf16[96,768]{1,0:T(8,128)(2,1)S(1)} %pad_maximum_fusion.5), channel_id=1, source_target_pairs={{0,0},{1,4},{2,1},{3,5},{4,2},{5,6},{6,3},{7,7},{8,8},{9,12},{10,9... | collective-permute-start | bytes 442376 | tf_op jit(solution)/shard_map/ppermute | solution.py:48
  3.6 9.6 %collective-permute-start.6 = (bf16[96,768]{1,0:T(8,128)(2,1)S(1)}, bf16[96,768]{1,0:T(8,128)(2,1)S(1)}, u32[]{:S(2)}, u32[]{:S(2)}) collective-permute-start(bf16[96,768]{1,0:T(8,128)(2,1)S(1)} %pad_maximum_fusion.5), channel_id=1, source_target_pairs={{0,2},{1,6},{2,3},{3,7},{4,0},{5,4},{6,1},{7,5},{8,10},{9,14},{10,... | collective-permute-start | bytes 442376 | tf_op jit(solution)/shard_map/ppermute | solution.py:48
  9.4 7.8 %collective-permute-start = (bf16[256,768]{1,0:T(8,128)(2,1)}, bf16[256,768]{1,0:T(8,128)(2,1)S(1)}, u32[]{:S(2)}, u32[]{:S(2)}) collective-permute-start(bf16[256,768]{1,0:T(8,128)(2,1)} %param.14), channel_id=1, source_target_pairs={{0,0},{1,1},{2,4},{3,5},{4,2},{5,3},{6,6},{7,7},{8,8},{9,9},{10,12... | collective-permute-start | bytes 1179656 | tf_op jit(solution)/shard_map/ppermute | solution.py:48
  12.6 3.4 %collective-permute-start.4 = (f32[1344]{0:T(1024)S(1)}, f32[1344]{0:T(1024)S(1)}, u32[]{:S(2)}, u32[]{:S(2)}) collective-permute-start(f32[1344]{0:T(1024)S(1)} %pad_maximum_fusion.6), channel_id=1, source_target_pairs={{0,0},{1,4},{2,1},{3,5},{4,2},{5,6},{6,3},{7,7},{8,8},{9,12},{10,9... | collective-permute-start | bytes 16136 | tf_op jit(solution)/shard_map/ppermute | solution.py:48
  13.3 16.3 %collective-permute-start.9 = (bf16[2,96,768]{2,1,0:T(8,128)(2,1)S(1)}, bf16[2,96,768]{2,1,0:T(8,128)(2,1)S(1)}, u32[]{:S(2)}, u32[]{:S(2)}) collective-permute-start(bf16[2,96,768]{2,1,0:T(8,128)(2,1)S(1)} %pad_maximum_fusion.1.refs_8_), channel_id=1, source_target_pairs={{0,24},{1,25},{2,26},{3,27},{4,28},{5,29},{6,30},{7,31},{8,16},{9,... | collective-permute-start | bytes 884744 | tf_op jit(solution)/shard_map/ppermute | solution.py:48
  16.0 20.8 %collective-permute-start.7 = (bf16[2,96,768]{2,1,0:T(8,128)(2,1)S(1)}, bf16[2,96,768]{2,1,0:T(8,128)(2,1)S(1)}, u32[]{:S(2)}, u32[]{:S(2)}) collective-permute-start(bf16[2,96,768]{2,1,0:T(8,128)(2,1)S(1)} %pad_maximum_fusion.1.refs_8_), channel_id=1, source_target_pairs={{0,8},{1,9},{2,10},{3,11},{4,12},{5,13},{6,14},{7,15},{8,0},{9,1},... | collective-permute-start | bytes 884744 | tf_op jit(solution)/shard_map/ppermute | solution.py:48
  16.6 13.7 %collective-permute-start.8 = (bf16[2,96,768]{2,1,0:T(8,128)(2,1)S(1)}, bf16[2,96,768]{2,1,0:T(8,128)(2,1)S(1)}, u32[]{:S(2)}, u32[]{:S(2)}) collective-permute-start(bf16[2,96,768]{2,1,0:T(8,128)(2,1)S(1)} %pad_maximum_fusion.1.refs_8_), channel_id=1, source_target_pairs={{0,16},{1,17},{2,18},{3,19},{4,20},{5,21},{6,22},{7,23},{8,24},{9,... | collective-permute-start | bytes 884744 | tf_op jit(solution)/shard_map/ppermute | solution.py:48
  17.2 66.9 %copy-start.4 = (bf16[256,768]{1,0:T(8,128)(2,1)}, bf16[256,768]{1,0:T(8,128)(2,1)S(1)}, u32[]{:S(2)}) copy-start(bf16[256,768]{1,0:T(8,128)(2,1)S(1)} %collective-permute-done.refs_1_.refs_9_.x0.x) | copy-start | bytes 1179652
  17.3 21.6 %collective-permute-start.1 = (bf16[256,768]{1,0:T(8,128)(2,1)S(1)}, bf16[256,768]{1,0:T(8,128)(2,1)S(1)}, u32[]{:S(2)}, u32[]{:S(2)}) collective-permute-start(bf16[256,768]{1,0:T(8,128)(2,1)S(1)} %collective-permute-done.refs_1_.refs_9_.x0.x), channel_id=1, source_target_pairs={{0,1},{1,0},{2,3},{3,2},{4,5},{5,4},{6,7},{7,6},{8,9},{9,8},{10,11... | collective-permute-start | bytes 1179656 | tf_op jit(solution)/shard_map/ppermute | solution.py:48
  29.6 14.8 %collective-permute-start.2 = (bf16[256,768]{1,0:T(8,128)(2,1)S(1)}, bf16[256,768]{1,0:T(8,128)(2,1)S(1)}, u32[]{:S(2)}, u32[]{:S(2)}) collective-permute-start(bf16[256,768]{1,0:T(8,128)(2,1)S(1)} %collective-permute-done.refs_1_.refs_9_.x0.x), channel_id=1, source_target_pairs={{0,4},{1,5},{2,6},{3,7},{4,0},{5,1},{6,2},{7,3},{8,12},{9,13},{10,... | collective-permute-start | bytes 1179656 | tf_op jit(solution)/shard_map/ppermute | solution.py:48
  29.6 9.2 %collective-permute-start.11 = (bf16[96,1536]{1,0:T(8,128)(2,1)S(1)}, bf16[96,1536]{1,0:T(8,128)(2,1)S(1)}, u32[]{:S(2)}, u32[]{:S(2)}) collective-permute-start(bf16[96,1536]{1,0:T(8,128)(2,1)S(1)} %pad_maximum_fusion.2), channel_id=1, source_target_pairs={{0,0},{1,4},{2,1},{3,5},{4,2},{5,6},{6,3},{7,7},{8,8},{9,12},{10,9... | collective-permute-start | bytes 884744 | tf_op jit(solution)/shard_map/ppermute | solution.py:48
  30.4 11.6 %collective-permute-start.12 = (bf16[96,1536]{1,0:T(8,128)(2,1)S(1)}, bf16[96,1536]{1,0:T(8,128)(2,1)S(1)}, u32[]{:S(2)}, u32[]{:S(2)}) collective-permute-start(bf16[96,1536]{1,0:T(8,128)(2,1)S(1)} %pad_maximum_fusion.2), channel_id=1, source_target_pairs={{0,2},{1,6},{2,3},{3,7},{4,0},{5,4},{6,1},{7,5},{8,10},{9,14},{10,... | collective-permute-start | bytes 884744 | tf_op jit(solution)/shard_map/ppermute | solution.py:48
  37.1 30.4 %collective-permute-start.19 = (bf16[4,2,96,192]{3,2,1,0:T(8,128)(2,1)S(1)}, bf16[4,2,96,192]{3,2,1,0:T(8,128)(2,1)S(1)}, u32[]{:S(2)}, u32[]{:S(2)}) collective-permute-start(bf16[4,2,96,192]{3,2,1,0:T(8,128)(2,1)S(1)} %pad_maximum_fusion.refs_5_), channel_id=1, source_target_pairs={{0,4},{1,5},{2,6},{3,7},{4,0},{5,1},{6,2},{7,3},{8,12},{9,13},{10,... | collective-permute-start | bytes 884744 | tf_op jit(solution)/shard_map/ppermute | solution.py:48
  38.8 6.8 %collective-permute-start.3 = (bf16[256,768]{1,0:T(8,128)(2,1)S(1)}, bf16[256,768]{1,0:T(8,128)(2,1)S(1)}, u32[]{:S(2)}, u32[]{:S(2)}) collective-permute-start(bf16[256,768]{1,0:T(8,128)(2,1)S(1)} %collective-permute-done.1.refs_2_.refs_10_.x1), channel_id=1, source_target_pairs={{0,4},{1,5},{2,6},{3,7},{4,0},{5,1},{6,2},{7,3},{8,12},{9,13},{10,... | collective-permute-start | bytes 1179656 | tf_op jit(solution)/shard_map/ppermute | solution.py:48
  42.1 9.9 %collective-permute-start.13 = (bf16[2,96,768]{2,1,0:T(8,128)(2,1)S(1)}, bf16[2,96,768]{2,1,0:T(8,128)(2,1)S(1)}, u32[]{:S(2)}, u32[]{:S(2)}) collective-permute-start(bf16[2,96,768]{2,1,0:T(8,128)(2,1)S(1)} %pad_maximum_fusion.3.refs_17_), channel_id=1, source_target_pairs={{0,8},{1,9},{2,10},{3,11},{4,12},{5,13},{6,14},{7,15},{8,0},{9,1},... | collective-permute-start | bytes 884744 | tf_op jit(solution)/shard_map/ppermute | solution.py:48
  42.7 21.9 %collective-permute-start.14 = (bf16[2,96,768]{2,1,0:T(8,128)(2,1)S(1)}, bf16[2,96,768]{2,1,0:T(8,128)(2,1)S(1)}, u32[]{:S(2)}, u32[]{:S(2)}) collective-permute-start(bf16[2,96,768]{2,1,0:T(8,128)(2,1)S(1)} %pad_maximum_fusion.3.refs_17_), channel_id=1, source_target_pairs={{0,16},{1,17},{2,18},{3,19},{4,20},{5,21},{6,22},{7,23},{8,24},{9,... | collective-permute-start | bytes 884744 | tf_op jit(solution)/shard_map/ppermute | solution.py:48
  44.4 20.2 %collective-permute-start.15 = (bf16[2,96,768]{2,1,0:T(8,128)(2,1)S(1)}, bf16[2,96,768]{2,1,0:T(8,128)(2,1)S(1)}, u32[]{:S(2)}, u32[]{:S(2)}) collective-permute-start(bf16[2,96,768]{2,1,0:T(8,128)(2,1)S(1)} %pad_maximum_fusion.3.refs_17_), channel_id=1, source_target_pairs={{0,24},{1,25},{2,26},{3,27},{4,28},{5,29},{6,30},{7,31},{8,16},{9,... | collective-permute-start | bytes 884744 | tf_op jit(solution)/shard_map/ppermute | solution.py:48
  45.6 19.0 %collective-permute-start.10 = (bf16[256,768]{1,0:T(8,128)(2,1)S(1)}, bf16[256,768]{1,0:T(8,128)(2,1)S(1)}, u32[]{:S(2)}, u32[]{:S(2)}) collective-permute-start(bf16[256,768]{1,0:T(8,128)(2,1)S(1)} %copy-done.38), channel_id=1, source_target_pairs={{0,0},{1,1},{2,4},{3,5},{4,2},{5,3},{6,6},{7,7},{8,8},{9,9},{10,12... | collective-permute-start | bytes 1179656 | tf_op jit(solution)/shard_map/ppermute | solution.py:48
  50.2 32.1 %copy-start.35 = (f32[768]{0:T(1024)S(1)}, f32[768]{0:T(1024)}, u32[]{:S(2)}) copy-start(f32[768]{0:T(1024)} %param.21) | copy-start | bytes 9220
  50.2 32.1 %copy-start.36 = (f32[768]{0:T(1024)S(1)}, f32[768]{0:T(1024)}, u32[]{:S(2)}) copy-start(f32[768]{0:T(1024)} %param.20) | copy-start | bytes 9220
  50.2 32.2 %copy-start.37 = (f32[768]{0:T(1024)S(1)}, f32[768]{0:T(1024)}, u32[]{:S(2)}) copy-start(f32[768]{0:T(1024)} %param.22) | copy-start | bytes 9220
  52.0 18.9 %collective-permute-start.18 = (bf16[4,2,96,192]{3,2,1,0:T(8,128)(2,1)S(1)}, bf16[4,2,96,192]{3,2,1,0:T(8,128)(2,1)S(1)}, u32[]{:S(2)}, u32[]{:S(2)}) collective-permute-start(bf16[4,2,96,192]{3,2,1,0:T(8,128)(2,1)S(1)} %pad_maximum_fusion.refs_5_), channel_id=1, source_target_pairs={{0,1},{1,0},{2,3},{3,2},{4,5},{5,4},{6,7},{7,6},{8,9},{9,8},{10,11... | collective-permute-start | bytes 884744 | tf_op jit(solution)/shard_map/ppermute | solution.py:48
  64.6 26.2 %copy-start.2 = (bf16[1024,192]{1,0:T(8,128)(2,1)}, bf16[1024,192]{1,0:T(8,128)(2,1)S(1)}, u32[]{:S(2)}) copy-start(bf16[1024,192]{1,0:T(8,128)(2,1)S(1)} %get-tuple-element.78.refs_1_.refs_7_) | copy-start | bytes 1179652
  64.6 17.6 %collective-permute-start.16 = (bf16[1024,192]{1,0:T(8,128)(2,1)S(1)}, bf16[1024,192]{1,0:T(8,128)(2,1)S(1)}, u32[]{:S(2)}, u32[]{:S(2)}) collective-permute-start(bf16[1024,192]{1,0:T(8,128)(2,1)S(1)} %get-tuple-element.78.refs_1_.refs_7_), channel_id=1, source_target_pairs={{0,1},{1,0},{2,3},{3,2},{4,5},{5,4},{6,7},{7,6},{8,9},{9,8},{10,11... | collective-permute-start | bytes 1179656 | tf_op jit(solution)/shard_map/ppermute | solution.py:48
  64.7 9.2 %collective-permute-start.21 = (bf16[2,96,768]{2,1,0:T(8,128)(2,1)S(1)}, bf16[2,96,768]{2,1,0:T(8,128)(2,1)S(1)}, u32[]{:S(2)}, u32[]{:S(2)}) collective-permute-start(bf16[2,96,768]{2,1,0:T(8,128)(2,1)S(1)} %pad_maximum_fusion.4.refs_1_), channel_id=1, source_target_pairs={{0,8},{1,9},{2,10},{3,11},{4,12},{5,13},{6,14},{7,15},{8,0},{9,1},... | collective-permute-start | bytes 884744 | tf_op jit(solution)/shard_map/ppermute | solution.py:48
  66.2 14.4 %collective-permute-start.22 = (bf16[2,96,768]{2,1,0:T(8,128)(2,1)S(1)}, bf16[2,96,768]{2,1,0:T(8,128)(2,1)S(1)}, u32[]{:S(2)}, u32[]{:S(2)}) collective-permute-start(bf16[2,96,768]{2,1,0:T(8,128)(2,1)S(1)} %pad_maximum_fusion.4.refs_1_), channel_id=1, source_target_pairs={{0,16},{1,17},{2,18},{3,19},{4,20},{5,21},{6,22},{7,23},{8,24},{9,... | collective-permute-start | bytes 884744 | tf_op jit(solution)/shard_map/ppermute | solution.py:48
  67.5 14.3 %collective-permute-start.23 = (bf16[2,96,768]{2,1,0:T(8,128)(2,1)S(1)}, bf16[2,96,768]{2,1,0:T(8,128)(2,1)S(1)}, u32[]{:S(2)}, u32[]{:S(2)}) collective-permute-start(bf16[2,96,768]{2,1,0:T(8,128)(2,1)S(1)} %pad_maximum_fusion.4.refs_1_), channel_id=1, source_target_pairs={{0,24},{1,25},{2,26},{3,27},{4,28},{5,29},{6,30},{7,31},{8,16},{9,... | collective-permute-start | bytes 884744 | tf_op jit(solution)/shard_map/ppermute | solution.py:48
  71.0 11.2 %collective-permute-start.20 = (bf16[4,2,96,192]{3,2,1,0:T(8,128)(2,1)S(1)}, bf16[4,2,96,192]{3,2,1,0:T(8,128)(2,1)S(1)}, u32[]{:S(2)}, u32[]{:S(2)}) collective-permute-start(bf16[4,2,96,192]{3,2,1,0:T(8,128)(2,1)S(1)} %collective-permute-done.18.refs_6_), channel_id=1, source_target_pairs={{0,4},{1,5},{2,6},{3,7},{4,0},{5,1},{6,2},{7,3},{8,12},{9,13},{10,... | collective-permute-start | bytes 884744 | tf_op jit(solution)/shard_map/ppermute | solution.py:48
  74.0 10.2 %collective-permute-start.17 = (bf16[1024,192]{1,0:T(8,128)(2,1)S(1)}, bf16[1024,192]{1,0:T(8,128)(2,1)S(1)}, u32[]{:S(2)}, u32[]{:S(2)}) collective-permute-start(bf16[1024,192]{1,0:T(8,128)(2,1)S(1)} %get-tuple-element.78.refs_1_.refs_7_), channel_id=1, source_target_pairs={{0,4},{1,5},{2,6},{3,7},{4,0},{5,1},{6,2},{7,3},{8,12},{9,13},{10,... | collective-permute-start | bytes 1179656 | tf_op jit(solution)/shard_map/ppermute | solution.py:48
  82.2 1.9 collective-permute-start.24
  82.4 11.5 %collective-permute-start.26 = (bf16[256,768]{1,0:T(8,128)(2,1)S(1)}, bf16[256,768]{1,0:T(8,128)(2,1)S(1)}, u32[]{:S(2)}, u32[]{:S(2)}) collective-permute-start(bf16[256,768]{1,0:T(8,128)(2,1)S(1)} %collective-permute-done.10.refs_5_.refs_2_.g), channel_id=1, source_target_pairs={{0,4},{1,5},{2,6},{3,7},{4,0},{5,1},{6,2},{7,3},{8,12},{9,13},{10,... | collective-permute-start | bytes 1179656 | tf_op jit(solution)/shard_map/ppermute | solution.py:48
  82.9 11.1 %collective-permute-start.25 = (bf16[256,768]{1,0:T(8,128)(2,1)S(1)}, bf16[256,768]{1,0:T(8,128)(2,1)S(1)}, u32[]{:S(2)}, u32[]{:S(2)}) collective-permute-start(bf16[256,768]{1,0:T(8,128)(2,1)S(1)} %collective-permute-done.10.refs_5_.refs_2_.g), channel_id=1, source_target_pairs={{0,1},{1,0},{2,3},{3,2},{4,5},{5,4},{6,7},{7,6},{8,9},{9,8},{10,11... | collective-permute-start | bytes 1179656 | tf_op jit(solution)/shard_map/ppermute | solution.py:48
  94.0 1.7 collective-permute-start.27
  99.4 2.6 %collective-permute-start.29 = (bf16[2,256,768]{2,1,0:T(8,128)(2,1)S(1)}, bf16[2,256,768]{2,1,0:T(8,128)(2,1)S(1)}, u32[]{:S(2)}, u32[]{:S(2)}) collective-permute-start(bf16[2,256,768]{2,1,0:T(8,128)(2,1)S(1)} %get-tuple-element.93), channel_id=1, source_target_pairs={{0,4},{1,5},{2,6},{3,7},{4,0},{5,1},{6,2},{7,3},{8,12},{9,13},{10,... | collective-permute-start | bytes 2359304 | tf_op jit(solution)/shard_map/ppermute | solution.py:48
  101.6 26.4 %collective-permute-start.28 = (bf16[2,256,768]{2,1,0:T(8,128)(2,1)S(1)}, bf16[2,256,768]{2,1,0:T(8,128)(2,1)S(1)}, u32[]{:S(2)}, u32[]{:S(2)}) collective-permute-start(bf16[2,256,768]{2,1,0:T(8,128)(2,1)S(1)} %get-tuple-element.90), channel_id=1, source_target_pairs={{0,4},{1,5},{2,6},{3,7},{4,0},{5,1},{6,2},{7,3},{8,12},{9,13},{10,... | collective-permute-start | bytes 2359304 | tf_op jit(solution)/shard_map/ppermute | solution.py:48
  102.1 11.2 %collective-permute-start.30 = (bf16[256,768]{1,0:T(8,128)(2,1)S(1)}, bf16[256,768]{1,0:T(8,128)(2,1)S(1)}, u32[]{:S(2)}, u32[]{:S(2)}) collective-permute-start(bf16[256,768]{1,0:T(8,128)(2,1)S(1)} %fusion.1), channel_id=1, source_target_pairs={{0,1},{1,0},{2,3},{3,2},{4,5},{5,4},{6,7},{7,6},{8,9},{9,8},{10,11... | collective-permute-start | bytes 1179656 | tf_op jit(solution)/shard_map/ppermute | solution.py:48
  106.9 15.2 %collective-permute-start.34 = (bf16[192,1536]{1,0:T(8,128)(2,1)S(1)}, bf16[192,1536]{1,0:T(8,128)(2,1)S(1)}, u32[]{:S(2)}, u32[]{:S(2)}) collective-permute-start(bf16[192,1536]{1,0:T(8,128)(2,1)S(1)} %get-tuple-element.105), channel_id=1, source_target_pairs={{0,8},{1,9},{2,10},{3,11},{4,12},{5,13},{6,14},{7,15},{8,0},{9,1},... | collective-permute-start | bytes 1769480 | tf_op jit(solution)/shard_map/ppermute | solution.py:48
  107.7 14.8 %collective-permute-start.35 = (bf16[192,1536]{1,0:T(8,128)(2,1)S(1)}, bf16[192,1536]{1,0:T(8,128)(2,1)S(1)}, u32[]{:S(2)}, u32[]{:S(2)}) collective-permute-start(bf16[192,1536]{1,0:T(8,128)(2,1)S(1)} %get-tuple-element.106), channel_id=1, source_target_pairs={{0,16},{1,17},{2,18},{3,19},{4,20},{5,21},{6,22},{7,23},{8,24},{9,... | collective-permute-start | bytes 1769480 | tf_op jit(solution)/shard_map/ppermute | solution.py:48
  115.6 25.7 %copy-start.7 = (bf16[256,768]{1,0:T(8,128)(2,1)}, bf16[256,768]{1,0:T(8,128)(2,1)S(1)}, u32[]{:S(2)}) copy-start(bf16[256,768]{1,0:T(8,128)(2,1)S(1)} %get-tuple-element.100.gh0.refs_3_) | copy-start | bytes 1179652
  115.6 10.3 %collective-permute-start.31 = (bf16[256,768]{1,0:T(8,128)(2,1)S(1)}, bf16[256,768]{1,0:T(8,128)(2,1)S(1)}, u32[]{:S(2)}, u32[]{:S(2)}) collective-permute-start(bf16[256,768]{1,0:T(8,128)(2,1)S(1)} %get-tuple-element.100.gh0.refs_3_), channel_id=1, source_target_pairs={{0,1},{1,0},{2,3},{3,2},{4,5},{5,4},{6,7},{7,6},{8,9},{9,8},{10,11... | collective-permute-start | bytes 1179656 | tf_op jit(solution)/shard_map/ppermute | solution.py:48
  116.8 12.3 %collective-permute-start.33 = (bf16[256,768]{1,0:T(8,128)(2,1)S(1)}, bf16[256,768]{1,0:T(8,128)(2,1)S(1)}, u32[]{:S(2)}, u32[]{:S(2)}) collective-permute-start(bf16[256,768]{1,0:T(8,128)(2,1)S(1)} %get-tuple-element.100.gh0.refs_3_), channel_id=1, source_target_pairs={{0,4},{1,5},{2,6},{3,7},{4,0},{5,1},{6,2},{7,3},{8,12},{9,13},{10,... | collective-permute-start | bytes 1179656 | tf_op jit(solution)/shard_map/ppermute | solution.py:48
  125.9 15.4 %copy-start.9 = (bf16[256,768]{1,0:T(8,128)(2,1)}, bf16[256,768]{1,0:T(8,128)(2,1)S(1)}, u32[]{:S(2)}) copy-start(bf16[256,768]{1,0:T(8,128)(2,1)S(1)} %collective-permute-done.31.gh1.refs_4_) | copy-start | bytes 1179652
  125.9 3.2 %collective-permute-start.36 = (bf16[256,768]{1,0:T(8,128)(2,1)S(1)}, bf16[256,768]{1,0:T(8,128)(2,1)S(1)}, u32[]{:S(2)}, u32[]{:S(2)}) collective-permute-start(bf16[256,768]{1,0:T(8,128)(2,1)S(1)} %collective-permute-done.31.gh1.refs_4_), channel_id=1, source_target_pairs={{0,4},{1,5},{2,6},{3,7},{4,0},{5,1},{6,2},{7,3},{8,12},{9,13},{10,... | collective-permute-start | bytes 1179656 | tf_op jit(solution)/shard_map/ppermute | solution.py:48
  125.9 18.0 %collective-permute-start.37 = (bf16[192,1536]{1,0:T(8,128)(2,1)S(1)}, bf16[192,1536]{1,0:T(8,128)(2,1)S(1)}, u32[]{:S(2)}, u32[]{:S(2)}) collective-permute-start(bf16[192,1536]{1,0:T(8,128)(2,1)S(1)} %get-tuple-element.98), channel_id=1, source_target_pairs={{0,24},{1,25},{2,26},{3,27},{4,28},{5,29},{6,30},{7,31},{8,16},{9,... | collective-permute-start | bytes 1769480 | tf_op jit(solution)/shard_map/ppermute | solution.py:48
  128.1 16.7 %collective-permute-start.32 = (bf16[256,768]{1,0:T(8,128)(2,1)S(1)}, bf16[256,768]{1,0:T(8,128)(2,1)}, u32[]{:S(2)}, u32[]{:S(2)}) collective-permute-start(bf16[256,768]{1,0:T(8,128)(2,1)S(1)} %fusion.2), channel_id=1, source_target_pairs={{0,1},{1,0},{2,3},{3,2},{4,5},{5,4},{6,7},{7,6},{8,9},{9,8},{10,11... | collective-permute-start | bytes 1179656 | tf_op jit(solution)/shard_map/ppermute | solution.py:48
  129.2 15.6 %copy-start.32 = (f32[768]{0:T(1024)S(1)}, f32[768]{0:T(1024)}, u32[]{:S(2)}) copy-start(f32[768]{0:T(1024)} %param.26) | copy-start | bytes 9220
  144.7 2.6 %collective-permute-start.38 = (bf16[2,256,768]{2,1,0:T(8,128)(2,1)}, bf16[2,256,768]{2,1,0:T(8,128)(2,1)}, u32[]{:S(2)}, u32[]{:S(2)}) collective-permute-start(bf16[2,256,768]{2,1,0:T(8,128)(2,1)} %get-tuple-element.112), channel_id=1, source_target_pairs={{0,4},{1,5},{2,6},{3,7},{4,0},{5,1},{6,2},{7,3},{8,12},{9,13},{10,... | collective-permute-start | bytes 2359304 | tf_op jit(solution)/shard_map/ppermute | solution.py:48
  148.4 28.5 %collective-permute-start.40 = (bf16[256,768]{1,0:T(8,128)(2,1)S(1)}, bf16[256,768]{1,0:T(8,128)(2,1)S(1)}, u32[]{:S(2)}, u32[]{:S(2)}) collective-permute-start(bf16[256,768]{1,0:T(8,128)(2,1)S(1)} %fusion), channel_id=1, source_target_pairs={{0,1},{1,0},{2,3},{3,2},{4,5},{5,4},{6,7},{7,6},{8,9},{9,8},{10,11... | collective-permute-start | bytes 1179656 | tf_op jit(solution)/shard_map/ppermute | solution.py:48
  149.5 1.2 collective-permute-start.42
  150.8 8.4 %collective-permute-start.43 = (f32[16,768]{1,0:T(8,128)S(1)}, f32[16,768]{1,0:T(8,128)S(1)}, u32[]{:S(2)}, u32[]{:S(2)}) collective-permute-start(f32[16,768]{1,0:T(8,128)S(1)} %add.103), channel_id=1, source_target_pairs={{0,8},{1,9},{2,10},{3,11},{4,12},{5,13},{6,14},{7,15},{8,0},{9,1},... | collective-permute-start | bytes 147464 | tf_op jit(solution)/shard_map/ppermute | solution.py:48
  151.5 11.8 %collective-permute-start.47 = (bf16[96,1536]{1,0:T(8,128)(2,1)S(1)}, bf16[96,1536]{1,0:T(8,128)(2,1)S(1)}, u32[]{:S(2)}, u32[]{:S(2)}) collective-permute-start(bf16[96,1536]{1,0:T(8,128)(2,1)S(1)} %get-tuple-element.157), channel_id=1, source_target_pairs={{0,0},{1,2},{2,4},{3,6},{4,1},{5,3},{6,5},{7,7},{8,8},{9,10},{10,1... | collective-permute-start | bytes 884744 | tf_op jit(solution)/shard_map/ppermute | solution.py:48
  152.2 21.1 %collective-permute-start.48 = (bf16[96,1536]{1,0:T(8,128)(2,1)S(1)}, bf16[96,1536]{1,0:T(8,128)(2,1)S(1)}, u32[]{:S(2)}, u32[]{:S(2)}) collective-permute-start(bf16[96,1536]{1,0:T(8,128)(2,1)S(1)} %get-tuple-element.158), channel_id=1, source_target_pairs={{0,4},{1,6},{2,0},{3,2},{4,5},{5,7},{6,1},{7,3},{8,12},{9,14},{10,... | collective-permute-start | bytes 884744 | tf_op jit(solution)/shard_map/ppermute | solution.py:48
  154.7 28.9 %collective-permute-start.39 = (bf16[256,768]{1,0:T(8,128)(2,1)}, bf16[256,768]{1,0:T(8,128)(2,1)}, u32[]{:S(2)}, u32[]{:S(2)}) collective-permute-start(bf16[256,768]{1,0:T(8,128)(2,1)} %fusion.5), channel_id=1, source_target_pairs={{0,0},{1,1},{2,4},{3,5},{4,2},{5,3},{6,6},{7,7},{8,8},{9,9},{10,12... | collective-permute-start | bytes 1179656 | tf_op jit(solution)/shard_map/ppermute | solution.py:48
  159.2 4.2 %collective-permute-start.44 = (f32[16,768]{1,0:T(8,128)S(1)}, f32[16,768]{1,0:T(8,128)S(1)}, u32[]{:S(2)}, u32[]{:S(2)}) collective-permute-start(f32[16,768]{1,0:T(8,128)S(1)} %add.104), channel_id=1, source_target_pairs={{0,16},{1,17},{2,18},{3,19},{4,20},{5,21},{6,22},{7,23},{8,24},{9,... | collective-permute-start | bytes 147464 | tf_op jit(solution)/shard_map/ppermute | solution.py:48
  160.3 16.7 %copy-start.18 = (f32[256,768]{1,0:T(8,128)S(1)}, f32[256,768]{1,0:T(8,128)}, u32[]{:S(2)}) copy-start(f32[256,768]{1,0:T(8,128)} %copy-done.17) | copy-start | bytes 2359300
  173.4 11.2 %collective-permute-start.49 = (bf16[192,768]{1,0:T(8,128)(2,1)S(1)}, bf16[192,768]{1,0:T(8,128)(2,1)}, u32[]{:S(2)}, u32[]{:S(2)}) collective-permute-start(bf16[192,768]{1,0:T(8,128)(2,1)S(1)} %get-tuple-element.130), channel_id=1, source_target_pairs={{0,8},{1,9},{2,10},{3,11},{4,12},{5,13},{6,14},{7,15},{8,0},{9,1},... | collective-permute-start | bytes 884744 | tf_op jit(solution)/shard_map/ppermute | solution.py:48
  174.6 10.0 %collective-permute-start.50 = (bf16[192,768]{1,0:T(8,128)(2,1)S(1)}, bf16[192,768]{1,0:T(8,128)(2,1)}, u32[]{:S(2)}, u32[]{:S(2)}) collective-permute-start(bf16[192,768]{1,0:T(8,128)(2,1)S(1)} %get-tuple-element.131), channel_id=1, source_target_pairs={{0,16},{1,17},{2,18},{3,19},{4,20},{5,21},{6,22},{7,23},{8,24},{9,... | collective-permute-start | bytes 884744 | tf_op jit(solution)/shard_map/ppermute | solution.py:48
  175.1 9.5 %collective-permute-start.51 = (bf16[192,768]{1,0:T(8,128)(2,1)S(1)}, bf16[192,768]{1,0:T(8,128)(2,1)}, u32[]{:S(2)}, u32[]{:S(2)}) collective-permute-start(bf16[192,768]{1,0:T(8,128)(2,1)S(1)} %get-tuple-element.132), channel_id=1, source_target_pairs={{0,24},{1,25},{2,26},{3,27},{4,28},{5,29},{6,30},{7,31},{8,16},{9,... | collective-permute-start | bytes 884744 | tf_op jit(solution)/shard_map/ppermute | solution.py:48
  178.7 4.2 %collective-permute-start.45 = (f32[16,768]{1,0:T(8,128)S(1)}, f32[16,768]{1,0:T(8,128)S(1)}, u32[]{:S(2)}, u32[]{:S(2)}) collective-permute-start(f32[16,768]{1,0:T(8,128)S(1)} %add.105), channel_id=1, source_target_pairs={{0,1},{1,0},{2,3},{3,2},{4,5},{5,4},{6,7},{7,6},{8,9},{9,8},{10,11... | collective-permute-start | bytes 147464 | tf_op jit(solution)/shard_map/ppermute | solution.py:48
  182.9 3.0 %collective-permute-start.41 = (bf16[256,768]{1,0:T(8,128)(2,1)S(1)}, bf16[256,768]{1,0:T(8,128)(2,1)S(1)}, u32[]{:S(2)}, u32[]{:S(2)}) collective-permute-start(bf16[256,768]{1,0:T(8,128)(2,1)S(1)} %shard_map.253), channel_id=1, source_target_pairs={{0,0},{1,1},{2,4},{3,5},{4,2},{5,3},{6,6},{7,7},{8,8},{9,9},{10,12... | collective-permute-start | bytes 1179656 | tf_op jit(solution)/shard_map/ppermute | solution.py:48
  183.6 16.3 %collective-permute-start.46 = (f32[16,768]{1,0:T(8,128)S(1)}, f32[16,768]{1,0:T(8,128)S(1)}, u32[]{:S(2)}, u32[]{:S(2)}) collective-permute-start(f32[16,768]{1,0:T(8,128)S(1)} %add.106), channel_id=1, source_target_pairs={{0,2},{1,3},{2,0},{3,1},{4,6},{5,7},{6,4},{7,5},{8,10},{9,11},{10,... | collective-permute-start | bytes 147464 | tf_op jit(solution)/shard_map/ppermute | solution.py:48
  187.0 14.2 %collective-permute-start.52 = (bf16[96,768]{0,1:T(8,128)(2,1)S(1)}, bf16[96,768]{0,1:T(8,128)(2,1)S(1)}, u32[]{:S(2)}, u32[]{:S(2)}) collective-permute-start(bf16[96,768]{0,1:T(8,128)(2,1)S(1)} %bitcast.67), channel_id=1, source_target_pairs={{0,0},{1,2},{2,4},{3,6},{4,1},{5,3},{6,5},{7,7},{8,8},{9,10},{10,1... | collective-permute-start | bytes 442376 | tf_op jit(solution)/shard_map/ppermute | solution.py:48
  187.9 20.5 %collective-permute-start.53 = (bf16[96,768]{0,1:T(8,128)(2,1)S(1)}, bf16[96,768]{0,1:T(8,128)(2,1)S(1)}, u32[]{:S(2)}, u32[]{:S(2)}) collective-permute-start(bf16[96,768]{0,1:T(8,128)(2,1)S(1)} %bitcast.68), channel_id=1, source_target_pairs={{0,4},{1,6},{2,0},{3,2},{4,5},{5,7},{6,1},{7,3},{8,12},{9,14},{10,... | collective-permute-start | bytes 442376 | tf_op jit(solution)/shard_map/ppermute | solution.py:48
  (29 other events, 232.7 us)
where the time goes:
time: 215 us; the launch traced here: 212 us
  starting transfers between devices  87 us (40%)
  waiting for transfers between devices  59.3 us (28%)
  Pallas kernels  41.5 us (19%)
  local copies, waits for them, and re-layouts  15.3 us (7%)
  other arithmetic  7.21 us (3%)
    ppermute x54, starting transfers between devices, send(): return lax.ppermute(value, AXES, pairs)  87 us
    ppermute x54, waiting for transfers between devices, send(): return lax.ppermute(value, AXES, pairs)  59.3 us
    pallas_call x10, Pallas kernels, call(): pl.pallas_call(body, out_shape=shapes, in_specs=[pl.BlockSpec(memory_spac...  41.5 us
    unnamed x82, local copies, waits for them, and re-layouts  10.7 us
  transfers between devices with their start and end apart: 54, of which 20 were waited for; matrix products, arithmetic and copies ran while one was open for 5% of the time, Pallas kernels for 18%

commit v1 on v0

--- a/solution.py
+++ b/solution.py
@@ -49,6 +49,9 @@
 
     def swap_home(self, value):
         return self.send(value, lambda d, t: (d, t) if d % 2 == t // 2 else (d ^ 1, t ^ 2))
+
+    def swap_next(self, value):
+        return self.send(value, lambda d, t: (d, t ^ 1) if d % 2 == t // 2 else (d ^ 1, t ^ 3))
 
     def over_z(self, value):
         return self.send(value, lambda d, t: (d, t ^ 1))
@@ -511,9 +514,6 @@
         3,
         11,
     )
-    out_t = jnp.stack([piece[..., wide3:] for piece in attn_w])
-    out_z = plan.over_z(after(out_t, mixed))
-    outs = [out_t, out_z, plan.over_core(out_t), plan.over_core(out_z)]
     g0 = plan.swap_home(after(cotangent, x1))
     up_pieces = plane_pieces(up_stack)
 
@@ -524,11 +524,13 @@
         6,
         10,
     )
+    out_t = jnp.stack([piece[..., wide3:] for piece in attn_w])
+    out_z = plan.over_z(after(out_t, mixed))
+    outs = [out_t, out_z, plan.over_core(out_t), plan.over_core(out_z)]
     att_z = plan.over_z(after(attended, g0, *up_pieces))
     down_pieces = plane_pieces(after(down_stack, attended))
     att_last = after(att_z, *outs, *down_pieces[1:])
     att = [attended, att_z, plan.over_core(attended), plan.over_core(att_last)]
-    g1 = plan.over_z(after(g0, att_z))
 
     hidden_own, normed_two, act, slope, up_j = call(
         lambda *refs: forward_kernel(n_w, shard, *refs),
@@ -549,6 +551,7 @@
         22,
         [pltpu.VMEM((4, width, wide), BF)],
     )
+    g1 = plan.over_z(after(g0, att_z))
     gs = [g0, g1, plan.over_core(g0), plan.over_core(after(g1, slope))]
     grad_up, gn2_own, gn2_one, gn2_second, up_bias_grad, down_t = call(
         lambda *refs: backward_kernel(n_w, shard, *refs),
@@ -569,6 +572,7 @@
     )
     out_core = plan.over_core(out_second)
     out_z_in = toward_z(out_one, out_core)
+    out_here = (hidden_own + out_own + out_core[0].astype(F32) + down_bias).astype(BF)
     mlp_grad = call(
         lambda *refs: mlp_grad_kernel(n_o, shard, *refs),
         grad_outs(2 * units),
@@ -587,21 +591,18 @@
     gh1 = plan.over_z(gh0)
     mlp_got = plane_got(mlp_grad)
     ghs = [gh0, gh1, plan.over_core(gh0), plan.over_core(after(gh1, *mlp_got[:2]))]
-    out_from_z = plan.over_z(after(out_z_in, gh1))
-    out_sum = hidden_own + out_own + out_core[0].astype(F32) + out_from_z.astype(F32)
-    output_here = (out_sum + down_bias).astype(BF)
-
+    out_sent = [plan.swap_home(after(out_here, gh1)), plan.swap_next(after(out_z_in, gh1))]
     grad_mixed, gn1_own, gn1_one, gn1_second, small = call(
         attend_back_kernel,
         [((length, wide3), BF)] + parts() + [((16, width), F32)],
-        [ids, after(mixed, out_z_in), logs, w_all]
+        [ids, after(mixed, out_z_in, out_here), logs, w_all]
         + ghs
         + [x0, x1, x2, x3, sums_two, up_bias_grad],
         12,
         22,
         [pltpu.VMEM((length, wide), F32), pltpu.VMEM((length, 3 * HEAD_DIM), F32)],
     )
-    gn1_core = plan.over_core(after(gn1_second, out_from_z, *mlp_got[2:]))
+    gn1_core = plan.over_core(after(gn1_second, *out_sent, *mlp_got[2:]))
     gn1_z_in = toward_z(gn1_one, gn1_core)
     gn1_z = plan.over_z(gn1_z_in)
     mlp_part = plane_total(mlp_grad, mlp_got, gn1_z_in).astype(BF).reshape(2, shard, 2 * units)
@@ -615,8 +616,6 @@
         [pltpu.VMEM((width, width), F32)],
     )
     small = plan.chip_sum(after(small, gn1_z_in))
-    attn_grad = lax.optimization_barrier(tuple(attn_grad) + (mlp_summed, small))[:-2]
-    attn_got = plane_got(attn_grad)
     (grad_low,) = call(
         norm_one_kernel,
         [((rows, width), BF)],
@@ -624,15 +623,18 @@
         2,
         12,
     )
-    grad_tokens = plan.swap_home(grad_low).astype(F32)
-    output = plan.swap_home(after(output_here, gn1_z_in))
-
+    home = plan.swap_home(grad_low)
+    attn_grad = lax.optimization_barrier(tuple(attn_grad) + (small,))[:-1]
+    attn_got = plane_got(attn_grad)
+
+    attn_total = plane_total(attn_grad, attn_got, home)
     small = after(small, grad_low)
     small = small + plan.over_z(small)
-    attn_total = plane_total(attn_grad, attn_got, small, output)
-    attn_part = attn_total.astype(BF).reshape(2, shard, width)
-    attn_summed = plan.unspread(after(attn_part, grad_tokens))
     small = small + plan.over_two(small)
+    attn_part = after(attn_total, small).astype(BF).reshape(2, shard, width)
+    attn_summed = plan.unspread(attn_part)
+    output = (out_sent[0].astype(F32) + out_sent[1].astype(F32)).astype(BF)
+    grad_tokens = home.astype(F32)
     mine = lax.dynamic_slice_in_dim(small, 6 + 2 * plan.t, 2, 0)
     return (
         output,

time: 215 us -> 207 us (0.963)
  starting transfers between devices: 87 us -> 80.8 us
  waiting for transfers between devices: 59.3 us -> 63.9 us
  other arithmetic: 7.21 us -> 4 us
  local copies, waits for them, and re-layouts: 15.3 us -> 13.1 us
    ppermute x54, starting transfers between devices: 87 us -> 80.8 us  [send(): return lax.ppermute(value, AXES, pairs)]
    ppermute x54, waiting for transfers between devices: 59.3 us -> 63.9 us  [send(): return lax.ppermute(value, AXES, pairs)]
    convert_element_type x3, other arithmetic: 4.29 us -> 2.03 us  [the longest x1 0.93 us: local(): grad_tokens = home.astype(F32)]
    unnamed x82 -> x79, local copies, waits for them, and re-layouts: 10.7 us -> 8.52 us
  transfers between devices with their start and end apart: 54 -> 54, of which waited for: 20 -> 21; matrix products, arithmetic and copies ran while one was open for 5% -> 4% of each run, Pallas kernels for 18% -> 18%
where the time goes in v1:
time: 207 us; the launch traced here: 204 us
  starting transfers between devices  80.8 us (39%)
  waiting for transfers between devices  63.9 us (31%)
  Pallas kernels  40.5 us (20%)
  local copies, waits for them, and re-layouts  13.1 us (6%)
  other arithmetic  4 us (2%)
    ppermute x54, starting transfers between devices, send(): return lax.ppermute(value, AXES, pairs)  80.8 us
    ppermute x54, waiting for transfers between devices, send(): return lax.ppermute(value, AXES, pairs)  63.9 us
    pallas_call x10, Pallas kernels, call(): pl.pallas_call(body, out_shape=shapes, in_specs=[pl.BlockSpec(memory_spac...  40.5 us
    unnamed x79, local copies, waits for them, and re-layouts  8.52 us
  transfers between devices with their start and end apart: 54, of which 21 were waited for; matrix products, arithmetic and copies ran while one was open for 4% of the time, Pallas kernels for 18%

profile of v1, /device:TPU:0, one launch (start us, length us, event | category | flops | bytes accessed | tf_op | source)
XLA Modules:
  0.0 204.0 jit_solution(14340265441123083431)
XLA Ops:
  0.7 1.1 copy.32
  2.0 0.9 copy.33
  3.6 5.8 %collective-permute-start.6 = (bf16[96,768]{1,0:T(8,128)(2,1)S(1)}, bf16[96,768]{1,0:T(8,128)(2,1)S(1)}, u32[]{:S(2)}, u32[]{:S(2)}) collective-permute-start(bf16[96,768]{1,0:T(8,128)(2,1)S(1)} %pad_maximum_fusion.5), channel_id=1, source_target_pairs={{0,2},{1,6},{2,3},{3,7},{4,0},{5,4},{6,1},{7,5},{8,10},{9,14},{10,... | collective-permute-start | bytes 442376 | tf_op jit(solution)/shard_map/ppermute | solution.py:48
  9.4 1.6 collective-permute-start
  13.3 2.5 %collective-permute-start.9 = (bf16[2,96,768]{2,1,0:T(8,128)(2,1)S(1)}, bf16[2,96,768]{2,1,0:T(8,128)(2,1)S(1)}, u32[]{:S(2)}, u32[]{:S(2)}) collective-permute-start(bf16[2,96,768]{2,1,0:T(8,128)(2,1)S(1)} %pad_maximum_fusion.1.refs_8_), channel_id=1, source_target_pairs={{0,24},{1,25},{2,26},{3,27},{4,28},{5,29},{6,30},{7,31},{8,16},{9,... | collective-permute-start | bytes 884744 | tf_op jit(solution)/shard_map/ppermute | solution.py:48
  17.3 12.3 %collective-permute-start.1 = (bf16[256,768]{1,0:T(8,128)(2,1)S(1)}, bf16[256,768]{1,0:T(8,128)(2,1)S(1)}, u32[]{:S(2)}, u32[]{:S(2)}) collective-permute-start(bf16[256,768]{1,0:T(8,128)(2,1)S(1)} %collective-permute-done.refs_1_.refs_9_.x0.x), channel_id=1, source_target_pairs={{0,1},{1,0},{2,3},{3,2},{4,5},{5,4},{6,7},{7,6},{8,9},{9,8},{10,11... | collective-permute-start | bytes 1179656 | tf_op jit(solution)/shard_map/ppermute | solution.py:48
  30.4 6.4 %collective-permute-start.12 = (bf16[96,1536]{1,0:T(8,128)(2,1)S(1)}, bf16[96,1536]{1,0:T(8,128)(2,1)S(1)}, u32[]{:S(2)}, u32[]{:S(2)}) collective-permute-start(bf16[96,1536]{1,0:T(8,128)(2,1)S(1)} %pad_maximum_fusion.2), channel_id=1, source_target_pairs={{0,2},{1,6},{2,3},{3,7},{4,0},{5,4},{6,1},{7,5},{8,10},{9,14},{10,... | collective-permute-start | bytes 884744 | tf_op jit(solution)/shard_map/ppermute | solution.py:48
  37.2 1.7 collective-permute-done.1.refs_2_.refs_10_.x1
  38.9 3.2 %collective-permute-done.12 = bf16[96,1536]{1,0:T(8,128)(2,1)S(1)} collective-permute-done((bf16[96,1536]{1,0:T(8,128)(2,1)S(1)}, bf16[96,1536]{1,0:T(8,128)(2,1)S(1)}, u32[]{:S(2)}, u32[]{:S(2)}) %collective-permute-start.12) | collective-permute-done | bytes 294944 | tf_op jit(solution)/shard_map/ppermute | solution.py:48
  42.7 1.7 collective-permute-start.14
  44.4 1.3 collective-permute-start.15
  45.6 1.2 collective-permute-start.10
  46.8 2.5 %shard_map.245 = (bf16[1024,768]{1,0:T(8,128)(2,1)S(1)}, bf16[1024,576]{1,0:T(8,128)(2,1)S(1)}, bf16[768,768]{1,0:T(8,128)(2,1)S(1)}) custom-call(s32[4]{0:T(128)S(1)} %pad_add_fusion.refs_0_.ids, bf16[256,768]{1,0:T(8,128)(2,1)S(1)} %collective-permute-done.refs_1_.refs_9_.x0.x, bf16[256,768]{1,0:T(8,128)(2,1)S(1)} %collective-permute-done.1.refs_2_.refs_10_.x1, ...), custom_call_target="tpu_custom_call" | custom-call | flops 3449999872 | bytes 9000000 | tf_op jit(solution)/shard_map/pallas_call | solution.py:163
  49.4 1.1 copy-done.15
  50.5 1.5 collective-permute-done.13.refs_18_
  52.0 7.5 %collective-permute-start.18 = (bf16[4,2,96,192]{3,2,1,0:T(8,128)(2,1)S(1)}, bf16[4,2,96,192]{3,2,1,0:T(8,128)(2,1)S(1)}, u32[]{:S(2)}, u32[]{:S(2)}) collective-permute-start(bf16[4,2,96,192]{3,2,1,0:T(8,128)(2,1)S(1)} %pad_maximum_fusion.refs_5_), channel_id=1, source_target_pairs={{0,1},{1,0},{2,3},{3,2},{4,5},{5,4},{6,7},{7,6},{8,9},{9,8},{10,11... | collective-permute-start | bytes 884744 | tf_op jit(solution)/shard_map/ppermute | solution.py:48
  59.5 5.4 %shard_map.246 = (bf16[1024,192]{1,0:T(8,128)(2,1)S(1)}, f32[8,1024]{1,0:T(8,128)S(1)}) custom-call(s32[4]{0:T(128)S(1)} %pad_add_fusion.refs_0_.ids, bf16[1024,576]{1,0:T(8,128)(2,1)S(1)} %get-tuple-element.103.mixed), custom_call_target="tpu_custom_call" | custom-call | flops 6899999744 | bytes 18000000 | tf_op jit(solution)/shard_map/pallas_call | solution.py:163
  65.1 1.5 collective-permute-start.21
  66.5 1.3 collective-permute-start.22
  67.8 0.8 collective-permute-start.23
  68.6 2.3 %collective-permute-done.18.refs_6_ = bf16[4,2,96,192]{3,2,1,0:T(8,128)(2,1)S(1)} collective-permute-done((bf16[4,2,96,192]{3,2,1,0:T(8,128)(2,1)S(1)}, bf16[4,2,96,192]{3,2,1,0:T(8,128)(2,1)S(1)}, u32[]{:S(2)}, u32[]{:S(2)}) %collective-permute-start.18) | collective-permute-done | bytes 294944 | tf_op jit(solution)/shard_map/ppermute | solution.py:48
  71.3 3.0 %collective-permute-done.21.refs_2_ = bf16[2,96,768]{2,1,0:T(8,128)(2,1)S(1)} collective-permute-done((bf16[2,96,768]{2,1,0:T(8,128)(2,1)S(1)}, bf16[2,96,768]{2,1,0:T(8,128)(2,1)S(1)}, u32[]{:S(2)}, u32[]{:S(2)}) %collective-permute-start.21) | collective-permute-done | bytes 294944 | tf_op jit(solution)/shard_map/ppermute | solution.py:48
  74.3 1.5 collective-permute-start.17
  75.8 5.2 %collective-permute-done.22.refs_3_ = bf16[2,96,768]{2,1,0:T(8,128)(2,1)S(1)} collective-permute-done((bf16[2,96,768]{2,1,0:T(8,128)(2,1)S(1)}, bf16[2,96,768]{2,1,0:T(8,128)(2,1)S(1)}, u32[]{:S(2)}, u32[]{:S(2)}) %collective-permute-start.22) | collective-permute-done | bytes 294944 | tf_op jit(solution)/shard_map/ppermute | solution.py:48
  81.0 1.1 collective-permute-done.23.refs_4_
  82.8 1.6 collective-permute-start.25
  84.5 6.6 %shard_map.247 = (f32[256,768]{1,0:T(8,128)S(1)}, bf16[1024,768]{1,0:T(8,128)(2,1)S(1)}, bf16[1024,768]{1,0:T(8,128)(2,1)S(1)}, bf16[1024,768]{1,0:T(8,128)(2,1)S(1)}, bf16[768,768]{1,0:T(8,128)(2,1)S(1)}) custom-call(s32[4]{0:T(128)S(1)} %pad_add_fusion.refs_0_.ids, bf16[1024,192]{1,0:T(8,128)(2,1)S(1)} %get-tuple-element.78.refs_1_.refs_7_, ...), custom_call_target="tpu_custom_call" | custom-call | flops 8049999872 | bytes 21000000 | tf_op jit(solution)/shard_map/pallas_call | solution.py:163
  91.1 3.2 %collective-permute-done.25.refs_6_.refs_3_ = bf16[256,768]{1,0:T(8,128)(2,1)S(1)} collective-permute-done((bf16[256,768]{1,0:T(8,128)(2,1)S(1)}, bf16[256,768]{1,0:T(8,128)(2,1)S(1)}, u32[]{:S(2)}, u32[]{:S(2)}) %collective-permute-start.25) | collective-permute-done | bytes 393248 | tf_op jit(solution)/shard_map/ppermute | solution.py:48
  94.3 1.7 collective-permute-done.27.refs_8_.refs_5_
  96.0 3.6 %shard_map.248 = (bf16[1024,768]{1,0:T(8,128)(2,1)S(1)}, f32[256,768]{1,0:T(8,128)S(1)}, f32[256,768]{1,0:T(8,128)S(1)}, bf16[2,256,768]{2,1,0:T(8,128)(2,1)S(1)...) custom-call(s32[4]{0:T(128)S(1)} %pad_add_fusion.refs_0_.ids, bf16[2,96,768]{2,1,0:T(8,128)(2,1)S(1)} %pad_maximum_fusion.4.refs_1_, ...), custom_call_target="tpu_custom_call" | custom-call | flops 5750000128 | bytes 15000000 | tf_op jit(solution)/shard_map/pallas_call | solution.py:163
  99.9 2.0 shard_map.249
  102.4 1.3 collective-permute-start.30
  103.7 3.5 %shard_map.250 = (f32[192,1536]{1,0:T(8,128)S(1)}, bf16[192,1536]{1,0:T(8,128)(2,1)S(1)}, bf16[192,1536]{1,0:T(8,128)(2,1)S(1)}, bf16[192,1536]{1,0:T(8,128)(2,1)S(1)}) custom-call(s32[4]{0:T(128)S(1)} %pad_add_fusion.refs_0_.ids, bf16[1024,768]{1,0:T(8,128)(2,1)S(1)} %get-tuple-element.95.refs_1_, ...), custom_call_target="tpu_custom_call" | custom-call | flops 5750000128 | bytes 15000000 | tf_op jit(solution)/shard_map/pallas_call | solution.py:163
  107.9 1.7 collective-permute-start.36
  109.6 4.0 %collective-permute-done.30.got_z = bf16[256,768]{1,0:T(8,128)(2,1)S(1)} collective-permute-done((bf16[256,768]{1,0:T(8,128)(2,1)S(1)}, bf16[256,768]{1,0:T(8,128)(2,1)S(1)}, u32[]{:S(2)}, u32[]{:S(2)}) %collective-permute-start.30) | collective-permute-done | bytes 393248 | tf_op jit(solution)/shard_map/ppermute | solution.py:48
  113.6 1.3 shard_map.251
  114.9 0.9 copy-done.11
  115.8 1.3 collective-permute-start.31
  117.1 5.3 %collective-permute-done.35 = bf16[192,1536]{1,0:T(8,128)(2,1)S(1)} collective-permute-done((bf16[192,1536]{1,0:T(8,128)(2,1)S(1)}, bf16[192,1536]{1,0:T(8,128)(2,1)S(1)}, u32[]{:S(2)}, u32[]{:S(2)}) %collective-permute-start.35) | collective-permute-done | bytes 589856 | tf_op jit(solution)/shard_map/ppermute | solution.py:48
  122.7 3.4 %collective-permute-done.31.gh1.refs_4_ = bf16[256,768]{1,0:T(8,128)(2,1)S(1)} collective-permute-done((bf16[256,768]{1,0:T(8,128)(2,1)S(1)}, bf16[256,768]{1,0:T(8,128)(2,1)S(1)}, u32[]{:S(2)}, u32[]{:S(2)}) %collective-permute-start.31) | collective-permute-done | bytes 393248 | tf_op jit(solution)/shard_map/ppermute | solution.py:48
  126.1 2.1 %collective-permute-start.38 = (bf16[192,1536]{1,0:T(8,128)(2,1)S(1)}, bf16[192,1536]{1,0:T(8,128)(2,1)S(1)}, u32[]{:S(2)}, u32[]{:S(2)}) collective-permute-start(bf16[192,1536]{1,0:T(8,128)(2,1)S(1)} %get-tuple-element.97), channel_id=1, source_target_pairs={{0,24},{1,25},{2,26},{3,27},{4,28},{5,29},{6,30},{7,31},{8,16},{9,... | collective-permute-start | bytes 1769480 | tf_op jit(solution)/shard_map/ppermute | solution.py:48
  128.5 0.9 collective-permute-start.32
  129.4 1.1 collective-permute-start.33
  130.5 11.8 %shard_map.252 = (bf16[1024,576]{1,0:T(8,128)(2,1)S(1)}, f32[256,768]{1,0:T(8,128)S(1)}, f32[256,768]{1,0:T(8,128)S(1)}, bf16[2,256,768]{2,1,0:T(8,128)(2,1)}, f32[16,768]{1,0:T(8,128)S(1)}) custom-call(s32[4]{0:T(128)S(1)} %pad_add_fusion.refs_0_.ids, bf16[1024,576]{1,0:T(8,128)(2,1)S(1)} %get-tuple-element.103.mixed, ...), custom_call_target="tpu_custom_call" | custom-call | flops 13799999488 | bytes 36000000 | tf_op jit(solution)/shard_map/pallas_call | solution.py:163
  142.3 0.9 copy-done.13
  143.2 1.1 copy-done.17
  145.9 3.5 %collective-permute-start.39 = (bf16[2,256,768]{2,1,0:T(8,128)(2,1)}, bf16[2,256,768]{2,1,0:T(8,128)(2,1)S(1)}, u32[]{:S(2)}, u32[]{:S(2)}) collective-permute-start(bf16[2,256,768]{2,1,0:T(8,128)(2,1)} %get-tuple-element.113), channel_id=1, source_target_pairs={{0,4},{1,5},{2,6},{3,7},{4,0},{5,1},{6,2},{7,3},{8,12},{9,13},{10,... | collective-permute-start | bytes 2359304 | tf_op jit(solution)/shard_map/ppermute | solution.py:48
  149.4 2.1 %collective-permute-done.39.got_core = bf16[2,256,768]{2,1,0:T(8,128)(2,1)S(1)} collective-permute-done((bf16[2,256,768]{2,1,0:T(8,128)(2,1)}, bf16[2,256,768]{2,1,0:T(8,128)(2,1)S(1)}, u32[]{:S(2)}, u32[]{:S(2)}) %collective-permute-start.39) | collective-permute-done | bytes 786464 | tf_op jit(solution)/shard_map/ppermute | solution.py:48
  152.1 0.8 add_convert_fusion.1
  152.9 3.3 %collective-permute-start.40 = (bf16[256,768]{1,0:T(8,128)(2,1)S(1)}, bf16[256,768]{1,0:T(8,128)(2,1)S(1)}, u32[]{:S(2)}, u32[]{:S(2)}) collective-permute-start(bf16[256,768]{1,0:T(8,128)(2,1)S(1)} %fusion), channel_id=1, source_target_pairs={{0,1},{1,0},{2,3},{3,2},{4,5},{5,4},{6,7},{7,6},{8,9},{9,8},{10,11... | collective-permute-start | bytes 1179656 | tf_op jit(solution)/shard_map/ppermute | solution.py:48
  157.2 3.1 %collective-permute-done.43 = f32[16,768]{1,0:T(8,128)S(1)} collective-permute-done((f32[16,768]{1,0:T(8,128)S(1)}, f32[16,768]{1,0:T(8,128)S(1)}, u32[]{:S(2)}, u32[]{:S(2)}) %collective-permute-start.43) | collective-permute-done | bytes 49184 | tf_op jit(solution)/shard_map/ppermute | solution.py:48
  161.2 1.7 collective-permute-start.53
  162.8 1.6 collective-permute-done.44
  164.5 1.1 collective-permute-done.40.got_z
  165.7 1.2 shard_map.253
  166.9 2.5 %collective-permute-start.45 = (f32[16,768]{1,0:T(8,128)S(1)}, f32[16,768]{1,0:T(8,128)S(1)}, u32[]{:S(2)}, u32[]{:S(2)}) collective-permute-start(f32[16,768]{1,0:T(8,128)S(1)} %add.105), channel_id=1, source_target_pairs={{0,1},{1,0},{2,3},{3,2},{4,5},{5,4},{6,7},{7,6},{8,9},{9,8},{10,11... | collective-permute-start | bytes 147464 | tf_op jit(solution)/shard_map/ppermute | solution.py:48
  169.5 2.6 %shard_map.254 = (f32[192,768]{1,0:T(8,128)S(1)}, bf16[192,768]{1,0:T(8,128)(2,1)S(1)}, bf16[192,768]{1,0:T(8,128)(2,1)S(1)}, bf16[192,768]{1,0:T(8,128)(2,1)S(1)}) custom-call(s32[4]{0:T(128)S(1)} %pad_add_fusion.refs_0_.ids, bf16[1024,768]{1,0:T(8,128)(2,1)S(1)} %copy-done.16, bf16[1024,576]{1,0:T(8,128)(2,1)S(1)} %copy-done.18, ...), custom_call_target="tpu_custom_call" | custom-call | flops 3449999872 | bytes 9000000 | tf_op jit(solution)/shard_map/pallas_call | solution.py:163
  173.3 2.3 %collective-permute-start.49 = (bf16[192,768]{1,0:T(8,128)(2,1)S(1)}, bf16[192,768]{1,0:T(8,128)(2,1)S(1)}, u32[]{:S(2)}, u32[]{:S(2)}) collective-permute-start(bf16[192,768]{1,0:T(8,128)(2,1)S(1)} %get-tuple-element.130), channel_id=1, source_target_pairs={{0,24},{1,25},{2,26},{3,27},{4,28},{5,29},{6,30},{7,31},{8,16},{9,... | collective-permute-start | bytes 884744 | tf_op jit(solution)/shard_map/ppermute | solution.py:48
  176.5 1.0 collective-permute-start.46
  177.6 11.9 %collective-permute-done.46 = f32[16,768]{1,0:T(8,128)S(1)} collective-permute-done((f32[16,768]{1,0:T(8,128)S(1)}, f32[16,768]{1,0:T(8,128)S(1)}, u32[]{:S(2)}, u32[]{:S(2)}) %collective-permute-start.46) | collective-permute-done | bytes 49184 | tf_op jit(solution)/shard_map/ppermute | solution.py:48
  191.3 0.8 slice_bitcast_fusion.4
  193.5 0.9 convert_element_type.99
  194.4 7.7 %collective-permute-done.51 = bf16[96,768]{0,1:T(8,128)(2,1)S(1)} collective-permute-done((bf16[96,768]{0,1:T(8,128)(2,1)S(1)}, bf16[96,768]{0,1:T(8,128)(2,1)S(1)}, u32[]{:S(2)}, u32[]{:S(2)}) %collective-permute-start.51) | collective-permute-done | bytes 147488 | tf_op jit(solution)/shard_map/ppermute | solution.py:48
  202.9 0.9 copy.37
  (182 shorter events, 19.7 us)
Async XLA Ops:
  0.6 15.2 %copy-start.29 = (bf16[768,96]{0,1:T(8,128)(2,1)S(1)}, bf16[768,96]{0,1:T(8,128)(2,1)}, u32[]{:S(2)}) copy-start(bf16[768,96]{0,1:T(8,128)(2,1)} %param.25) | copy-start | bytes 442372
  0.7 15.2 %copy-start.30 = (bf16[96,768]{1,0:T(8,128)(2,1)S(1)}, bf16[96,768]{1,0:T(8,128)(2,1)}, u32[]{:S(2)}) copy-start(bf16[96,768]{1,0:T(8,128)(2,1)} %param.23) | copy-start | bytes 442372
  0.7 15.3 %copy-start.32 = (f32[768]{0:T(1024)S(1)}, f32[768]{0:T(1024)}, u32[]{:S(2)}) copy-start(f32[768]{0:T(1024)} %param.15) | copy-start | bytes 9220
  0.7 15.3 %copy-start.33 = (f32[768]{0:T(1024)S(1)}, f32[768]{0:T(1024)}, u32[]{:S(2)}) copy-start(f32[768]{0:T(1024)} %param.16) | copy-start | bytes 9220
  3.0 10.3 %collective-permute-start.5 = (bf16[96,768]{1,0:T(8,128)(2,1)S(1)}, bf16[96,768]{1,0:T(8,128)(2,1)S(1)}, u32[]{:S(2)}, u32[]{:S(2)}) collective-permute-start(bf16[96,768]{1,0:T(8,128)(2,1)S(1)} %pad_maximum_fusion.5), channel_id=1, source_target_pairs={{0,0},{1,4},{2,1},{3,5},{4,2},{5,6},{6,3},{7,7},{8,8},{9,12},{10,9... | collective-permute-start | bytes 442376 | tf_op jit(solution)/shard_map/ppermute | solution.py:48
  3.6 9.6 %collective-permute-start.6 = (bf16[96,768]{1,0:T(8,128)(2,1)S(1)}, bf16[96,768]{1,0:T(8,128)(2,1)S(1)}, u32[]{:S(2)}, u32[]{:S(2)}) collective-permute-start(bf16[96,768]{1,0:T(8,128)(2,1)S(1)} %pad_maximum_fusion.5), channel_id=1, source_target_pairs={{0,2},{1,6},{2,3},{3,7},{4,0},{5,4},{6,1},{7,5},{8,10},{9,14},{10,... | collective-permute-start | bytes 442376 | tf_op jit(solution)/shard_map/ppermute | solution.py:48
  9.4 7.8 %collective-permute-start = (bf16[256,768]{1,0:T(8,128)(2,1)}, bf16[256,768]{1,0:T(8,128)(2,1)S(1)}, u32[]{:S(2)}, u32[]{:S(2)}) collective-permute-start(bf16[256,768]{1,0:T(8,128)(2,1)} %param.14), channel_id=1, source_target_pairs={{0,0},{1,1},{2,4},{3,5},{4,2},{5,3},{6,6},{7,7},{8,8},{9,9},{10,12... | collective-permute-start | bytes 1179656 | tf_op jit(solution)/shard_map/ppermute | solution.py:48
  12.6 3.4 %collective-permute-start.4 = (f32[1344]{0:T(1024)S(1)}, f32[1344]{0:T(1024)S(1)}, u32[]{:S(2)}, u32[]{:S(2)}) collective-permute-start(f32[1344]{0:T(1024)S(1)} %pad_maximum_fusion.6), channel_id=1, source_target_pairs={{0,0},{1,4},{2,1},{3,5},{4,2},{5,6},{6,3},{7,7},{8,8},{9,12},{10,9... | collective-permute-start | bytes 16136 | tf_op jit(solution)/shard_map/ppermute | solution.py:48
  13.3 16.3 %collective-permute-start.9 = (bf16[2,96,768]{2,1,0:T(8,128)(2,1)S(1)}, bf16[2,96,768]{2,1,0:T(8,128)(2,1)S(1)}, u32[]{:S(2)}, u32[]{:S(2)}) collective-permute-start(bf16[2,96,768]{2,1,0:T(8,128)(2,1)S(1)} %pad_maximum_fusion.1.refs_8_), channel_id=1, source_target_pairs={{0,24},{1,25},{2,26},{3,27},{4,28},{5,29},{6,30},{7,31},{8,16},{9,... | collective-permute-start | bytes 884744 | tf_op jit(solution)/shard_map/ppermute | solution.py:48
  16.0 20.8 %collective-permute-start.7 = (bf16[2,96,768]{2,1,0:T(8,128)(2,1)S(1)}, bf16[2,96,768]{2,1,0:T(8,128)(2,1)S(1)}, u32[]{:S(2)}, u32[]{:S(2)}) collective-permute-start(bf16[2,96,768]{2,1,0:T(8,128)(2,1)S(1)} %pad_maximum_fusion.1.refs_8_), channel_id=1, source_target_pairs={{0,8},{1,9},{2,10},{3,11},{4,12},{5,13},{6,14},{7,15},{8,0},{9,1},... | collective-permute-start | bytes 884744 | tf_op jit(solution)/shard_map/ppermute | solution.py:48
  16.6 13.7 %collective-permute-start.8 = (bf16[2,96,768]{2,1,0:T(8,128)(2,1)S(1)}, bf16[2,96,768]{2,1,0:T(8,128)(2,1)S(1)}, u32[]{:S(2)}, u32[]{:S(2)}) collective-permute-start(bf16[2,96,768]{2,1,0:T(8,128)(2,1)S(1)} %pad_maximum_fusion.1.refs_8_), channel_id=1, source_target_pairs={{0,16},{1,17},{2,18},{3,19},{4,20},{5,21},{6,22},{7,23},{8,24},{9,... | collective-permute-start | bytes 884744 | tf_op jit(solution)/shard_map/ppermute | solution.py:48
  17.2 67.2 %copy-start = (bf16[256,768]{1,0:T(8,128)(2,1)}, bf16[256,768]{1,0:T(8,128)(2,1)S(1)}, u32[]{:S(2)}) copy-start(bf16[256,768]{1,0:T(8,128)(2,1)S(1)} %collective-permute-done.refs_1_.refs_9_.x0.x) | copy-start | bytes 1179652
  17.3 21.6 %collective-permute-start.1 = (bf16[256,768]{1,0:T(8,128)(2,1)S(1)}, bf16[256,768]{1,0:T(8,128)(2,1)S(1)}, u32[]{:S(2)}, u32[]{:S(2)}) collective-permute-start(bf16[256,768]{1,0:T(8,128)(2,1)S(1)} %collective-permute-done.refs_1_.refs_9_.x0.x), channel_id=1, source_target_pairs={{0,1},{1,0},{2,3},{3,2},{4,5},{5,4},{6,7},{7,6},{8,9},{9,8},{10,11... | collective-permute-start | bytes 1179656 | tf_op jit(solution)/shard_map/ppermute | solution.py:48
  29.6 14.8 %collective-permute-start.2 = (bf16[256,768]{1,0:T(8,128)(2,1)S(1)}, bf16[256,768]{1,0:T(8,128)(2,1)S(1)}, u32[]{:S(2)}, u32[]{:S(2)}) collective-permute-start(bf16[256,768]{1,0:T(8,128)(2,1)S(1)} %collective-permute-done.refs_1_.refs_9_.x0.x), channel_id=1, source_target_pairs={{0,4},{1,5},{2,6},{3,7},{4,0},{5,1},{6,2},{7,3},{8,12},{9,13},{10,... | collective-permute-start | bytes 1179656 | tf_op jit(solution)/shard_map/ppermute | solution.py:48
  29.6 9.2 %collective-permute-start.11 = (bf16[96,1536]{1,0:T(8,128)(2,1)S(1)}, bf16[96,1536]{1,0:T(8,128)(2,1)S(1)}, u32[]{:S(2)}, u32[]{:S(2)}) collective-permute-start(bf16[96,1536]{1,0:T(8,128)(2,1)S(1)} %pad_maximum_fusion.2), channel_id=1, source_target_pairs={{0,0},{1,4},{2,1},{3,5},{4,2},{5,6},{6,3},{7,7},{8,8},{9,12},{10,9... | collective-permute-start | bytes 884744 | tf_op jit(solution)/shard_map/ppermute | solution.py:48
  30.4 11.6 %collective-permute-start.12 = (bf16[96,1536]{1,0:T(8,128)(2,1)S(1)}, bf16[96,1536]{1,0:T(8,128)(2,1)S(1)}, u32[]{:S(2)}, u32[]{:S(2)}) collective-permute-start(bf16[96,1536]{1,0:T(8,128)(2,1)S(1)} %pad_maximum_fusion.2), channel_id=1, source_target_pairs={{0,2},{1,6},{2,3},{3,7},{4,0},{5,4},{6,1},{7,5},{8,10},{9,14},{10,... | collective-permute-start | bytes 884744 | tf_op jit(solution)/shard_map/ppermute | solution.py:48
  37.1 30.8 %collective-permute-start.19 = (bf16[4,2,96,192]{3,2,1,0:T(8,128)(2,1)S(1)}, bf16[4,2,96,192]{3,2,1,0:T(8,128)(2,1)S(1)}, u32[]{:S(2)}, u32[]{:S(2)}) collective-permute-start(bf16[4,2,96,192]{3,2,1,0:T(8,128)(2,1)S(1)} %pad_maximum_fusion.refs_5_), channel_id=1, source_target_pairs={{0,4},{1,5},{2,6},{3,7},{4,0},{5,1},{6,2},{7,3},{8,12},{9,13},{10,... | collective-permute-start | bytes 884744 | tf_op jit(solution)/shard_map/ppermute | solution.py:48
  38.8 6.8 %collective-permute-start.3 = (bf16[256,768]{1,0:T(8,128)(2,1)S(1)}, bf16[256,768]{1,0:T(8,128)(2,1)S(1)}, u32[]{:S(2)}, u32[]{:S(2)}) collective-permute-start(bf16[256,768]{1,0:T(8,128)(2,1)S(1)} %collective-permute-done.1.refs_2_.refs_10_.x1), channel_id=1, source_target_pairs={{0,4},{1,5},{2,6},{3,7},{4,0},{5,1},{6,2},{7,3},{8,12},{9,13},{10,... | collective-permute-start | bytes 1179656 | tf_op jit(solution)/shard_map/ppermute | solution.py:48
  42.1 9.9 %collective-permute-start.13 = (bf16[2,96,768]{2,1,0:T(8,128)(2,1)S(1)}, bf16[2,96,768]{2,1,0:T(8,128)(2,1)S(1)}, u32[]{:S(2)}, u32[]{:S(2)}) collective-permute-start(bf16[2,96,768]{2,1,0:T(8,128)(2,1)S(1)} %pad_maximum_fusion.3.refs_17_), channel_id=1, source_target_pairs={{0,8},{1,9},{2,10},{3,11},{4,12},{5,13},{6,14},{7,15},{8,0},{9,1},... | collective-permute-start | bytes 884744 | tf_op jit(solution)/shard_map/ppermute | solution.py:48
  42.7 22.3 %collective-permute-start.14 = (bf16[2,96,768]{2,1,0:T(8,128)(2,1)S(1)}, bf16[2,96,768]{2,1,0:T(8,128)(2,1)S(1)}, u32[]{:S(2)}, u32[]{:S(2)}) collective-permute-start(bf16[2,96,768]{2,1,0:T(8,128)(2,1)S(1)} %pad_maximum_fusion.3.refs_17_), channel_id=1, source_target_pairs={{0,16},{1,17},{2,18},{3,19},{4,20},{5,21},{6,22},{7,23},{8,24},{9,... | collective-permute-start | bytes 884744 | tf_op jit(solution)/shard_map/ppermute | solution.py:48
  44.4 20.6 %collective-permute-start.15 = (bf16[2,96,768]{2,1,0:T(8,128)(2,1)S(1)}, bf16[2,96,768]{2,1,0:T(8,128)(2,1)S(1)}, u32[]{:S(2)}, u32[]{:S(2)}) collective-permute-start(bf16[2,96,768]{2,1,0:T(8,128)(2,1)S(1)} %pad_maximum_fusion.3.refs_17_), channel_id=1, source_target_pairs={{0,24},{1,25},{2,26},{3,27},{4,28},{5,29},{6,30},{7,31},{8,16},{9,... | collective-permute-start | bytes 884744 | tf_op jit(solution)/shard_map/ppermute | solution.py:48
  45.6 19.3 %collective-permute-start.10 = (bf16[256,768]{1,0:T(8,128)(2,1)S(1)}, bf16[256,768]{1,0:T(8,128)(2,1)S(1)}, u32[]{:S(2)}, u32[]{:S(2)}) collective-permute-start(bf16[256,768]{1,0:T(8,128)(2,1)S(1)} %copy-done.37), channel_id=1, source_target_pairs={{0,0},{1,1},{2,4},{3,5},{4,2},{5,3},{6,6},{7,7},{8,8},{9,9},{10,12... | collective-permute-start | bytes 1179656 | tf_op jit(solution)/shard_map/ppermute | solution.py:48
  50.5 32.1 %copy-start.34 = (f32[768]{0:T(1024)S(1)}, f32[768]{0:T(1024)}, u32[]{:S(2)}) copy-start(f32[768]{0:T(1024)} %param.21) | copy-start | bytes 9220
  50.5 32.1 %copy-start.35 = (f32[768]{0:T(1024)S(1)}, f32[768]{0:T(1024)}, u32[]{:S(2)}) copy-start(f32[768]{0:T(1024)} %param.20) | copy-start | bytes 9220
  50.5 32.1 %copy-start.36 = (f32[768]{0:T(1024)S(1)}, f32[768]{0:T(1024)}, u32[]{:S(2)}) copy-start(f32[768]{0:T(1024)} %param.22) | copy-start | bytes 9220
  52.0 18.9 %collective-permute-start.18 = (bf16[4,2,96,192]{3,2,1,0:T(8,128)(2,1)S(1)}, bf16[4,2,96,192]{3,2,1,0:T(8,128)(2,1)S(1)}, u32[]{:S(2)}, u32[]{:S(2)}) collective-permute-start(bf16[4,2,96,192]{3,2,1,0:T(8,128)(2,1)S(1)} %pad_maximum_fusion.refs_5_), channel_id=1, source_target_pairs={{0,1},{1,0},{2,3},{3,2},{4,5},{5,4},{6,7},{7,6},{8,9},{9,8},{10,11... | collective-permute-start | bytes 884744 | tf_op jit(solution)/shard_map/ppermute | solution.py:48
  64.9 17.3 %collective-permute-start.16 = (bf16[1024,192]{1,0:T(8,128)(2,1)S(1)}, bf16[1024,192]{1,0:T(8,128)(2,1)S(1)}, u32[]{:S(2)}, u32[]{:S(2)}) collective-permute-start(bf16[1024,192]{1,0:T(8,128)(2,1)S(1)} %get-tuple-element.78.refs_1_.refs_7_), channel_id=1, source_target_pairs={{0,1},{1,0},{2,3},{3,2},{4,5},{5,4},{6,7},{7,6},{8,9},{9,8},{10,11... | collective-permute-start | bytes 1179656 | tf_op jit(solution)/shard_map/ppermute | solution.py:48
  65.1 9.2 %collective-permute-start.21 = (bf16[2,96,768]{2,1,0:T(8,128)(2,1)S(1)}, bf16[2,96,768]{2,1,0:T(8,128)(2,1)S(1)}, u32[]{:S(2)}, u32[]{:S(2)}) collective-permute-start(bf16[2,96,768]{2,1,0:T(8,128)(2,1)S(1)} %pad_maximum_fusion.4.refs_1_), channel_id=1, source_target_pairs={{0,8},{1,9},{2,10},{3,11},{4,12},{5,13},{6,14},{7,15},{8,0},{9,1},... | collective-permute-start | bytes 884744 | tf_op jit(solution)/shard_map/ppermute | solution.py:48
  66.5 14.5 %collective-permute-start.22 = (bf16[2,96,768]{2,1,0:T(8,128)(2,1)S(1)}, bf16[2,96,768]{2,1,0:T(8,128)(2,1)S(1)}, u32[]{:S(2)}, u32[]{:S(2)}) collective-permute-start(bf16[2,96,768]{2,1,0:T(8,128)(2,1)S(1)} %pad_maximum_fusion.4.refs_1_), channel_id=1, source_target_pairs={{0,16},{1,17},{2,18},{3,19},{4,20},{5,21},{6,22},{7,23},{8,24},{9,... | collective-permute-start | bytes 884744 | tf_op jit(solution)/shard_map/ppermute | solution.py:48
  67.8 14.3 %collective-permute-start.23 = (bf16[2,96,768]{2,1,0:T(8,128)(2,1)S(1)}, bf16[2,96,768]{2,1,0:T(8,128)(2,1)S(1)}, u32[]{:S(2)}, u32[]{:S(2)}) collective-permute-start(bf16[2,96,768]{2,1,0:T(8,128)(2,1)S(1)} %pad_maximum_fusion.4.refs_1_), channel_id=1, source_target_pairs={{0,24},{1,25},{2,26},{3,27},{4,28},{5,29},{6,30},{7,31},{8,16},{9,... | collective-permute-start | bytes 884744 | tf_op jit(solution)/shard_map/ppermute | solution.py:48
  71.0 11.2 %collective-permute-start.20 = (bf16[4,2,96,192]{3,2,1,0:T(8,128)(2,1)S(1)}, bf16[4,2,96,192]{3,2,1,0:T(8,128)(2,1)S(1)}, u32[]{:S(2)}, u32[]{:S(2)}) collective-permute-start(bf16[4,2,96,192]{3,2,1,0:T(8,128)(2,1)S(1)} %collective-permute-done.18.refs_6_), channel_id=1, source_target_pairs={{0,4},{1,5},{2,6},{3,7},{4,0},{5,1},{6,2},{7,3},{8,12},{9,13},{10,... | collective-permute-start | bytes 884744 | tf_op jit(solution)/shard_map/ppermute | solution.py:48
  74.3 10.2 %collective-permute-start.17 = (bf16[1024,192]{1,0:T(8,128)(2,1)S(1)}, bf16[1024,192]{1,0:T(8,128)(2,1)S(1)}, u32[]{:S(2)}, u32[]{:S(2)}) collective-permute-start(bf16[1024,192]{1,0:T(8,128)(2,1)S(1)} %get-tuple-element.78.refs_1_.refs_7_), channel_id=1, source_target_pairs={{0,4},{1,5},{2,6},{3,7},{4,0},{5,1},{6,2},{7,3},{8,12},{9,13},{10,... | collective-permute-start | bytes 1179656 | tf_op jit(solution)/shard_map/ppermute | solution.py:48
  82.2 2.3 %collective-permute-start.24 = (bf16[1024,192]{1,0:T(8,128)(2,1)S(1)}, bf16[1024,192]{1,0:T(8,128)(2,1)S(1)}, u32[]{:S(2)}, u32[]{:S(2)}) collective-permute-start(bf16[1024,192]{1,0:T(8,128)(2,1)S(1)} %collective-permute-done.16.refs_2_), channel_id=1, source_target_pairs={{0,4},{1,5},{2,6},{3,7},{4,0},{5,1},{6,2},{7,3},{8,12},{9,13},{10,... | collective-permute-start | bytes 1179656 | tf_op jit(solution)/shard_map/ppermute | solution.py:48
  82.7 11.6 %collective-permute-start.26 = (bf16[256,768]{1,0:T(8,128)(2,1)S(1)}, bf16[256,768]{1,0:T(8,128)(2,1)S(1)}, u32[]{:S(2)}, u32[]{:S(2)}) collective-permute-start(bf16[256,768]{1,0:T(8,128)(2,1)S(1)} %collective-permute-done.10.refs_5_.refs_2_.g), channel_id=1, source_target_pairs={{0,4},{1,5},{2,6},{3,7},{4,0},{5,1},{6,2},{7,3},{8,12},{9,13},{10,... | collective-permute-start | bytes 1179656 | tf_op jit(solution)/shard_map/ppermute | solution.py:48
  82.8 11.5 %collective-permute-start.25 = (bf16[256,768]{1,0:T(8,128)(2,1)S(1)}, bf16[256,768]{1,0:T(8,128)(2,1)S(1)}, u32[]{:S(2)}, u32[]{:S(2)}) collective-permute-start(bf16[256,768]{1,0:T(8,128)(2,1)S(1)} %collective-permute-done.10.refs_5_.refs_2_.g), channel_id=1, source_target_pairs={{0,1},{1,0},{2,3},{3,2},{4,5},{5,4},{6,7},{7,6},{8,9},{9,8},{10,11... | collective-permute-start | bytes 1179656 | tf_op jit(solution)/shard_map/ppermute | solution.py:48
  94.3 1.7 collective-permute-start.27
  99.7 2.6 %collective-permute-start.29 = (bf16[2,256,768]{2,1,0:T(8,128)(2,1)S(1)}, bf16[2,256,768]{2,1,0:T(8,128)(2,1)S(1)}, u32[]{:S(2)}, u32[]{:S(2)}) collective-permute-start(bf16[2,256,768]{2,1,0:T(8,128)(2,1)S(1)} %get-tuple-element.92), channel_id=1, source_target_pairs={{0,4},{1,5},{2,6},{3,7},{4,0},{5,1},{6,2},{7,3},{8,12},{9,13},{10,... | collective-permute-start | bytes 2359304 | tf_op jit(solution)/shard_map/ppermute | solution.py:48
  101.8 26.4 %collective-permute-start.28 = (bf16[2,256,768]{2,1,0:T(8,128)(2,1)S(1)}, bf16[2,256,768]{2,1,0:T(8,128)(2,1)S(1)}, u32[]{:S(2)}, u32[]{:S(2)}) collective-permute-start(bf16[2,256,768]{2,1,0:T(8,128)(2,1)S(1)} %get-tuple-element.90), channel_id=1, source_target_pairs={{0,4},{1,5},{2,6},{3,7},{4,0},{5,1},{6,2},{7,3},{8,12},{9,13},{10,... | collective-permute-start | bytes 2359304 | tf_op jit(solution)/shard_map/ppermute | solution.py:48
  102.4 11.2 %collective-permute-start.30 = (bf16[256,768]{1,0:T(8,128)(2,1)S(1)}, bf16[256,768]{1,0:T(8,128)(2,1)S(1)}, u32[]{:S(2)}, u32[]{:S(2)}) collective-permute-start(bf16[256,768]{1,0:T(8,128)(2,1)S(1)} %fusion.2), channel_id=1, source_target_pairs={{0,1},{1,0},{2,3},{3,2},{4,5},{5,4},{6,7},{7,6},{8,9},{9,8},{10,11... | collective-permute-start | bytes 1179656 | tf_op jit(solution)/shard_map/ppermute | solution.py:48
  107.2 15.1 %collective-permute-start.35 = (bf16[192,1536]{1,0:T(8,128)(2,1)S(1)}, bf16[192,1536]{1,0:T(8,128)(2,1)S(1)}, u32[]{:S(2)}, u32[]{:S(2)}) collective-permute-start(bf16[192,1536]{1,0:T(8,128)(2,1)S(1)} %get-tuple-element.106), channel_id=1, source_target_pairs={{0,8},{1,9},{2,10},{3,11},{4,12},{5,13},{6,14},{7,15},{8,0},{9,1},... | collective-permute-start | bytes 1769480 | tf_op jit(solution)/shard_map/ppermute | solution.py:48
  107.9 14.8 %collective-permute-start.36 = (bf16[192,1536]{1,0:T(8,128)(2,1)S(1)}, bf16[192,1536]{1,0:T(8,128)(2,1)S(1)}, u32[]{:S(2)}, u32[]{:S(2)}) collective-permute-start(bf16[192,1536]{1,0:T(8,128)(2,1)S(1)} %get-tuple-element.107), channel_id=1, source_target_pairs={{0,16},{1,17},{2,18},{3,19},{4,20},{5,21},{6,22},{7,23},{8,24},{9,... | collective-permute-start | bytes 1769480 | tf_op jit(solution)/shard_map/ppermute | solution.py:48
  113.6 14.6 %copy-start.31 = (f32[768]{0:T(1024)S(1)}, f32[768]{0:T(1024)}, u32[]{:S(2)}) copy-start(f32[768]{0:T(1024)} %param.26) | copy-start | bytes 9220
  115.8 14.7 %copy-start.3 = (bf16[256,768]{1,0:T(8,128)(2,1)}, bf16[256,768]{1,0:T(8,128)(2,1)S(1)}, u32[]{:S(2)}) copy-start(bf16[256,768]{1,0:T(8,128)(2,1)S(1)} %get-tuple-element.99.gh0.refs_3_) | copy-start | bytes 1179652
  115.8 10.3 %collective-permute-start.31 = (bf16[256,768]{1,0:T(8,128)(2,1)S(1)}, bf16[256,768]{1,0:T(8,128)(2,1)S(1)}, u32[]{:S(2)}, u32[]{:S(2)}) collective-permute-start(bf16[256,768]{1,0:T(8,128)(2,1)S(1)} %get-tuple-element.99.gh0.refs_3_), channel_id=1, source_target_pairs={{0,1},{1,0},{2,3},{3,2},{4,5},{5,4},{6,7},{7,6},{8,9},{9,8},{10,11... | collective-permute-start | bytes 1179656 | tf_op jit(solution)/shard_map/ppermute | solution.py:48
  117.0 13.4 %collective-permute-start.34 = (bf16[256,768]{1,0:T(8,128)(2,1)S(1)}, bf16[256,768]{1,0:T(8,128)(2,1)S(1)}, u32[]{:S(2)}, u32[]{:S(2)}) collective-permute-start(bf16[256,768]{1,0:T(8,128)(2,1)S(1)} %get-tuple-element.99.gh0.refs_3_), channel_id=1, source_target_pairs={{0,4},{1,5},{2,6},{3,7},{4,0},{5,1},{6,2},{7,3},{8,12},{9,13},{10,... | collective-permute-start | bytes 1179656 | tf_op jit(solution)/shard_map/ppermute | solution.py:48
  126.1 4.4 %collective-permute-start.37 = (bf16[256,768]{1,0:T(8,128)(2,1)S(1)}, bf16[256,768]{1,0:T(8,128)(2,1)S(1)}, u32[]{:S(2)}, u32[]{:S(2)}) collective-permute-start(bf16[256,768]{1,0:T(8,128)(2,1)S(1)} %collective-permute-done.31.gh1.refs_4_), channel_id=1, source_target_pairs={{0,4},{1,5},{2,6},{3,7},{4,0},{5,1},{6,2},{7,3},{8,12},{9,13},{10,... | collective-permute-start | bytes 1179656 | tf_op jit(solution)/shard_map/ppermute | solution.py:48
  126.1 18.2 %collective-permute-start.38 = (bf16[192,1536]{1,0:T(8,128)(2,1)S(1)}, bf16[192,1536]{1,0:T(8,128)(2,1)S(1)}, u32[]{:S(2)}, u32[]{:S(2)}) collective-permute-start(bf16[192,1536]{1,0:T(8,128)(2,1)S(1)} %get-tuple-element.97), channel_id=1, source_target_pairs={{0,24},{1,25},{2,26},{3,27},{4,28},{5,29},{6,30},{7,31},{8,16},{9,... | collective-permute-start | bytes 1769480 | tf_op jit(solution)/shard_map/ppermute | solution.py:48
  128.5 15.8 %collective-permute-start.32 = (bf16[256,768]{1,0:T(8,128)(2,1)S(1)}, bf16[256,768]{1,0:T(8,128)(2,1)S(1)}, u32[]{:S(2)}, u32[]{:S(2)}) collective-permute-start(bf16[256,768]{1,0:T(8,128)(2,1)S(1)} %get-tuple-element.100), channel_id=1, source_target_pairs={{0,0},{1,1},{2,4},{3,5},{4,2},{5,3},{6,6},{7,7},{8,8},{9,9},{10,12... | collective-permute-start | bytes 1179656 | tf_op jit(solution)/shard_map/ppermute | solution.py:48
  129.4 14.9 %collective-permute-start.33 = (bf16[256,768]{1,0:T(8,128)(2,1)S(1)}, bf16[256,768]{1,0:T(8,128)(2,1)S(1)}, u32[]{:S(2)}, u32[]{:S(2)}) collective-permute-start(bf16[256,768]{1,0:T(8,128)(2,1)S(1)} %get-tuple-element.102), channel_id=1, source_target_pairs={{0,1},{1,0},{2,5},{3,4},{4,3},{5,2},{6,7},{7,6},{8,9},{9,8},{10,13... | collective-permute-start | bytes 1179656 | tf_op jit(solution)/shard_map/ppermute | solution.py:48
  145.9 5.7 %collective-permute-start.39 = (bf16[2,256,768]{2,1,0:T(8,128)(2,1)}, bf16[2,256,768]{2,1,0:T(8,128)(2,1)S(1)}, u32[]{:S(2)}, u32[]{:S(2)}) collective-permute-start(bf16[2,256,768]{2,1,0:T(8,128)(2,1)} %get-tuple-element.113), channel_id=1, source_target_pairs={{0,4},{1,5},{2,6},{3,7},{4,0},{5,1},{6,2},{7,3},{8,12},{9,13},{10,... | collective-permute-start | bytes 2359304 | tf_op jit(solution)/shard_map/ppermute | solution.py:48
  151.6 4.5 %collective-permute-start.42 = (f32[16,768]{1,0:T(8,128)S(1)}, f32[16,768]{1,0:T(8,128)S(1)}, u32[]{:S(2)}, u32[]{:S(2)}) collective-permute-start(f32[16,768]{1,0:T(8,128)S(1)} %get-tuple-element.117), channel_id=1, source_target_pairs={{0,4},{1,5},{2,6},{3,7},{4,0},{5,1},{6,2},{7,3},{8,12},{9,13},{10,... | collective-permute-start | bytes 147464 | tf_op jit(solution)/shard_map/ppermute | solution.py:48
  152.9 12.7 %collective-permute-start.40 = (bf16[256,768]{1,0:T(8,128)(2,1)S(1)}, bf16[256,768]{1,0:T(8,128)(2,1)S(1)}, u32[]{:S(2)}, u32[]{:S(2)}) collective-permute-start(bf16[256,768]{1,0:T(8,128)(2,1)S(1)} %fusion), channel_id=1, source_target_pairs={{0,1},{1,0},{2,3},{3,2},{4,5},{5,4},{6,7},{7,6},{8,9},{9,8},{10,11... | collective-permute-start | bytes 1179656 | tf_op jit(solution)/shard_map/ppermute | solution.py:48
  156.2 4.2 %collective-permute-start.43 = (f32[16,768]{1,0:T(8,128)S(1)}, f32[16,768]{1,0:T(8,128)S(1)}, u32[]{:S(2)}, u32[]{:S(2)}) collective-permute-start(f32[16,768]{1,0:T(8,128)S(1)} %add.103), channel_id=1, source_target_pairs={{0,8},{1,9},{2,10},{3,11},{4,12},{5,13},{6,14},{7,15},{8,0},{9,1},... | collective-permute-start | bytes 147464 | tf_op jit(solution)/shard_map/ppermute | solution.py:48
  160.3 4.2 %collective-permute-start.44 = (f32[16,768]{1,0:T(8,128)S(1)}, f32[16,768]{1,0:T(8,128)S(1)}, u32[]{:S(2)}, u32[]{:S(2)}) collective-permute-start(f32[16,768]{1,0:T(8,128)S(1)} %add.104), channel_id=1, source_target_pairs={{0,16},{1,17},{2,18},{3,19},{4,20},{5,21},{6,22},{7,23},{8,24},{9,... | collective-permute-start | bytes 147464 | tf_op jit(solution)/shard_map/ppermute | solution.py:48
  160.5 15.1 %collective-permute-start.52 = (bf16[96,1536]{1,0:T(8,128)(2,1)S(1)}, bf16[96,1536]{1,0:T(8,128)(2,1)S(1)}, u32[]{:S(2)}, u32[]{:S(2)}) collective-permute-start(bf16[96,1536]{1,0:T(8,128)(2,1)S(1)} %get-tuple-element.159), channel_id=1, source_target_pairs={{0,0},{1,2},{2,4},{3,6},{4,1},{5,3},{6,5},{7,7},{8,8},{9,10},{10,1... | collective-permute-start | bytes 884744 | tf_op jit(solution)/shard_map/ppermute | solution.py:48
  161.2 15.4 %collective-permute-start.53 = (bf16[96,1536]{1,0:T(8,128)(2,1)S(1)}, bf16[96,1536]{1,0:T(8,128)(2,1)S(1)}, u32[]{:S(2)}, u32[]{:S(2)}) collective-permute-start(bf16[96,1536]{1,0:T(8,128)(2,1)S(1)} %get-tuple-element.160), channel_id=1, source_target_pairs={{0,4},{1,6},{2,0},{3,2},{4,5},{5,7},{6,1},{7,3},{8,12},{9,14},{10,... | collective-permute-start | bytes 884744 | tf_op jit(solution)/shard_map/ppermute | solution.py:48
  166.9 6.4 %collective-permute-start.45 = (f32[16,768]{1,0:T(8,128)S(1)}, f32[16,768]{1,0:T(8,128)S(1)}, u32[]{:S(2)}, u32[]{:S(2)}) collective-permute-start(f32[16,768]{1,0:T(8,128)S(1)} %add.105), channel_id=1, source_target_pairs={{0,1},{1,0},{2,3},{3,2},{4,5},{5,4},{6,7},{7,6},{8,9},{9,8},{10,11... | collective-permute-start | bytes 147464 | tf_op jit(solution)/shard_map/ppermute | solution.py:48
  172.0 17.5 %collective-permute-start.47 = (bf16[192,768]{1,0:T(8,128)(2,1)S(1)}, bf16[192,768]{1,0:T(8,128)(2,1)S(1)}, u32[]{:S(2)}, u32[]{:S(2)}) collective-permute-start(bf16[192,768]{1,0:T(8,128)(2,1)S(1)} %get-tuple-element.128), channel_id=1, source_target_pairs={{0,8},{1,9},{2,10},{3,11},{4,12},{5,13},{6,14},{7,15},{8,0},{9,1},... | collective-permute-start | bytes 884744 | tf_op jit(solution)/shard_map/ppermute | solution.py:48
  172.8 16.7 %collective-permute-start.48 = (bf16[192,768]{1,0:T(8,128)(2,1)S(1)}, bf16[192,768]{1,0:T(8,128)(2,1)S(1)}, u32[]{:S(2)}, u32[]{:S(2)}) collective-permute-start(bf16[192,768]{1,0:T(8,128)(2,1)S(1)} %get-tuple-element.129), channel_id=1, source_target_pairs={{0,16},{1,17},{2,18},{3,19},{4,20},{5,21},{6,22},{7,23},{8,24},{9,... | collective-permute-start | bytes 884744 | tf_op jit(solution)/shard_map/ppermute | solution.py:48
  173.3 16.2 %collective-permute-start.49 = (bf16[192,768]{1,0:T(8,128)(2,1)S(1)}, bf16[192,768]{1,0:T(8,128)(2,1)S(1)}, u32[]{:S(2)}, u32[]{:S(2)}) collective-permute-start(bf16[192,768]{1,0:T(8,128)(2,1)S(1)} %get-tuple-element.130), channel_id=1, source_target_pairs={{0,24},{1,25},{2,26},{3,27},{4,28},{5,29},{6,30},{7,31},{8,16},{9,... | collective-permute-start | bytes 884744 | tf_op jit(solution)/shard_map/ppermute | solution.py:48
  175.6 13.9 %collective-permute-start.41 = (bf16[256,768]{1,0:T(8,128)(2,1)S(1)}, bf16[256,768]{1,0:T(8,128)(2,1)S(1)}, u32[]{:S(2)}, u32[]{:S(2)}) collective-permute-start(bf16[256,768]{1,0:T(8,128)(2,1)S(1)} %shard_map.253), channel_id=1, source_target_pairs={{0,0},{1,1},{2,4},{3,5},{4,2},{5,3},{6,6},{7,7},{8,8},{9,9},{10,12... | collective-permute-start | bytes 1179656 | tf_op jit(solution)/shard_map/ppermute | solution.py:48
  176.5 12.9 %collective-permute-start.46 = (f32[16,768]{1,0:T(8,128)S(1)}, f32[16,768]{1,0:T(8,128)S(1)}, u32[]{:S(2)}, u32[]{:S(2)}) collective-permute-start(f32[16,768]{1,0:T(8,128)S(1)} %add.106), channel_id=1, source_target_pairs={{0,2},{1,3},{2,0},{3,1},{4,6},{5,7},{6,4},{7,5},{8,10},{9,11},{10,... | collective-permute-start | bytes 147464 | tf_op jit(solution)/shard_map/ppermute | solution.py:48
  189.9 4.5 %collective-permute-start.50 = (bf16[96,768]{0,1:T(8,128)(2,1)S(1)}, bf16[96,768]{0,1:T(8,128)(2,1)S(1)}, u32[]{:S(2)}, u32[]{:S(2)}) collective-permute-start(bf16[96,768]{0,1:T(8,128)(2,1)S(1)} %bitcast.67), channel_id=1, source_target_pairs={{0,0},{1,2},{2,4},{3,6},{4,1},{5,3},{6,5},{7,7},{8,8},{9,10},{10,1... | collective-permute-start | bytes 442376 | tf_op jit(solution)/shard_map/ppermute | solution.py:48
  190.7 11.4 %collective-permute-start.51 = (bf16[96,768]{0,1:T(8,128)(2,1)S(1)}, bf16[96,768]{0,1:T(8,128)(2,1)S(1)}, u32[]{:S(2)}, u32[]{:S(2)}) collective-permute-start(bf16[96,768]{0,1:T(8,128)(2,1)S(1)} %bitcast.68), channel_id=1, source_target_pairs={{0,4},{1,6},{2,0},{3,2},{4,5},{5,7},{6,1},{7,3},{8,12},{9,14},{10,... | collective-permute-start | bytes 442376 | tf_op jit(solution)/shard_map/ppermute | solution.py:48
  (28 other events, 127.0 us)

commit v2 on v1

--- a/solution.py
+++ b/solution.py
@@ -220,7 +220,7 @@
 
 def attend_kernel(ids, mixed, attended, logs):
     length, wide = attended.shape
-    block = min(256, length)
+    block = min(512, length)
     tri = lax.broadcasted_iota(jnp.int32, (block, block), 0) <= lax.broadcasted_iota(
         jnp.int32, (block, block), 1
     )
@@ -361,7 +361,7 @@
     length, wide3 = mixed.shape
     wide = wide3 // 3
     rows = x0.shape[0]
-    block = min(256, length)
+    block = min(512, length)
     for i, gh in enumerate((gh0, gh1, gh2, gh3)):
         g_rows[chunk_at(ids, i, rows), :] = dot_nn(gh[...], w_all[:, wide3:])
     tri = lax.broadcasted_iota(jnp.int32, (block, block), 0) <= lax.broadcasted_iota(
@@ -619,7 +619,7 @@
     (grad_low,) = call(
         norm_one_kernel,
         [((rows, width), BF)],
-        [ids, gn1_own, gn1_core, gn1_z, x0, row_gain_one, grad_hidden],
+        [ids, gn1_own, gn1_core, gn1_z, after(x0, attn_grad[-1]), row_gain_one, grad_hidden],
         2,
         12,
     )
@@ -630,8 +630,8 @@
     attn_total = plane_total(attn_grad, attn_got, home)
     small = after(small, grad_low)
     small = small + plan.over_z(small)
+    attn_part = after(attn_total, small).astype(BF).reshape(2, shard, width)
     small = small + plan.over_two(small)
-    attn_part = after(attn_total, small).astype(BF).reshape(2, shard, width)
     attn_summed = plan.unspread(attn_part)
     output = (out_sent[0].astype(F32) + out_sent[1].astype(F32)).astype(BF)
     grad_tokens = home.astype(F32)

time: 207 us -> 200 us (0.966)
  waiting for transfers between devices: 63.9 us -> 55.6 us
    ppermute x54, waiting for transfers between devices: 63.9 us -> 55.6 us  [send(): return lax.ppermute(value, AXES, pairs)]
    unnamed x79 -> x71, local copies, waits for them, and re-layouts: 8.52 us -> 7.81 us
where the time goes in v2:
time: 200 us; the launch traced here: 197 us
  starting transfers between devices  82.5 us (41%)
  waiting for transfers between devices  55.6 us (28%)
  Pallas kernels  39.7 us (20%)
  local copies, waits for them, and re-layouts  12.4 us (6%)
  other arithmetic  5.25 us (3%)
    ppermute x54, starting transfers between devices, send(): return lax.ppermute(value, AXES, pairs)  82.5 us
    ppermute x54, waiting for transfers between devices, send(): return lax.ppermute(value, AXES, pairs)  55.6 us
    pallas_call x10, Pallas kernels, call(): pl.pallas_call(body, out_shape=shapes, in_specs=[pl.BlockSpec(memory_spac...  39.7 us
    unnamed x71, local copies, waits for them, and re-layouts  7.81 us
  transfers between devices with their start and end apart: 54, of which 21 were waited for; matrix products, arithmetic and copies ran while one was open for 4% of the time, Pallas kernels for 18%

profile of v2, /device:TPU:0, one launch (start us, length us, event | category | flops | bytes accessed | tf_op | source)
XLA Modules:
  0.0 197.2 jit_solution(9936993619196318512)
XLA Ops:
  0.7 1.1 copy.32
  2.0 0.9 copy.33
  3.6 5.8 %collective-permute-start.6 = (bf16[96,768]{1,0:T(8,128)(2,1)S(1)}, bf16[96,768]{1,0:T(8,128)(2,1)S(1)}, u32[]{:S(2)}, u32[]{:S(2)}) collective-permute-start(bf16[96,768]{1,0:T(8,128)(2,1)S(1)} %pad_maximum_fusion.5), channel_id=1, source_target_pairs={{0,2},{1,6},{2,3},{3,7},{4,0},{5,4},{6,1},{7,5},{8,10},{9,14},{10,... | collective-permute-start | bytes 442376 | tf_op jit(solution)/shard_map/ppermute | solution.py:48
  9.4 1.6 collective-permute-start
  13.3 2.5 %collective-permute-start.9 = (bf16[2,96,768]{2,1,0:T(8,128)(2,1)S(1)}, bf16[2,96,768]{2,1,0:T(8,128)(2,1)S(1)}, u32[]{:S(2)}, u32[]{:S(2)}) collective-permute-start(bf16[2,96,768]{2,1,0:T(8,128)(2,1)S(1)} %pad_maximum_fusion.1.refs_8_), channel_id=1, source_target_pairs={{0,24},{1,25},{2,26},{3,27},{4,28},{5,29},{6,30},{7,31},{8,16},{9,... | collective-permute-start | bytes 884744 | tf_op jit(solution)/shard_map/ppermute | solution.py:48
  17.3 12.3 %collective-permute-start.1 = (bf16[256,768]{1,0:T(8,128)(2,1)S(1)}, bf16[256,768]{1,0:T(8,128)(2,1)S(1)}, u32[]{:S(2)}, u32[]{:S(2)}) collective-permute-start(bf16[256,768]{1,0:T(8,128)(2,1)S(1)} %collective-permute-done.refs_1_.refs_9_.x0.x), channel_id=1, source_target_pairs={{0,1},{1,0},{2,3},{3,2},{4,5},{5,4},{6,7},{7,6},{8,9},{9,8},{10,11... | collective-permute-start | bytes 1179656 | tf_op jit(solution)/shard_map/ppermute | solution.py:48
  30.4 6.4 %collective-permute-start.12 = (bf16[96,1536]{1,0:T(8,128)(2,1)S(1)}, bf16[96,1536]{1,0:T(8,128)(2,1)S(1)}, u32[]{:S(2)}, u32[]{:S(2)}) collective-permute-start(bf16[96,1536]{1,0:T(8,128)(2,1)S(1)} %pad_maximum_fusion.2), channel_id=1, source_target_pairs={{0,2},{1,6},{2,3},{3,7},{4,0},{5,4},{6,1},{7,5},{8,10},{9,14},{10,... | collective-permute-start | bytes 884744 | tf_op jit(solution)/shard_map/ppermute | solution.py:48
  37.2 1.7 collective-permute-done.1.refs_2_.refs_10_.x1
  38.9 3.2 %collective-permute-done.12 = bf16[96,1536]{1,0:T(8,128)(2,1)S(1)} collective-permute-done((bf16[96,1536]{1,0:T(8,128)(2,1)S(1)}, bf16[96,1536]{1,0:T(8,128)(2,1)S(1)}, u32[]{:S(2)}, u32[]{:S(2)}) %collective-permute-start.12) | collective-permute-done | bytes 294944 | tf_op jit(solution)/shard_map/ppermute | solution.py:48
  42.7 1.7 collective-permute-start.14
  44.4 1.3 collective-permute-start.15
  45.6 1.2 collective-permute-start.10
  46.8 2.5 %shard_map.245 = (bf16[1024,768]{1,0:T(8,128)(2,1)S(1)}, bf16[1024,576]{1,0:T(8,128)(2,1)S(1)}, bf16[768,768]{1,0:T(8,128)(2,1)S(1)}) custom-call(s32[4]{0:T(128)S(1)} %pad_add_fusion.refs_0_.ids, bf16[256,768]{1,0:T(8,128)(2,1)S(1)} %collective-permute-done.refs_1_.refs_9_.x0.x, bf16[256,768]{1,0:T(8,128)(2,1)S(1)} %collective-permute-done.1.refs_2_.refs_10_.x1, ...), custom_call_target="tpu_custom_call" | custom-call | flops 3449999872 | bytes 9000000 | tf_op jit(solution)/shard_map/pallas_call | solution.py:163
  49.4 1.2 copy-done.15
  50.6 1.5 collective-permute-done.13.refs_18_
  52.0 7.5 %collective-permute-start.18 = (bf16[4,2,96,192]{3,2,1,0:T(8,128)(2,1)S(1)}, bf16[4,2,96,192]{3,2,1,0:T(8,128)(2,1)S(1)}, u32[]{:S(2)}, u32[]{:S(2)}) collective-permute-start(bf16[4,2,96,192]{3,2,1,0:T(8,128)(2,1)S(1)} %pad_maximum_fusion.refs_5_), channel_id=1, source_target_pairs={{0,1},{1,0},{2,3},{3,2},{4,5},{5,4},{6,7},{7,6},{8,9},{9,8},{10,11... | collective-permute-start | bytes 884744 | tf_op jit(solution)/shard_map/ppermute | solution.py:48
  59.5 4.5 %shard_map.246 = (bf16[1024,192]{1,0:T(8,128)(2,1)S(1)}, f32[8,1024]{1,0:T(8,128)S(1)}) custom-call(s32[4]{0:T(128)S(1)} %pad_add_fusion.refs_0_.ids, bf16[1024,576]{1,0:T(8,128)(2,1)S(1)} %get-tuple-element.104.mixed), custom_call_target="tpu_custom_call" | custom-call | flops 6899999744 | bytes 18000000 | tf_op jit(solution)/shard_map/pallas_call | solution.py:163
  64.2 1.5 collective-permute-start.21
  65.7 1.3 collective-permute-start.22
  67.0 0.8 collective-permute-start.23
  67.8 3.2 %collective-permute-done.18.refs_6_ = bf16[4,2,96,192]{3,2,1,0:T(8,128)(2,1)S(1)} collective-permute-done((bf16[4,2,96,192]{3,2,1,0:T(8,128)(2,1)S(1)}, bf16[4,2,96,192]{3,2,1,0:T(8,128)(2,1)S(1)}, u32[]{:S(2)}, u32[]{:S(2)}) %collective-permute-start.18) | collective-permute-done | bytes 294944 | tf_op jit(solution)/shard_map/ppermute | solution.py:48
  71.3 2.2 %collective-permute-done.21.refs_2_ = bf16[2,96,768]{2,1,0:T(8,128)(2,1)S(1)} collective-permute-done((bf16[2,96,768]{2,1,0:T(8,128)(2,1)S(1)}, bf16[2,96,768]{2,1,0:T(8,128)(2,1)S(1)}, u32[]{:S(2)}, u32[]{:S(2)}) %collective-permute-start.21) | collective-permute-done | bytes 294944 | tf_op jit(solution)/shard_map/ppermute | solution.py:48
  73.4 1.5 collective-permute-start.17
  75.0 5.2 %collective-permute-done.22.refs_3_ = bf16[2,96,768]{2,1,0:T(8,128)(2,1)S(1)} collective-permute-done((bf16[2,96,768]{2,1,0:T(8,128)(2,1)S(1)}, bf16[2,96,768]{2,1,0:T(8,128)(2,1)S(1)}, u32[]{:S(2)}, u32[]{:S(2)}) %collective-permute-start.22) | collective-permute-done | bytes 294944 | tf_op jit(solution)/shard_map/ppermute | solution.py:48
  80.1 1.1 collective-permute-done.23.refs_4_
  81.2 1.0 collective-permute-done.16.refs_2_
  84.1 6.6 %shard_map.247 = (f32[256,768]{1,0:T(8,128)S(1)}, bf16[1024,768]{1,0:T(8,128)(2,1)S(1)}, bf16[1024,768]{1,0:T(8,128)(2,1)S(1)}, bf16[1024,768]{1,0:T(8,128)(2,1)S(1)}, bf16[768,768]{1,0:T(8,128)(2,1)S(1)}) custom-call(s32[4]{0:T(128)S(1)} %pad_add_fusion.refs_0_.ids, bf16[1024,192]{1,0:T(8,128)(2,1)S(1)} %get-tuple-element.79.refs_1_.refs_7_, ...), custom_call_target="tpu_custom_call" | custom-call | flops 8049999872 | bytes 21000000 | tf_op jit(solution)/shard_map/pallas_call | solution.py:163
  90.7 3.3 %collective-permute-done.25.refs_6_.refs_3_ = bf16[256,768]{1,0:T(8,128)(2,1)S(1)} collective-permute-done((bf16[256,768]{1,0:T(8,128)(2,1)S(1)}, bf16[256,768]{1,0:T(8,128)(2,1)S(1)}, u32[]{:S(2)}, u32[]{:S(2)}) %collective-permute-start.25) | collective-permute-done | bytes 393248 | tf_op jit(solution)/shard_map/ppermute | solution.py:48
  94.0 1.7 collective-permute-done.27.refs_8_.refs_5_
  95.7 3.6 %shard_map.248 = (bf16[1024,768]{1,0:T(8,128)(2,1)S(1)}, f32[256,768]{1,0:T(8,128)S(1)}, f32[256,768]{1,0:T(8,128)S(1)}, bf16[2,256,768]{2,1,0:T(8,128)(2,1)S(1)...) custom-call(s32[4]{0:T(128)S(1)} %pad_add_fusion.refs_0_.ids, bf16[2,96,768]{2,1,0:T(8,128)(2,1)S(1)} %pad_maximum_fusion.4.refs_1_, ...), custom_call_target="tpu_custom_call" | custom-call | flops 5750000128 | bytes 15000000 | tf_op jit(solution)/shard_map/pallas_call | solution.py:163
  99.5 2.0 %shard_map.249 = (f32[256,768]{1,0:T(8,128)S(1)}, f32[256,768]{1,0:T(8,128)S(1)}, bf16[2,256,768]{2,1,0:T(8,128)(2,1)S(1)}) custom-call(s32[4]{0:T(128)S(1)} %pad_add_fusion.refs_0_.ids, bf16[1024,768]{1,0:T(8,128)(2,1)S(1)} %get-tuple-element.84.act.refs_6_, bf16[768,768]{1,0:T(8,128)(2,1)S(1)} %get-tuple-element.89.down_t), custom_call_target="tpu_custom_call" | custom-call | flops 2300000000 | bytes 6000000 | tf_op jit(solution)/shard_map/pallas_call | solution.py:163
  102.8 3.5 %shard_map.250 = (f32[192,1536]{1,0:T(8,128)S(1)}, bf16[192,1536]{1,0:T(8,128)(2,1)S(1)}, bf16[192,1536]{1,0:T(8,128)(2,1)S(1)}, bf16[192,1536]{1,0:T(8,128)(2,1)S(1)}) custom-call(s32[4]{0:T(128)S(1)} %pad_add_fusion.refs_0_.ids, bf16[1024,768]{1,0:T(8,128)(2,1)S(1)} %get-tuple-element.96.refs_1_, ...), custom_call_target="tpu_custom_call" | custom-call | flops 5750000128 | bytes 15000000 | tf_op jit(solution)/shard_map/pallas_call | solution.py:163
  107.1 1.7 collective-permute-start.36
  108.8 4.5 %collective-permute-done.30.got_z = bf16[256,768]{1,0:T(8,128)(2,1)S(1)} collective-permute-done((bf16[256,768]{1,0:T(8,128)(2,1)S(1)}, bf16[256,768]{1,0:T(8,128)(2,1)S(1)}, u32[]{:S(2)}, u32[]{:S(2)}) %collective-permute-start.30) | collective-permute-done | bytes 393248 | tf_op jit(solution)/shard_map/ppermute | solution.py:48
  113.3 1.3 shard_map.251
  114.6 0.9 copy-done.11
  116.2 5.3 %collective-permute-done.35 = bf16[192,1536]{1,0:T(8,128)(2,1)S(1)} collective-permute-done((bf16[192,1536]{1,0:T(8,128)(2,1)S(1)}, bf16[192,1536]{1,0:T(8,128)(2,1)S(1)}, u32[]{:S(2)}, u32[]{:S(2)}) %collective-permute-start.35) | collective-permute-done | bytes 589856 | tf_op jit(solution)/shard_map/ppermute | solution.py:48
  121.9 3.9 %collective-permute-done.31.gh1.refs_4_ = bf16[256,768]{1,0:T(8,128)(2,1)S(1)} collective-permute-done((bf16[256,768]{1,0:T(8,128)(2,1)S(1)}, bf16[256,768]{1,0:T(8,128)(2,1)S(1)}, u32[]{:S(2)}, u32[]{:S(2)}) %collective-permute-start.31) | collective-permute-done | bytes 393248 | tf_op jit(solution)/shard_map/ppermute | solution.py:48
  125.8 1.5 collective-permute-start.38
  127.6 1.6 collective-permute-start.32
  129.2 1.1 collective-permute-start.33
  130.4 11.9 %shard_map.252 = (bf16[1024,576]{1,0:T(8,128)(2,1)S(1)}, f32[256,768]{1,0:T(8,128)S(1)}, f32[256,768]{1,0:T(8,128)S(1)}, bf16[2,256,768]{2,1,0:T(8,128)(2,1)}, f32[16,768]{1,0:T(8,128)S(1)}) custom-call(s32[4]{0:T(128)S(1)} %pad_add_fusion.refs_0_.ids, bf16[1024,576]{1,0:T(8,128)(2,1)S(1)} %get-tuple-element.104.mixed, ...), custom_call_target="tpu_custom_call" | custom-call | flops 13799999488 | bytes 36000000 | tf_op jit(solution)/shard_map/pallas_call | solution.py:163
  142.2 0.9 copy-done.13
  143.1 1.1 copy-done.17
  144.2 0.8 copy-done.23
  145.0 2.8 %collective-permute-start.39 = (bf16[2,256,768]{2,1,0:T(8,128)(2,1)}, bf16[2,256,768]{2,1,0:T(8,128)(2,1)S(1)}, u32[]{:S(2)}, u32[]{:S(2)}) collective-permute-start(bf16[2,256,768]{2,1,0:T(8,128)(2,1)} %get-tuple-element.114), channel_id=1, source_target_pairs={{0,4},{1,5},{2,6},{3,7},{4,0},{5,1},{6,2},{7,3},{8,12},{9,13},{10,... | collective-permute-start | bytes 2359304 | tf_op jit(solution)/shard_map/ppermute | solution.py:48
  147.9 2.1 %add_convert_fusion.1 = bf16[256,768]{1,0:T(8,128)(2,1)} fusion(bf16[256,768]{1,0:T(8,128)(2,1)} %collective-permute-done.33, bf16[256,768]{1,0:T(8,128)(2,1)} %collective-permute-done.32), kind=kLoop, calls=%fused_computation.10 | loop fusion | flops 786432 | bytes 1179648 | tf_op jit(solution)/shard_map/convert_element_type | solution.py:636
  150.1 3.4 %collective-permute-start.40 = (bf16[256,768]{1,0:T(8,128)(2,1)S(1)}, bf16[256,768]{1,0:T(8,128)(2,1)S(1)}, u32[]{:S(2)}, u32[]{:S(2)}) collective-permute-start(bf16[256,768]{1,0:T(8,128)(2,1)S(1)} %fusion), channel_id=1, source_target_pairs={{0,1},{1,0},{2,3},{3,2},{4,5},{5,4},{6,7},{7,6},{8,9},{9,8},{10,11... | collective-permute-start | bytes 1179656 | tf_op jit(solution)/shard_map/ppermute | solution.py:48
  156.1 1.7 collective-permute-start.53
  157.9 1.0 collective-permute-done.43
  159.4 2.6 %shard_map.253 = (f32[192,768]{1,0:T(8,128)S(1)}, bf16[192,768]{1,0:T(8,128)(2,1)S(1)}, bf16[192,768]{1,0:T(8,128)(2,1)S(1)}, bf16[192,768]{1,0:T(8,128)(2,1)S(1)}) custom-call(s32[4]{0:T(128)S(1)} %pad_add_fusion.refs_0_.ids, bf16[1024,768]{1,0:T(8,128)(2,1)S(1)} %copy-done.16, bf16[1024,576]{1,0:T(8,128)(2,1)S(1)} %copy-done.18, ...), custom_call_target="tpu_custom_call" | custom-call | flops 3449999872 | bytes 9000000 | tf_op jit(solution)/shard_map/pallas_call | solution.py:163
  162.0 1.3 collective-permute-done.44
  163.3 0.9 collective-permute-start.47
  164.2 1.2 collective-permute-start.48
  165.5 1.4 collective-permute-start.49
  166.8 1.2 shard_map.254
  168.7 3.4 %collective-permute-done.53 = bf16[96,1536]{1,0:T(8,128)(2,1)S(1)} collective-permute-done((bf16[96,1536]{1,0:T(8,128)(2,1)S(1)}, bf16[96,1536]{1,0:T(8,128)(2,1)S(1)}, u32[]{:S(2)}, u32[]{:S(2)}) %collective-permute-start.53) | collective-permute-done | bytes 294944 | tf_op jit(solution)/shard_map/ppermute | solution.py:48
  172.2 4.3 %collective-permute-done.45 = f32[16,768]{1,0:T(8,128)S(1)} collective-permute-done((f32[16,768]{1,0:T(8,128)S(1)}, f32[16,768]{1,0:T(8,128)S(1)}, u32[]{:S(2)}, u32[]{:S(2)}) %collective-permute-start.45) | collective-permute-done | bytes 49184 | tf_op jit(solution)/shard_map/ppermute | solution.py:48
  176.5 3.4 %collective-permute-start.46 = (f32[16,768]{1,0:T(8,128)S(1)}, f32[16,768]{1,0:T(8,128)S(1)}, u32[]{:S(2)}, u32[]{:S(2)}) collective-permute-start(f32[16,768]{1,0:T(8,128)S(1)} %add.106), channel_id=1, source_target_pairs={{0,2},{1,3},{2,0},{3,1},{4,6},{5,7},{6,4},{7,5},{8,10},{9,11},{10,... | collective-permute-start | bytes 147464 | tf_op jit(solution)/shard_map/ppermute | solution.py:48
  181.2 4.7 %collective-permute-start.51 = (bf16[96,768]{0,1:T(8,128)(2,1)S(1)}, bf16[96,768]{0,1:T(8,128)(2,1)S(1)}, u32[]{:S(2)}, u32[]{:S(2)}) collective-permute-start(bf16[96,768]{0,1:T(8,128)(2,1)S(1)} %bitcast.68), channel_id=1, source_target_pairs={{0,4},{1,6},{2,0},{3,2},{4,5},{5,7},{6,1},{7,3},{8,12},{9,14},{10,... | collective-permute-start | bytes 442376 | tf_op jit(solution)/shard_map/ppermute | solution.py:48
  185.9 0.8 slice_bitcast_fusion.4
  188.1 0.9 convert_element_type.99
  189.0 6.3 %collective-permute-done.51 = bf16[96,768]{0,1:T(8,128)(2,1)S(1)} collective-permute-done((bf16[96,768]{0,1:T(8,128)(2,1)S(1)}, bf16[96,768]{0,1:T(8,128)(2,1)S(1)}, u32[]{:S(2)}, u32[]{:S(2)}) %collective-permute-start.51) | collective-permute-done | bytes 147488 | tf_op jit(solution)/shard_map/ppermute | solution.py:48
  196.0 0.9 copy.37
  (174 shorter events, 19.6 us)
Async XLA Ops:
  0.6 15.2 %copy-start.25 = (bf16[768,96]{0,1:T(8,128)(2,1)S(1)}, bf16[768,96]{0,1:T(8,128)(2,1)}, u32[]{:S(2)}) copy-start(bf16[768,96]{0,1:T(8,128)(2,1)} %param.25) | copy-start | bytes 442372
  0.7 15.2 %copy-start.26 = (bf16[96,768]{1,0:T(8,128)(2,1)S(1)}, bf16[96,768]{1,0:T(8,128)(2,1)}, u32[]{:S(2)}) copy-start(bf16[96,768]{1,0:T(8,128)(2,1)} %param.23) | copy-start | bytes 442372
  0.7 15.3 %copy-start.28 = (f32[768]{0:T(1024)S(1)}, f32[768]{0:T(1024)}, u32[]{:S(2)}) copy-start(f32[768]{0:T(1024)} %param.15) | copy-start | bytes 9220
  0.7 15.3 %copy-start.29 = (f32[768]{0:T(1024)S(1)}, f32[768]{0:T(1024)}, u32[]{:S(2)}) copy-start(f32[768]{0:T(1024)} %param.16) | copy-start | bytes 9220
  3.0 10.3 %collective-permute-start.5 = (bf16[96,768]{1,0:T(8,128)(2,1)S(1)}, bf16[96,768]{1,0:T(8,128)(2,1)S(1)}, u32[]{:S(2)}, u32[]{:S(2)}) collective-permute-start(bf16[96,768]{1,0:T(8,128)(2,1)S(1)} %pad_maximum_fusion.5), channel_id=1, source_target_pairs={{0,0},{1,4},{2,1},{3,5},{4,2},{5,6},{6,3},{7,7},{8,8},{9,12},{10,9... | collective-permute-start | bytes 442376 | tf_op jit(solution)/shard_map/ppermute | solution.py:48
  3.6 9.6 %collective-permute-start.6 = (bf16[96,768]{1,0:T(8,128)(2,1)S(1)}, bf16[96,768]{1,0:T(8,128)(2,1)S(1)}, u32[]{:S(2)}, u32[]{:S(2)}) collective-permute-start(bf16[96,768]{1,0:T(8,128)(2,1)S(1)} %pad_maximum_fusion.5), channel_id=1, source_target_pairs={{0,2},{1,6},{2,3},{3,7},{4,0},{5,4},{6,1},{7,5},{8,10},{9,14},{10,... | collective-permute-start | bytes 442376 | tf_op jit(solution)/shard_map/ppermute | solution.py:48
  9.4 7.8 %collective-permute-start = (bf16[256,768]{1,0:T(8,128)(2,1)}, bf16[256,768]{1,0:T(8,128)(2,1)S(1)}, u32[]{:S(2)}, u32[]{:S(2)}) collective-permute-start(bf16[256,768]{1,0:T(8,128)(2,1)} %param.14), channel_id=1, source_target_pairs={{0,0},{1,1},{2,4},{3,5},{4,2},{5,3},{6,6},{7,7},{8,8},{9,9},{10,12... | collective-permute-start | bytes 1179656 | tf_op jit(solution)/shard_map/ppermute | solution.py:48
  12.6 3.4 %collective-permute-start.4 = (f32[1344]{0:T(1024)S(1)}, f32[1344]{0:T(1024)S(1)}, u32[]{:S(2)}, u32[]{:S(2)}) collective-permute-start(f32[1344]{0:T(1024)S(1)} %pad_maximum_fusion.6), channel_id=1, source_target_pairs={{0,0},{1,4},{2,1},{3,5},{4,2},{5,6},{6,3},{7,7},{8,8},{9,12},{10,9... | collective-permute-start | bytes 16136 | tf_op jit(solution)/shard_map/ppermute | solution.py:48
  13.3 16.3 %collective-permute-start.9 = (bf16[2,96,768]{2,1,0:T(8,128)(2,1)S(1)}, bf16[2,96,768]{2,1,0:T(8,128)(2,1)S(1)}, u32[]{:S(2)}, u32[]{:S(2)}) collective-permute-start(bf16[2,96,768]{2,1,0:T(8,128)(2,1)S(1)} %pad_maximum_fusion.1.refs_8_), channel_id=1, source_target_pairs={{0,24},{1,25},{2,26},{3,27},{4,28},{5,29},{6,30},{7,31},{8,16},{9,... | collective-permute-start | bytes 884744 | tf_op jit(solution)/shard_map/ppermute | solution.py:48
  16.0 20.8 %collective-permute-start.7 = (bf16[2,96,768]{2,1,0:T(8,128)(2,1)S(1)}, bf16[2,96,768]{2,1,0:T(8,128)(2,1)S(1)}, u32[]{:S(2)}, u32[]{:S(2)}) collective-permute-start(bf16[2,96,768]{2,1,0:T(8,128)(2,1)S(1)} %pad_maximum_fusion.1.refs_8_), channel_id=1, source_target_pairs={{0,8},{1,9},{2,10},{3,11},{4,12},{5,13},{6,14},{7,15},{8,0},{9,1},... | collective-permute-start | bytes 884744 | tf_op jit(solution)/shard_map/ppermute | solution.py:48
  16.6 13.7 %collective-permute-start.8 = (bf16[2,96,768]{2,1,0:T(8,128)(2,1)S(1)}, bf16[2,96,768]{2,1,0:T(8,128)(2,1)S(1)}, u32[]{:S(2)}, u32[]{:S(2)}) collective-permute-start(bf16[2,96,768]{2,1,0:T(8,128)(2,1)S(1)} %pad_maximum_fusion.1.refs_8_), channel_id=1, source_target_pairs={{0,16},{1,17},{2,18},{3,19},{4,20},{5,21},{6,22},{7,23},{8,24},{9,... | collective-permute-start | bytes 884744 | tf_op jit(solution)/shard_map/ppermute | solution.py:48
  17.2 66.9 %copy-start = (bf16[256,768]{1,0:T(8,128)(2,1)}, bf16[256,768]{1,0:T(8,128)(2,1)S(1)}, u32[]{:S(2)}) copy-start(bf16[256,768]{1,0:T(8,128)(2,1)S(1)} %collective-permute-done.refs_1_.refs_9_.x0.x) | copy-start | bytes 1179652
  17.3 21.6 %collective-permute-start.1 = (bf16[256,768]{1,0:T(8,128)(2,1)S(1)}, bf16[256,768]{1,0:T(8,128)(2,1)S(1)}, u32[]{:S(2)}, u32[]{:S(2)}) collective-permute-start(bf16[256,768]{1,0:T(8,128)(2,1)S(1)} %collective-permute-done.refs_1_.refs_9_.x0.x), channel_id=1, source_target_pairs={{0,1},{1,0},{2,3},{3,2},{4,5},{5,4},{6,7},{7,6},{8,9},{9,8},{10,11... | collective-permute-start | bytes 1179656 | tf_op jit(solution)/shard_map/ppermute | solution.py:48
  29.6 14.8 %collective-permute-start.2 = (bf16[256,768]{1,0:T(8,128)(2,1)S(1)}, bf16[256,768]{1,0:T(8,128)(2,1)S(1)}, u32[]{:S(2)}, u32[]{:S(2)}) collective-permute-start(bf16[256,768]{1,0:T(8,128)(2,1)S(1)} %collective-permute-done.refs_1_.refs_9_.x0.x), channel_id=1, source_target_pairs={{0,4},{1,5},{2,6},{3,7},{4,0},{5,1},{6,2},{7,3},{8,12},{9,13},{10,... | collective-permute-start | bytes 1179656 | tf_op jit(solution)/shard_map/ppermute | solution.py:48
  29.6 9.2 %collective-permute-start.11 = (bf16[96,1536]{1,0:T(8,128)(2,1)S(1)}, bf16[96,1536]{1,0:T(8,128)(2,1)S(1)}, u32[]{:S(2)}, u32[]{:S(2)}) collective-permute-start(bf16[96,1536]{1,0:T(8,128)(2,1)S(1)} %pad_maximum_fusion.2), channel_id=1, source_target_pairs={{0,0},{1,4},{2,1},{3,5},{4,2},{5,6},{6,3},{7,7},{8,8},{9,12},{10,9... | collective-permute-start | bytes 884744 | tf_op jit(solution)/shard_map/ppermute | solution.py:48
  30.4 11.6 %collective-permute-start.12 = (bf16[96,1536]{1,0:T(8,128)(2,1)S(1)}, bf16[96,1536]{1,0:T(8,128)(2,1)S(1)}, u32[]{:S(2)}, u32[]{:S(2)}) collective-permute-start(bf16[96,1536]{1,0:T(8,128)(2,1)S(1)} %pad_maximum_fusion.2), channel_id=1, source_target_pairs={{0,2},{1,6},{2,3},{3,7},{4,0},{5,4},{6,1},{7,5},{8,10},{9,14},{10,... | collective-permute-start | bytes 884744 | tf_op jit(solution)/shard_map/ppermute | solution.py:48
  37.1 29.9 %collective-permute-start.19 = (bf16[4,2,96,192]{3,2,1,0:T(8,128)(2,1)S(1)}, bf16[4,2,96,192]{3,2,1,0:T(8,128)(2,1)S(1)}, u32[]{:S(2)}, u32[]{:S(2)}) collective-permute-start(bf16[4,2,96,192]{3,2,1,0:T(8,128)(2,1)S(1)} %pad_maximum_fusion.refs_5_), channel_id=1, source_target_pairs={{0,4},{1,5},{2,6},{3,7},{4,0},{5,1},{6,2},{7,3},{8,12},{9,13},{10,... | collective-permute-start | bytes 884744 | tf_op jit(solution)/shard_map/ppermute | solution.py:48
  38.8 6.8 %collective-permute-start.3 = (bf16[256,768]{1,0:T(8,128)(2,1)S(1)}, bf16[256,768]{1,0:T(8,128)(2,1)S(1)}, u32[]{:S(2)}, u32[]{:S(2)}) collective-permute-start(bf16[256,768]{1,0:T(8,128)(2,1)S(1)} %collective-permute-done.1.refs_2_.refs_10_.x1), channel_id=1, source_target_pairs={{0,4},{1,5},{2,6},{3,7},{4,0},{5,1},{6,2},{7,3},{8,12},{9,13},{10,... | collective-permute-start | bytes 1179656 | tf_op jit(solution)/shard_map/ppermute | solution.py:48
  42.1 9.9 %collective-permute-start.13 = (bf16[2,96,768]{2,1,0:T(8,128)(2,1)S(1)}, bf16[2,96,768]{2,1,0:T(8,128)(2,1)S(1)}, u32[]{:S(2)}, u32[]{:S(2)}) collective-permute-start(bf16[2,96,768]{2,1,0:T(8,128)(2,1)S(1)} %pad_maximum_fusion.3.refs_17_), channel_id=1, source_target_pairs={{0,8},{1,9},{2,10},{3,11},{4,12},{5,13},{6,14},{7,15},{8,0},{9,1},... | collective-permute-start | bytes 884744 | tf_op jit(solution)/shard_map/ppermute | solution.py:48
  42.7 21.4 %collective-permute-start.14 = (bf16[2,96,768]{2,1,0:T(8,128)(2,1)S(1)}, bf16[2,96,768]{2,1,0:T(8,128)(2,1)S(1)}, u32[]{:S(2)}, u32[]{:S(2)}) collective-permute-start(bf16[2,96,768]{2,1,0:T(8,128)(2,1)S(1)} %pad_maximum_fusion.3.refs_17_), channel_id=1, source_target_pairs={{0,16},{1,17},{2,18},{3,19},{4,20},{5,21},{6,22},{7,23},{8,24},{9,... | collective-permute-start | bytes 884744 | tf_op jit(solution)/shard_map/ppermute | solution.py:48
  44.4 19.7 %collective-permute-start.15 = (bf16[2,96,768]{2,1,0:T(8,128)(2,1)S(1)}, bf16[2,96,768]{2,1,0:T(8,128)(2,1)S(1)}, u32[]{:S(2)}, u32[]{:S(2)}) collective-permute-start(bf16[2,96,768]{2,1,0:T(8,128)(2,1)S(1)} %pad_maximum_fusion.3.refs_17_), channel_id=1, source_target_pairs={{0,24},{1,25},{2,26},{3,27},{4,28},{5,29},{6,30},{7,31},{8,16},{9,... | collective-permute-start | bytes 884744 | tf_op jit(solution)/shard_map/ppermute | solution.py:48
  45.6 18.4 %collective-permute-start.10 = (bf16[256,768]{1,0:T(8,128)(2,1)S(1)}, bf16[256,768]{1,0:T(8,128)(2,1)S(1)}, u32[]{:S(2)}, u32[]{:S(2)}) collective-permute-start(bf16[256,768]{1,0:T(8,128)(2,1)S(1)} %copy-done.33), channel_id=1, source_target_pairs={{0,0},{1,1},{2,4},{3,5},{4,2},{5,3},{6,6},{7,7},{8,8},{9,9},{10,12... | collective-permute-start | bytes 1179656 | tf_op jit(solution)/shard_map/ppermute | solution.py:48
  50.6 31.8 %copy-start.30 = (f32[768]{0:T(1024)S(1)}, f32[768]{0:T(1024)}, u32[]{:S(2)}) copy-start(f32[768]{0:T(1024)} %param.21) | copy-start | bytes 9220
  50.6 31.8 %copy-start.31 = (f32[768]{0:T(1024)S(1)}, f32[768]{0:T(1024)}, u32[]{:S(2)}) copy-start(f32[768]{0:T(1024)} %param.20) | copy-start | bytes 9220
  50.6 31.8 %copy-start.32 = (f32[768]{0:T(1024)S(1)}, f32[768]{0:T(1024)}, u32[]{:S(2)}) copy-start(f32[768]{0:T(1024)} %param.22) | copy-start | bytes 9220
  52.0 18.9 %collective-permute-start.18 = (bf16[4,2,96,192]{3,2,1,0:T(8,128)(2,1)S(1)}, bf16[4,2,96,192]{3,2,1,0:T(8,128)(2,1)S(1)}, u32[]{:S(2)}, u32[]{:S(2)}) collective-permute-start(bf16[4,2,96,192]{3,2,1,0:T(8,128)(2,1)S(1)} %pad_maximum_fusion.refs_5_), channel_id=1, source_target_pairs={{0,1},{1,0},{2,3},{3,2},{4,5},{5,4},{6,7},{7,6},{8,9},{9,8},{10,11... | collective-permute-start | bytes 884744 | tf_op jit(solution)/shard_map/ppermute | solution.py:48
  64.1 18.1 %collective-permute-start.16 = (bf16[1024,192]{1,0:T(8,128)(2,1)S(1)}, bf16[1024,192]{1,0:T(8,128)(2,1)S(1)}, u32[]{:S(2)}, u32[]{:S(2)}) collective-permute-start(bf16[1024,192]{1,0:T(8,128)(2,1)S(1)} %get-tuple-element.79.refs_1_.refs_7_), channel_id=1, source_target_pairs={{0,1},{1,0},{2,3},{3,2},{4,5},{5,4},{6,7},{7,6},{8,9},{9,8},{10,11... | collective-permute-start | bytes 1179656 | tf_op jit(solution)/shard_map/ppermute | solution.py:48
  64.2 9.2 %collective-permute-start.21 = (bf16[2,96,768]{2,1,0:T(8,128)(2,1)S(1)}, bf16[2,96,768]{2,1,0:T(8,128)(2,1)S(1)}, u32[]{:S(2)}, u32[]{:S(2)}) collective-permute-start(bf16[2,96,768]{2,1,0:T(8,128)(2,1)S(1)} %pad_maximum_fusion.4.refs_1_), channel_id=1, source_target_pairs={{0,8},{1,9},{2,10},{3,11},{4,12},{5,13},{6,14},{7,15},{8,0},{9,1},... | collective-permute-start | bytes 884744 | tf_op jit(solution)/shard_map/ppermute | solution.py:48
  65.7 14.5 %collective-permute-start.22 = (bf16[2,96,768]{2,1,0:T(8,128)(2,1)S(1)}, bf16[2,96,768]{2,1,0:T(8,128)(2,1)S(1)}, u32[]{:S(2)}, u32[]{:S(2)}) collective-permute-start(bf16[2,96,768]{2,1,0:T(8,128)(2,1)S(1)} %pad_maximum_fusion.4.refs_1_), channel_id=1, source_target_pairs={{0,16},{1,17},{2,18},{3,19},{4,20},{5,21},{6,22},{7,23},{8,24},{9,... | collective-permute-start | bytes 884744 | tf_op jit(solution)/shard_map/ppermute | solution.py:48
  67.0 14.3 %collective-permute-start.23 = (bf16[2,96,768]{2,1,0:T(8,128)(2,1)S(1)}, bf16[2,96,768]{2,1,0:T(8,128)(2,1)S(1)}, u32[]{:S(2)}, u32[]{:S(2)}) collective-permute-start(bf16[2,96,768]{2,1,0:T(8,128)(2,1)S(1)} %pad_maximum_fusion.4.refs_1_), channel_id=1, source_target_pairs={{0,24},{1,25},{2,26},{3,27},{4,28},{5,29},{6,30},{7,31},{8,16},{9,... | collective-permute-start | bytes 884744 | tf_op jit(solution)/shard_map/ppermute | solution.py:48
  71.0 11.2 %collective-permute-start.20 = (bf16[4,2,96,192]{3,2,1,0:T(8,128)(2,1)S(1)}, bf16[4,2,96,192]{3,2,1,0:T(8,128)(2,1)S(1)}, u32[]{:S(2)}, u32[]{:S(2)}) collective-permute-start(bf16[4,2,96,192]{3,2,1,0:T(8,128)(2,1)S(1)} %collective-permute-done.18.refs_6_), channel_id=1, source_target_pairs={{0,4},{1,5},{2,6},{3,7},{4,0},{5,1},{6,2},{7,3},{8,12},{9,13},{10,... | collective-permute-start | bytes 884744 | tf_op jit(solution)/shard_map/ppermute | solution.py:48
  73.4 10.2 %collective-permute-start.17 = (bf16[1024,192]{1,0:T(8,128)(2,1)S(1)}, bf16[1024,192]{1,0:T(8,128)(2,1)S(1)}, u32[]{:S(2)}, u32[]{:S(2)}) collective-permute-start(bf16[1024,192]{1,0:T(8,128)(2,1)S(1)} %get-tuple-element.79.refs_1_.refs_7_), channel_id=1, source_target_pairs={{0,4},{1,5},{2,6},{3,7},{4,0},{5,1},{6,2},{7,3},{8,12},{9,13},{10,... | collective-permute-start | bytes 1179656 | tf_op jit(solution)/shard_map/ppermute | solution.py:48
  82.2 1.9 collective-permute-start.24
  82.4 11.5 %collective-permute-start.26 = (bf16[256,768]{1,0:T(8,128)(2,1)S(1)}, bf16[256,768]{1,0:T(8,128)(2,1)S(1)}, u32[]{:S(2)}, u32[]{:S(2)}) collective-permute-start(bf16[256,768]{1,0:T(8,128)(2,1)S(1)} %collective-permute-done.10.refs_5_.refs_2_.g), channel_id=1, source_target_pairs={{0,4},{1,5},{2,6},{3,7},{4,0},{5,1},{6,2},{7,3},{8,12},{9,13},{10,... | collective-permute-start | bytes 1179656 | tf_op jit(solution)/shard_map/ppermute | solution.py:48
  82.8 11.1 %collective-permute-start.25 = (bf16[256,768]{1,0:T(8,128)(2,1)S(1)}, bf16[256,768]{1,0:T(8,128)(2,1)S(1)}, u32[]{:S(2)}, u32[]{:S(2)}) collective-permute-start(bf16[256,768]{1,0:T(8,128)(2,1)S(1)} %collective-permute-done.10.refs_5_.refs_2_.g), channel_id=1, source_target_pairs={{0,1},{1,0},{2,3},{3,2},{4,5},{5,4},{6,7},{7,6},{8,9},{9,8},{10,11... | collective-permute-start | bytes 1179656 | tf_op jit(solution)/shard_map/ppermute | solution.py:48
  94.0 1.7 collective-permute-start.27
  99.3 2.6 %collective-permute-start.29 = (bf16[2,256,768]{2,1,0:T(8,128)(2,1)S(1)}, bf16[2,256,768]{2,1,0:T(8,128)(2,1)S(1)}, u32[]{:S(2)}, u32[]{:S(2)}) collective-permute-start(bf16[2,256,768]{2,1,0:T(8,128)(2,1)S(1)} %get-tuple-element.93), channel_id=1, source_target_pairs={{0,4},{1,5},{2,6},{3,7},{4,0},{5,1},{6,2},{7,3},{8,12},{9,13},{10,... | collective-permute-start | bytes 2359304 | tf_op jit(solution)/shard_map/ppermute | solution.py:48
  101.5 25.8 %collective-permute-start.28 = (bf16[2,256,768]{2,1,0:T(8,128)(2,1)S(1)}, bf16[2,256,768]{2,1,0:T(8,128)(2,1)S(1)}, u32[]{:S(2)}, u32[]{:S(2)}) collective-permute-start(bf16[2,256,768]{2,1,0:T(8,128)(2,1)S(1)} %get-tuple-element.91), channel_id=1, source_target_pairs={{0,4},{1,5},{2,6},{3,7},{4,0},{5,1},{6,2},{7,3},{8,12},{9,13},{10,... | collective-permute-start | bytes 2359304 | tf_op jit(solution)/shard_map/ppermute | solution.py:48
  102.0 11.2 %collective-permute-start.30 = (bf16[256,768]{1,0:T(8,128)(2,1)S(1)}, bf16[256,768]{1,0:T(8,128)(2,1)S(1)}, u32[]{:S(2)}, u32[]{:S(2)}) collective-permute-start(bf16[256,768]{1,0:T(8,128)(2,1)S(1)} %fusion.2), channel_id=1, source_target_pairs={{0,1},{1,0},{2,3},{3,2},{4,5},{5,4},{6,7},{7,6},{8,9},{9,8},{10,11... | collective-permute-start | bytes 1179656 | tf_op jit(solution)/shard_map/ppermute | solution.py:48
  106.3 15.1 %collective-permute-start.35 = (bf16[192,1536]{1,0:T(8,128)(2,1)S(1)}, bf16[192,1536]{1,0:T(8,128)(2,1)S(1)}, u32[]{:S(2)}, u32[]{:S(2)}) collective-permute-start(bf16[192,1536]{1,0:T(8,128)(2,1)S(1)} %get-tuple-element.107), channel_id=1, source_target_pairs={{0,8},{1,9},{2,10},{3,11},{4,12},{5,13},{6,14},{7,15},{8,0},{9,1},... | collective-permute-start | bytes 1769480 | tf_op jit(solution)/shard_map/ppermute | solution.py:48
  107.1 14.8 %collective-permute-start.36 = (bf16[192,1536]{1,0:T(8,128)(2,1)S(1)}, bf16[192,1536]{1,0:T(8,128)(2,1)S(1)}, u32[]{:S(2)}, u32[]{:S(2)}) collective-permute-start(bf16[192,1536]{1,0:T(8,128)(2,1)S(1)} %get-tuple-element.108), channel_id=1, source_target_pairs={{0,16},{1,17},{2,18},{3,19},{4,20},{5,21},{6,22},{7,23},{8,24},{9,... | collective-permute-start | bytes 1769480 | tf_op jit(solution)/shard_map/ppermute | solution.py:48
  113.3 14.1 %copy-start.27 = (f32[768]{0:T(1024)S(1)}, f32[768]{0:T(1024)}, u32[]{:S(2)}) copy-start(f32[768]{0:T(1024)} %param.26) | copy-start | bytes 9220
  115.5 14.9 %copy-start.3 = (bf16[256,768]{1,0:T(8,128)(2,1)}, bf16[256,768]{1,0:T(8,128)(2,1)S(1)}, u32[]{:S(2)}) copy-start(bf16[256,768]{1,0:T(8,128)(2,1)S(1)} %get-tuple-element.100.gh0.refs_3_) | copy-start | bytes 1179652
  115.5 10.3 %collective-permute-start.31 = (bf16[256,768]{1,0:T(8,128)(2,1)S(1)}, bf16[256,768]{1,0:T(8,128)(2,1)S(1)}, u32[]{:S(2)}, u32[]{:S(2)}) collective-permute-start(bf16[256,768]{1,0:T(8,128)(2,1)S(1)} %get-tuple-element.100.gh0.refs_3_), channel_id=1, source_target_pairs={{0,1},{1,0},{2,3},{3,2},{4,5},{5,4},{6,7},{7,6},{8,9},{9,8},{10,11... | collective-permute-start | bytes 1179656 | tf_op jit(solution)/shard_map/ppermute | solution.py:48
  116.2 14.1 %collective-permute-start.34 = (bf16[256,768]{1,0:T(8,128)(2,1)S(1)}, bf16[256,768]{1,0:T(8,128)(2,1)S(1)}, u32[]{:S(2)}, u32[]{:S(2)}) collective-permute-start(bf16[256,768]{1,0:T(8,128)(2,1)S(1)} %get-tuple-element.100.gh0.refs_3_), channel_id=1, source_target_pairs={{0,4},{1,5},{2,6},{3,7},{4,0},{5,1},{6,2},{7,3},{8,12},{9,13},{10,... | collective-permute-start | bytes 1179656 | tf_op jit(solution)/shard_map/ppermute | solution.py:48
  125.8 4.5 %collective-permute-start.37 = (bf16[256,768]{1,0:T(8,128)(2,1)S(1)}, bf16[256,768]{1,0:T(8,128)(2,1)S(1)}, u32[]{:S(2)}, u32[]{:S(2)}) collective-permute-start(bf16[256,768]{1,0:T(8,128)(2,1)S(1)} %collective-permute-done.31.gh1.refs_4_), channel_id=1, source_target_pairs={{0,4},{1,5},{2,6},{3,7},{4,0},{5,1},{6,2},{7,3},{8,12},{9,13},{10,... | collective-permute-start | bytes 1179656 | tf_op jit(solution)/shard_map/ppermute | solution.py:48
  125.8 18.4 %collective-permute-start.38 = (bf16[192,1536]{1,0:T(8,128)(2,1)S(1)}, bf16[192,1536]{1,0:T(8,128)(2,1)S(1)}, u32[]{:S(2)}, u32[]{:S(2)}) collective-permute-start(bf16[192,1536]{1,0:T(8,128)(2,1)S(1)} %get-tuple-element.98), channel_id=1, source_target_pairs={{0,24},{1,25},{2,26},{3,27},{4,28},{5,29},{6,30},{7,31},{8,16},{9,... | collective-permute-start | bytes 1769480 | tf_op jit(solution)/shard_map/ppermute | solution.py:48
  127.6 16.6 %collective-permute-start.32 = (bf16[256,768]{1,0:T(8,128)(2,1)S(1)}, bf16[256,768]{1,0:T(8,128)(2,1)}, u32[]{:S(2)}, u32[]{:S(2)}) collective-permute-start(bf16[256,768]{1,0:T(8,128)(2,1)S(1)} %get-tuple-element.101), channel_id=1, source_target_pairs={{0,0},{1,1},{2,4},{3,5},{4,2},{5,3},{6,6},{7,7},{8,8},{9,9},{10,12... | collective-permute-start | bytes 1179656 | tf_op jit(solution)/shard_map/ppermute | solution.py:48
  129.2 15.0 %collective-permute-start.33 = (bf16[256,768]{1,0:T(8,128)(2,1)S(1)}, bf16[256,768]{1,0:T(8,128)(2,1)}, u32[]{:S(2)}, u32[]{:S(2)}) collective-permute-start(bf16[256,768]{1,0:T(8,128)(2,1)S(1)} %get-tuple-element.103), channel_id=1, source_target_pairs={{0,1},{1,0},{2,5},{3,4},{4,3},{5,2},{6,7},{7,6},{8,9},{9,8},{10,13... | collective-permute-start | bytes 1179656 | tf_op jit(solution)/shard_map/ppermute | solution.py:48
  145.0 5.0 %collective-permute-start.39 = (bf16[2,256,768]{2,1,0:T(8,128)(2,1)}, bf16[2,256,768]{2,1,0:T(8,128)(2,1)S(1)}, u32[]{:S(2)}, u32[]{:S(2)}) collective-permute-start(bf16[2,256,768]{2,1,0:T(8,128)(2,1)} %get-tuple-element.114), channel_id=1, source_target_pairs={{0,4},{1,5},{2,6},{3,7},{4,0},{5,1},{6,2},{7,3},{8,12},{9,13},{10,... | collective-permute-start | bytes 2359304 | tf_op jit(solution)/shard_map/ppermute | solution.py:48
  150.1 15.4 %collective-permute-start.40 = (bf16[256,768]{1,0:T(8,128)(2,1)S(1)}, bf16[256,768]{1,0:T(8,128)(2,1)S(1)}, u32[]{:S(2)}, u32[]{:S(2)}) collective-permute-start(bf16[256,768]{1,0:T(8,128)(2,1)S(1)} %fusion), channel_id=1, source_target_pairs={{0,1},{1,0},{2,3},{3,2},{4,5},{5,4},{6,7},{7,6},{8,9},{9,8},{10,11... | collective-permute-start | bytes 1179656 | tf_op jit(solution)/shard_map/ppermute | solution.py:48
  153.4 1.2 collective-permute-start.42
  154.7 4.1 %collective-permute-start.43 = (f32[16,768]{1,0:T(8,128)S(1)}, f32[16,768]{1,0:T(8,128)S(1)}, u32[]{:S(2)}, u32[]{:S(2)}) collective-permute-start(f32[16,768]{1,0:T(8,128)S(1)} %add.103), channel_id=1, source_target_pairs={{0,8},{1,9},{2,10},{3,11},{4,12},{5,13},{6,14},{7,15},{8,0},{9,1},... | collective-permute-start | bytes 147464 | tf_op jit(solution)/shard_map/ppermute | solution.py:48
  155.4 12.6 %collective-permute-start.52 = (bf16[96,1536]{1,0:T(8,128)(2,1)S(1)}, bf16[96,1536]{1,0:T(8,128)(2,1)S(1)}, u32[]{:S(2)}, u32[]{:S(2)}) collective-permute-start(bf16[96,1536]{1,0:T(8,128)(2,1)S(1)} %get-tuple-element.161), channel_id=1, source_target_pairs={{0,0},{1,2},{2,4},{3,6},{4,1},{5,3},{6,5},{7,7},{8,8},{9,10},{10,1... | collective-permute-start | bytes 884744 | tf_op jit(solution)/shard_map/ppermute | solution.py:48
  156.1 16.0 %collective-permute-start.53 = (bf16[96,1536]{1,0:T(8,128)(2,1)S(1)}, bf16[96,1536]{1,0:T(8,128)(2,1)S(1)}, u32[]{:S(2)}, u32[]{:S(2)}) collective-permute-start(bf16[96,1536]{1,0:T(8,128)(2,1)S(1)} %get-tuple-element.162), channel_id=1, source_target_pairs={{0,4},{1,6},{2,0},{3,2},{4,5},{5,7},{6,1},{7,3},{8,12},{9,14},{10,... | collective-permute-start | bytes 884744 | tf_op jit(solution)/shard_map/ppermute | solution.py:48
  158.8 4.4 %collective-permute-start.44 = (f32[16,768]{1,0:T(8,128)S(1)}, f32[16,768]{1,0:T(8,128)S(1)}, u32[]{:S(2)}, u32[]{:S(2)}) collective-permute-start(f32[16,768]{1,0:T(8,128)S(1)} %add.104), channel_id=1, source_target_pairs={{0,16},{1,17},{2,18},{3,19},{4,20},{5,21},{6,22},{7,23},{8,24},{9,... | collective-permute-start | bytes 147464 | tf_op jit(solution)/shard_map/ppermute | solution.py:48
  163.3 16.7 %collective-permute-start.47 = (bf16[192,768]{1,0:T(8,128)(2,1)S(1)}, bf16[192,768]{1,0:T(8,128)(2,1)S(1)}, u32[]{:S(2)}, u32[]{:S(2)}) collective-permute-start(bf16[192,768]{1,0:T(8,128)(2,1)S(1)} %get-tuple-element.130), channel_id=1, source_target_pairs={{0,8},{1,9},{2,10},{3,11},{4,12},{5,13},{6,14},{7,15},{8,0},{9,1},... | collective-permute-start | bytes 884744 | tf_op jit(solution)/shard_map/ppermute | solution.py:48
  164.2 15.7 %collective-permute-start.48 = (bf16[192,768]{1,0:T(8,128)(2,1)S(1)}, bf16[192,768]{1,0:T(8,128)(2,1)S(1)}, u32[]{:S(2)}, u32[]{:S(2)}) collective-permute-start(bf16[192,768]{1,0:T(8,128)(2,1)S(1)} %get-tuple-element.131), channel_id=1, source_target_pairs={{0,16},{1,17},{2,18},{3,19},{4,20},{5,21},{6,22},{7,23},{8,24},{9,... | collective-permute-start | bytes 884744 | tf_op jit(solution)/shard_map/ppermute | solution.py:48
  165.5 14.5 %collective-permute-start.49 = (bf16[192,768]{1,0:T(8,128)(2,1)S(1)}, bf16[192,768]{1,0:T(8,128)(2,1)S(1)}, u32[]{:S(2)}, u32[]{:S(2)}) collective-permute-start(bf16[192,768]{1,0:T(8,128)(2,1)S(1)} %get-tuple-element.132), channel_id=1, source_target_pairs={{0,24},{1,25},{2,26},{3,27},{4,28},{5,29},{6,30},{7,31},{8,16},{9,... | collective-permute-start | bytes 884744 | tf_op jit(solution)/shard_map/ppermute | solution.py:48
  168.0 11.9 %collective-permute-start.41 = (bf16[256,768]{1,0:T(8,128)(2,1)S(1)}, bf16[256,768]{1,0:T(8,128)(2,1)S(1)}, u32[]{:S(2)}, u32[]{:S(2)}) collective-permute-start(bf16[256,768]{1,0:T(8,128)(2,1)S(1)} %shard_map.254), channel_id=1, source_target_pairs={{0,0},{1,1},{2,4},{3,5},{4,2},{5,3},{6,6},{7,7},{8,8},{9,9},{10,12... | collective-permute-start | bytes 1179656 | tf_op jit(solution)/shard_map/ppermute | solution.py:48
  172.2 4.4 %collective-permute-start.45 = (f32[16,768]{1,0:T(8,128)S(1)}, f32[16,768]{1,0:T(8,128)S(1)}, u32[]{:S(2)}, u32[]{:S(2)}) collective-permute-start(f32[16,768]{1,0:T(8,128)S(1)} %add.105), channel_id=1, source_target_pairs={{0,1},{1,0},{2,3},{3,2},{4,5},{5,4},{6,7},{7,6},{8,9},{9,8},{10,11... | collective-permute-start | bytes 147464 | tf_op jit(solution)/shard_map/ppermute | solution.py:48
  176.5 10.2 %collective-permute-start.46 = (f32[16,768]{1,0:T(8,128)S(1)}, f32[16,768]{1,0:T(8,128)S(1)}, u32[]{:S(2)}, u32[]{:S(2)}) collective-permute-start(f32[16,768]{1,0:T(8,128)S(1)} %add.106), channel_id=1, source_target_pairs={{0,2},{1,3},{2,0},{3,1},{4,6},{5,7},{6,4},{7,5},{8,10},{9,11},{10,... | collective-permute-start | bytes 147464 | tf_op jit(solution)/shard_map/ppermute | solution.py:48
  180.3 8.7 %collective-permute-start.50 = (bf16[96,768]{0,1:T(8,128)(2,1)S(1)}, bf16[96,768]{0,1:T(8,128)(2,1)S(1)}, u32[]{:S(2)}, u32[]{:S(2)}) collective-permute-start(bf16[96,768]{0,1:T(8,128)(2,1)S(1)} %bitcast.67), channel_id=1, source_target_pairs={{0,0},{1,2},{2,4},{3,6},{4,1},{5,3},{6,5},{7,7},{8,8},{9,10},{10,1... | collective-permute-start | bytes 442376 | tf_op jit(solution)/shard_map/ppermute | solution.py:48
  181.2 14.1 %collective-permute-start.51 = (bf16[96,768]{0,1:T(8,128)(2,1)S(1)}, bf16[96,768]{0,1:T(8,128)(2,1)S(1)}, u32[]{:S(2)}, u32[]{:S(2)}) collective-permute-start(bf16[96,768]{0,1:T(8,128)(2,1)S(1)} %bitcast.68), channel_id=1, source_target_pairs={{0,4},{1,6},{2,0},{3,2},{4,5},{5,7},{6,1},{7,3},{8,12},{9,14},{10,... | collective-permute-start | bytes 442376 | tf_op jit(solution)/shard_map/ppermute | solution.py:48
  (24 other events, 130.0 us)

commit v3 on v2

--- a/solution.py
+++ b/solution.py
@@ -602,8 +602,8 @@
         22,
         [pltpu.VMEM((length, wide), F32), pltpu.VMEM((length, 3 * HEAD_DIM), F32)],
     )
-    gn1_core = plan.over_core(after(gn1_second, *out_sent, *mlp_got[2:]))
-    gn1_z_in = toward_z(gn1_one, gn1_core)
+    gn1_core = plan.over_core(after(gn1_second, *out_sent))
+    gn1_z_in = toward_z(after(gn1_one, *mlp_got[2:]), gn1_core)
     gn1_z = plan.over_z(gn1_z_in)
     mlp_part = plane_total(mlp_grad, mlp_got, gn1_z_in).astype(BF).reshape(2, shard, 2 * units)
     mlp_summed = plan.unspread(mlp_part)

time: 200 us -> 201 us (level)
    unnamed x71 -> x75, local copies, waits for them, and re-layouts: 7.81 us -> 8.53 us
  transfers between devices with their start and end apart: 54 -> 54, of which waited for: 21 -> 21; matrix products, arithmetic and copies ran while one was open for 4% -> 5% of each run, Pallas kernels for 18% -> 18%
where the time goes in v3:
time: 201 us; the launch traced here: 198 us
  starting transfers between devices  83.3 us (41%)
  waiting for transfers between devices  54.1 us (27%)
  Pallas kernels  39.8 us (20%)
  local copies, waits for them, and re-layouts  13.1 us (7%)
  other arithmetic  6.37 us (3%)
    ppermute x54, starting transfers between devices, send(): return lax.ppermute(value, AXES, pairs)  83.3 us
    ppermute x54, waiting for transfers between devices, send(): return lax.ppermute(value, AXES, pairs)  54.1 us
    pallas_call x10, Pallas kernels, call(): pl.pallas_call(body, out_shape=shapes, in_specs=[pl.BlockSpec(memory_spac...  39.8 us
    unnamed x75, local copies, waits for them, and re-layouts  8.53 us
  transfers between devices with their start and end apart: 54, of which 21 were waited for; matrix products, arithmetic and copies ran while one was open for 5% of the time, Pallas kernels for 18%

profile of v3, /device:TPU:0, one launch (start us, length us, event | category | flops | bytes accessed | tf_op | source)
XLA Modules:
  0.0 198.5 jit_solution(5868120539611142655)
XLA Ops:
  0.7 1.1 copy.32
  2.0 0.9 copy.33
  3.6 5.8 %collective-permute-start.6 = (bf16[96,768]{1,0:T(8,128)(2,1)S(1)}, bf16[96,768]{1,0:T(8,128)(2,1)S(1)}, u32[]{:S(2)}, u32[]{:S(2)}) collective-permute-start(bf16[96,768]{1,0:T(8,128)(2,1)S(1)} %pad_maximum_fusion.5), channel_id=1, source_target_pairs={{0,2},{1,6},{2,3},{3,7},{4,0},{5,4},{6,1},{7,5},{8,10},{9,14},{10,... | collective-permute-start | bytes 442376 | tf_op jit(solution)/shard_map/ppermute | solution.py:48
  9.4 1.6 collective-permute-start
  13.3 2.5 %collective-permute-start.9 = (bf16[2,96,768]{2,1,0:T(8,128)(2,1)S(1)}, bf16[2,96,768]{2,1,0:T(8,128)(2,1)S(1)}, u32[]{:S(2)}, u32[]{:S(2)}) collective-permute-start(bf16[2,96,768]{2,1,0:T(8,128)(2,1)S(1)} %pad_maximum_fusion.1.refs_8_), channel_id=1, source_target_pairs={{0,24},{1,25},{2,26},{3,27},{4,28},{5,29},{6,30},{7,31},{8,16},{9,... | collective-permute-start | bytes 884744 | tf_op jit(solution)/shard_map/ppermute | solution.py:48
  17.3 12.3 %collective-permute-start.1 = (bf16[256,768]{1,0:T(8,128)(2,1)S(1)}, bf16[256,768]{1,0:T(8,128)(2,1)S(1)}, u32[]{:S(2)}, u32[]{:S(2)}) collective-permute-start(bf16[256,768]{1,0:T(8,128)(2,1)S(1)} %collective-permute-done.refs_1_.refs_9_.x0.x), channel_id=1, source_target_pairs={{0,1},{1,0},{2,3},{3,2},{4,5},{5,4},{6,7},{7,6},{8,9},{9,8},{10,11... | collective-permute-start | bytes 1179656 | tf_op jit(solution)/shard_map/ppermute | solution.py:48
  30.4 6.4 %collective-permute-start.12 = (bf16[96,1536]{1,0:T(8,128)(2,1)S(1)}, bf16[96,1536]{1,0:T(8,128)(2,1)S(1)}, u32[]{:S(2)}, u32[]{:S(2)}) collective-permute-start(bf16[96,1536]{1,0:T(8,128)(2,1)S(1)} %pad_maximum_fusion.2), channel_id=1, source_target_pairs={{0,2},{1,6},{2,3},{3,7},{4,0},{5,4},{6,1},{7,5},{8,10},{9,14},{10,... | collective-permute-start | bytes 884744 | tf_op jit(solution)/shard_map/ppermute | solution.py:48
  37.2 1.7 collective-permute-done.1.refs_2_.refs_10_.x1
  38.9 3.2 %collective-permute-done.12 = bf16[96,1536]{1,0:T(8,128)(2,1)S(1)} collective-permute-done((bf16[96,1536]{1,0:T(8,128)(2,1)S(1)}, bf16[96,1536]{1,0:T(8,128)(2,1)S(1)}, u32[]{:S(2)}, u32[]{:S(2)}) %collective-permute-start.12) | collective-permute-done | bytes 294944 | tf_op jit(solution)/shard_map/ppermute | solution.py:48
  42.7 1.7 collective-permute-start.14
  44.4 1.3 collective-permute-start.15
  45.6 1.2 collective-permute-start.10
  46.8 2.6 %shard_map.245 = (bf16[1024,768]{1,0:T(8,128)(2,1)S(1)}, bf16[1024,576]{1,0:T(8,128)(2,1)S(1)}, bf16[768,768]{1,0:T(8,128)(2,1)S(1)}) custom-call(s32[4]{0:T(128)S(1)} %pad_add_fusion.refs_0_.ids, bf16[256,768]{1,0:T(8,128)(2,1)S(1)} %collective-permute-done.refs_1_.refs_9_.x0.x, bf16[256,768]{1,0:T(8,128)(2,1)S(1)} %collective-permute-done.1.refs_2_.refs_10_.x1, ...), custom_call_target="tpu_custom_call" | custom-call | flops 3449999872 | bytes 9000000 | tf_op jit(solution)/shard_map/pallas_call | solution.py:163
  49.5 1.1 copy-done.17
  50.6 1.4 collective-permute-done.13.refs_18_
  52.0 7.5 %collective-permute-start.18 = (bf16[4,2,96,192]{3,2,1,0:T(8,128)(2,1)S(1)}, bf16[4,2,96,192]{3,2,1,0:T(8,128)(2,1)S(1)}, u32[]{:S(2)}, u32[]{:S(2)}) collective-permute-start(bf16[4,2,96,192]{3,2,1,0:T(8,128)(2,1)S(1)} %pad_maximum_fusion.refs_5_), channel_id=1, source_target_pairs={{0,1},{1,0},{2,3},{3,2},{4,5},{5,4},{6,7},{7,6},{8,9},{9,8},{10,11... | collective-permute-start | bytes 884744 | tf_op jit(solution)/shard_map/ppermute | solution.py:48
  59.6 4.5 %shard_map.246 = (bf16[1024,192]{1,0:T(8,128)(2,1)S(1)}, f32[8,1024]{1,0:T(8,128)S(1)}) custom-call(s32[4]{0:T(128)S(1)} %pad_add_fusion.refs_0_.ids, bf16[1024,576]{1,0:T(8,128)(2,1)S(1)} %get-tuple-element.105.mixed), custom_call_target="tpu_custom_call" | custom-call | flops 6899999744 | bytes 18000000 | tf_op jit(solution)/shard_map/pallas_call | solution.py:163
  64.2 1.5 collective-permute-start.21
  65.7 1.3 collective-permute-start.22
  67.8 3.2 %collective-permute-done.18.refs_6_ = bf16[4,2,96,192]{3,2,1,0:T(8,128)(2,1)S(1)} collective-permute-done((bf16[4,2,96,192]{3,2,1,0:T(8,128)(2,1)S(1)}, bf16[4,2,96,192]{3,2,1,0:T(8,128)(2,1)S(1)}, u32[]{:S(2)}, u32[]{:S(2)}) %collective-permute-start.18) | collective-permute-done | bytes 294944 | tf_op jit(solution)/shard_map/ppermute | solution.py:48
  71.3 2.2 %collective-permute-done.21.refs_2_ = bf16[2,96,768]{2,1,0:T(8,128)(2,1)S(1)} collective-permute-done((bf16[2,96,768]{2,1,0:T(8,128)(2,1)S(1)}, bf16[2,96,768]{2,1,0:T(8,128)(2,1)S(1)}, u32[]{:S(2)}, u32[]{:S(2)}) %collective-permute-start.21) | collective-permute-done | bytes 294944 | tf_op jit(solution)/shard_map/ppermute | solution.py:48
  73.5 1.5 collective-permute-start.17
  75.0 5.2 %collective-permute-done.22.refs_3_ = bf16[2,96,768]{2,1,0:T(8,128)(2,1)S(1)} collective-permute-done((bf16[2,96,768]{2,1,0:T(8,128)(2,1)S(1)}, bf16[2,96,768]{2,1,0:T(8,128)(2,1)S(1)}, u32[]{:S(2)}, u32[]{:S(2)}) %collective-permute-start.22) | collective-permute-done | bytes 294944 | tf_op jit(solution)/shard_map/ppermute | solution.py:48
  80.2 1.1 collective-permute-done.23.refs_4_
  81.3 0.9 collective-permute-done.16.refs_2_
  82.8 0.8 collective-permute-start.25
  84.1 6.6 %shard_map.247 = (f32[256,768]{1,0:T(8,128)S(1)}, bf16[1024,768]{1,0:T(8,128)(2,1)S(1)}, bf16[1024,768]{1,0:T(8,128)(2,1)S(1)}, bf16[1024,768]{1,0:T(8,128)(2,1)S(1)}, bf16[768,768]{1,0:T(8,128)(2,1)S(1)}) custom-call(s32[4]{0:T(128)S(1)} %pad_add_fusion.refs_0_.ids, bf16[1024,192]{1,0:T(8,128)(2,1)S(1)} %get-tuple-element.80.refs_1_.refs_7_, ...), custom_call_target="tpu_custom_call" | custom-call | flops 8049999872 | bytes 21000000 | tf_op jit(solution)/shard_map/pallas_call | solution.py:163
  90.8 3.2 %collective-permute-done.25.refs_6_.refs_3_ = bf16[256,768]{1,0:T(8,128)(2,1)S(1)} collective-permute-done((bf16[256,768]{1,0:T(8,128)(2,1)S(1)}, bf16[256,768]{1,0:T(8,128)(2,1)S(1)}, u32[]{:S(2)}, u32[]{:S(2)}) %collective-permute-start.25) | collective-permute-done | bytes 393248 | tf_op jit(solution)/shard_map/ppermute | solution.py:48
  94.0 1.7 collective-permute-done.27.refs_8_.refs_5_
  95.7 3.6 %shard_map.248 = (bf16[1024,768]{1,0:T(8,128)(2,1)S(1)}, f32[256,768]{1,0:T(8,128)S(1)}, f32[256,768]{1,0:T(8,128)S(1)}, bf16[2,256,768]{2,1,0:T(8,128)(2,1)S(1)...) custom-call(s32[4]{0:T(128)S(1)} %pad_add_fusion.refs_0_.ids, bf16[2,96,768]{2,1,0:T(8,128)(2,1)S(1)} %pad_maximum_fusion.4.refs_1_, ...), custom_call_target="tpu_custom_call" | custom-call | flops 5750000128 | bytes 15000000 | tf_op jit(solution)/shard_map/pallas_call | solution.py:163
  99.5 2.0 shard_map.249
  102.0 0.8 collective-permute-start.30
  102.9 3.5 %shard_map.250 = (f32[192,1536]{1,0:T(8,128)S(1)}, bf16[192,1536]{1,0:T(8,128)(2,1)S(1)}, bf16[192,1536]{1,0:T(8,128)(2,1)S(1)}, bf16[192,1536]{1,0:T(8,128)(2,1)S(1)}) custom-call(s32[4]{0:T(128)S(1)} %pad_add_fusion.refs_0_.ids, bf16[1024,768]{1,0:T(8,128)(2,1)S(1)} %get-tuple-element.97.refs_1_, ...), custom_call_target="tpu_custom_call" | custom-call | flops 5750000128 | bytes 15000000 | tf_op jit(solution)/shard_map/pallas_call | solution.py:163
  107.1 1.7 collective-permute-start.36
  108.8 4.4 %collective-permute-done.30.got_z = bf16[256,768]{1,0:T(8,128)(2,1)S(1)} collective-permute-done((bf16[256,768]{1,0:T(8,128)(2,1)S(1)}, bf16[256,768]{1,0:T(8,128)(2,1)S(1)}, u32[]{:S(2)}, u32[]{:S(2)}) %collective-permute-start.30) | collective-permute-done | bytes 393248 | tf_op jit(solution)/shard_map/ppermute | solution.py:48
  113.3 1.3 shard_map.251
  114.6 0.9 copy-done.13
  116.2 5.3 %collective-permute-done.35 = bf16[192,1536]{1,0:T(8,128)(2,1)S(1)} collective-permute-done((bf16[192,1536]{1,0:T(8,128)(2,1)S(1)}, bf16[192,1536]{1,0:T(8,128)(2,1)S(1)}, u32[]{:S(2)}, u32[]{:S(2)}) %collective-permute-start.35) | collective-permute-done | bytes 589856 | tf_op jit(solution)/shard_map/ppermute | solution.py:48
  121.9 3.8 %collective-permute-done.31.gh1.refs_4_ = bf16[256,768]{1,0:T(8,128)(2,1)S(1)} collective-permute-done((bf16[256,768]{1,0:T(8,128)(2,1)S(1)}, bf16[256,768]{1,0:T(8,128)(2,1)S(1)}, u32[]{:S(2)}, u32[]{:S(2)}) %collective-permute-start.31) | collective-permute-done | bytes 393248 | tf_op jit(solution)/shard_map/ppermute | solution.py:48
  125.8 1.6 collective-permute-start.39
  127.6 0.9 collective-permute-start.32
  128.5 1.1 collective-permute-start.33
  129.6 11.9 %shard_map.252 = (bf16[1024,576]{1,0:T(8,128)(2,1)S(1)}, f32[256,768]{1,0:T(8,128)S(1)}, f32[256,768]{1,0:T(8,128)S(1)}, bf16[2,256,768]{2,1,0:T(8,128)(2,1)}, f32[16,768]{1,0:T(8,128)S(1)}) custom-call(s32[4]{0:T(128)S(1)} %pad_add_fusion.refs_0_.ids, bf16[1024,576]{1,0:T(8,128)(2,1)S(1)} %get-tuple-element.105.mixed, ...), custom_call_target="tpu_custom_call" | custom-call | flops 13799999488 | bytes 36000000 | tf_op jit(solution)/shard_map/pallas_call | solution.py:163
  141.6 0.9 copy-done.15
  142.5 1.1 copy-done.19
  145.1 3.5 %collective-permute-start.38 = (bf16[2,256,768]{2,1,0:T(8,128)(2,1)}, bf16[2,256,768]{2,1,0:T(8,128)(2,1)S(1)}, u32[]{:S(2)}, u32[]{:S(2)}) collective-permute-start(bf16[2,256,768]{2,1,0:T(8,128)(2,1)} %get-tuple-element.115), channel_id=1, source_target_pairs={{0,4},{1,5},{2,6},{3,7},{4,0},{5,1},{6,2},{7,3},{8,12},{9,13},{10,... | collective-permute-start | bytes 2359304 | tf_op jit(solution)/shard_map/ppermute | solution.py:48
  148.6 2.0 %add_convert_fusion.1 = bf16[256,768]{1,0:T(8,128)(2,1)} fusion(bf16[256,768]{1,0:T(8,128)(2,1)} %copy-done.26, bf16[256,768]{1,0:T(8,128)(2,1)} %copy-done.25), kind=kLoop, calls=%fused_computation.10 | loop fusion | flops 786432 | bytes 1179648 | tf_op jit(solution)/shard_map/convert_element_type | solution.py:636
  150.8 3.3 %collective-permute-start.40 = (bf16[256,768]{1,0:T(8,128)(2,1)S(1)}, bf16[256,768]{1,0:T(8,128)(2,1)S(1)}, u32[]{:S(2)}, u32[]{:S(2)}) collective-permute-start(bf16[256,768]{1,0:T(8,128)(2,1)S(1)} %fusion), channel_id=1, source_target_pairs={{0,1},{1,0},{2,3},{3,2},{4,5},{5,4},{6,7},{7,6},{8,9},{9,8},{10,11... | collective-permute-start | bytes 1179656 | tf_op jit(solution)/shard_map/ppermute | solution.py:48
  154.2 1.5 add_convert_fusion
  157.2 2.0 %collective-permute-start.53 = (bf16[96,1536]{1,0:T(8,128)(2,1)S(1)}, bf16[96,1536]{1,0:T(8,128)(2,1)S(1)}, u32[]{:S(2)}, u32[]{:S(2)}) collective-permute-start(bf16[96,1536]{1,0:T(8,128)(2,1)S(1)} %get-tuple-element.164), channel_id=1, source_target_pairs={{0,4},{1,6},{2,0},{3,2},{4,5},{5,7},{6,1},{7,3},{8,12},{9,14},{10,... | collective-permute-start | bytes 884744 | tf_op jit(solution)/shard_map/ppermute | solution.py:48
  160.6 2.6 %shard_map.253 = (f32[192,768]{1,0:T(8,128)S(1)}, bf16[192,768]{1,0:T(8,128)(2,1)S(1)}, bf16[192,768]{1,0:T(8,128)(2,1)S(1)}, bf16[192,768]{1,0:T(8,128)(2,1)S(1)}) custom-call(s32[4]{0:T(128)S(1)} %pad_add_fusion.refs_0_.ids, bf16[1024,768]{1,0:T(8,128)(2,1)S(1)} %copy-done.18, bf16[1024,576]{1,0:T(8,128)(2,1)S(1)} %copy-done.20, ...), custom_call_target="tpu_custom_call" | custom-call | flops 3449999872 | bytes 9000000 | tf_op jit(solution)/shard_map/pallas_call | solution.py:163
  163.2 1.0 collective-permute-done.44
  164.3 1.0 collective-permute-start.47
  165.3 1.3 collective-permute-start.48
  166.6 1.2 collective-permute-start.49
  167.8 1.2 shard_map.254
  169.7 3.6 %collective-permute-done.53 = bf16[96,1536]{1,0:T(8,128)(2,1)S(1)} collective-permute-done((bf16[96,1536]{1,0:T(8,128)(2,1)S(1)}, bf16[96,1536]{1,0:T(8,128)(2,1)S(1)}, u32[]{:S(2)}, u32[]{:S(2)}) %collective-permute-start.53) | collective-permute-done | bytes 294944 | tf_op jit(solution)/shard_map/ppermute | solution.py:48
  173.4 4.3 %collective-permute-done.45 = f32[16,768]{1,0:T(8,128)S(1)} collective-permute-done((f32[16,768]{1,0:T(8,128)S(1)}, f32[16,768]{1,0:T(8,128)S(1)}, u32[]{:S(2)}, u32[]{:S(2)}) %collective-permute-start.45) | collective-permute-done | bytes 49184 | tf_op jit(solution)/shard_map/ppermute | solution.py:48
  177.7 3.6 %collective-permute-start.46 = (f32[16,768]{1,0:T(8,128)S(1)}, f32[16,768]{1,0:T(8,128)S(1)}, u32[]{:S(2)}, u32[]{:S(2)}) collective-permute-start(f32[16,768]{1,0:T(8,128)S(1)} %add.106), channel_id=1, source_target_pairs={{0,2},{1,3},{2,0},{3,1},{4,6},{5,7},{6,4},{7,5},{8,10},{9,11},{10,... | collective-permute-start | bytes 147464 | tf_op jit(solution)/shard_map/ppermute | solution.py:48
  182.5 4.7 %collective-permute-start.51 = (bf16[96,768]{0,1:T(8,128)(2,1)S(1)}, bf16[96,768]{0,1:T(8,128)(2,1)S(1)}, u32[]{:S(2)}, u32[]{:S(2)}) collective-permute-start(bf16[96,768]{0,1:T(8,128)(2,1)S(1)} %bitcast.68), channel_id=1, source_target_pairs={{0,4},{1,6},{2,0},{3,2},{4,5},{5,7},{6,1},{7,3},{8,12},{9,14},{10,... | collective-permute-start | bytes 442376 | tf_op jit(solution)/shard_map/ppermute | solution.py:48
  187.2 0.8 slice_bitcast_fusion.4
  189.4 0.9 convert_element_type.99
  190.3 6.3 %collective-permute-done.51 = bf16[96,768]{0,1:T(8,128)(2,1)S(1)} collective-permute-done((bf16[96,768]{0,1:T(8,128)(2,1)S(1)}, bf16[96,768]{0,1:T(8,128)(2,1)S(1)}, u32[]{:S(2)}, u32[]{:S(2)}) %collective-permute-start.51) | collective-permute-done | bytes 147488 | tf_op jit(solution)/shard_map/ppermute | solution.py:48
  197.3 0.9 copy.37
  (178 shorter events, 20.0 us)
Async XLA Ops:
  0.6 15.2 %copy-start.27 = (bf16[768,96]{0,1:T(8,128)(2,1)S(1)}, bf16[768,96]{0,1:T(8,128)(2,1)}, u32[]{:S(2)}) copy-start(bf16[768,96]{0,1:T(8,128)(2,1)} %param.25) | copy-start | bytes 442372
  0.7 15.2 %copy-start.28 = (bf16[96,768]{1,0:T(8,128)(2,1)S(1)}, bf16[96,768]{1,0:T(8,128)(2,1)}, u32[]{:S(2)}) copy-start(bf16[96,768]{1,0:T(8,128)(2,1)} %param.23) | copy-start | bytes 442372
  0.7 15.3 %copy-start.30 = (f32[768]{0:T(1024)S(1)}, f32[768]{0:T(1024)}, u32[]{:S(2)}) copy-start(f32[768]{0:T(1024)} %param.15) | copy-start | bytes 9220
  0.7 15.3 %copy-start.31 = (f32[768]{0:T(1024)S(1)}, f32[768]{0:T(1024)}, u32[]{:S(2)}) copy-start(f32[768]{0:T(1024)} %param.16) | copy-start | bytes 9220
  3.0 10.3 %collective-permute-start.5 = (bf16[96,768]{1,0:T(8,128)(2,1)S(1)}, bf16[96,768]{1,0:T(8,128)(2,1)S(1)}, u32[]{:S(2)}, u32[]{:S(2)}) collective-permute-start(bf16[96,768]{1,0:T(8,128)(2,1)S(1)} %pad_maximum_fusion.5), channel_id=1, source_target_pairs={{0,0},{1,4},{2,1},{3,5},{4,2},{5,6},{6,3},{7,7},{8,8},{9,12},{10,9... | collective-permute-start | bytes 442376 | tf_op jit(solution)/shard_map/ppermute | solution.py:48
  3.6 9.6 %collective-permute-start.6 = (bf16[96,768]{1,0:T(8,128)(2,1)S(1)}, bf16[96,768]{1,0:T(8,128)(2,1)S(1)}, u32[]{:S(2)}, u32[]{:S(2)}) collective-permute-start(bf16[96,768]{1,0:T(8,128)(2,1)S(1)} %pad_maximum_fusion.5), channel_id=1, source_target_pairs={{0,2},{1,6},{2,3},{3,7},{4,0},{5,4},{6,1},{7,5},{8,10},{9,14},{10,... | collective-permute-start | bytes 442376 | tf_op jit(solution)/shard_map/ppermute | solution.py:48
  9.4 7.8 %collective-permute-start = (bf16[256,768]{1,0:T(8,128)(2,1)}, bf16[256,768]{1,0:T(8,128)(2,1)S(1)}, u32[]{:S(2)}, u32[]{:S(2)}) collective-permute-start(bf16[256,768]{1,0:T(8,128)(2,1)} %param.14), channel_id=1, source_target_pairs={{0,0},{1,1},{2,4},{3,5},{4,2},{5,3},{6,6},{7,7},{8,8},{9,9},{10,12... | collective-permute-start | bytes 1179656 | tf_op jit(solution)/shard_map/ppermute | solution.py:48
  12.6 3.4 %collective-permute-start.4 = (f32[1344]{0:T(1024)S(1)}, f32[1344]{0:T(1024)S(1)}, u32[]{:S(2)}, u32[]{:S(2)}) collective-permute-start(f32[1344]{0:T(1024)S(1)} %pad_maximum_fusion.6), channel_id=1, source_target_pairs={{0,0},{1,4},{2,1},{3,5},{4,2},{5,6},{6,3},{7,7},{8,8},{9,12},{10,9... | collective-permute-start | bytes 16136 | tf_op jit(solution)/shard_map/ppermute | solution.py:48
  13.3 16.3 %collective-permute-start.9 = (bf16[2,96,768]{2,1,0:T(8,128)(2,1)S(1)}, bf16[2,96,768]{2,1,0:T(8,128)(2,1)S(1)}, u32[]{:S(2)}, u32[]{:S(2)}) collective-permute-start(bf16[2,96,768]{2,1,0:T(8,128)(2,1)S(1)} %pad_maximum_fusion.1.refs_8_), channel_id=1, source_target_pairs={{0,24},{1,25},{2,26},{3,27},{4,28},{5,29},{6,30},{7,31},{8,16},{9,... | collective-permute-start | bytes 884744 | tf_op jit(solution)/shard_map/ppermute | solution.py:48
  16.0 20.8 %collective-permute-start.7 = (bf16[2,96,768]{2,1,0:T(8,128)(2,1)S(1)}, bf16[2,96,768]{2,1,0:T(8,128)(2,1)S(1)}, u32[]{:S(2)}, u32[]{:S(2)}) collective-permute-start(bf16[2,96,768]{2,1,0:T(8,128)(2,1)S(1)} %pad_maximum_fusion.1.refs_8_), channel_id=1, source_target_pairs={{0,8},{1,9},{2,10},{3,11},{4,12},{5,13},{6,14},{7,15},{8,0},{9,1},... | collective-permute-start | bytes 884744 | tf_op jit(solution)/shard_map/ppermute | solution.py:48
  16.6 13.7 %collective-permute-start.8 = (bf16[2,96,768]{2,1,0:T(8,128)(2,1)S(1)}, bf16[2,96,768]{2,1,0:T(8,128)(2,1)S(1)}, u32[]{:S(2)}, u32[]{:S(2)}) collective-permute-start(bf16[2,96,768]{2,1,0:T(8,128)(2,1)S(1)} %pad_maximum_fusion.1.refs_8_), channel_id=1, source_target_pairs={{0,16},{1,17},{2,18},{3,19},{4,20},{5,21},{6,22},{7,23},{8,24},{9,... | collective-permute-start | bytes 884744 | tf_op jit(solution)/shard_map/ppermute | solution.py:48
  17.2 66.9 %copy-start.2 = (bf16[256,768]{1,0:T(8,128)(2,1)}, bf16[256,768]{1,0:T(8,128)(2,1)S(1)}, u32[]{:S(2)}) copy-start(bf16[256,768]{1,0:T(8,128)(2,1)S(1)} %collective-permute-done.refs_1_.refs_9_.x0.x) | copy-start | bytes 1179652
  17.3 21.6 %collective-permute-start.1 = (bf16[256,768]{1,0:T(8,128)(2,1)S(1)}, bf16[256,768]{1,0:T(8,128)(2,1)S(1)}, u32[]{:S(2)}, u32[]{:S(2)}) collective-permute-start(bf16[256,768]{1,0:T(8,128)(2,1)S(1)} %collective-permute-done.refs_1_.refs_9_.x0.x), channel_id=1, source_target_pairs={{0,1},{1,0},{2,3},{3,2},{4,5},{5,4},{6,7},{7,6},{8,9},{9,8},{10,11... | collective-permute-start | bytes 1179656 | tf_op jit(solution)/shard_map/ppermute | solution.py:48
  29.6 14.8 %collective-permute-start.2 = (bf16[256,768]{1,0:T(8,128)(2,1)S(1)}, bf16[256,768]{1,0:T(8,128)(2,1)S(1)}, u32[]{:S(2)}, u32[]{:S(2)}) collective-permute-start(bf16[256,768]{1,0:T(8,128)(2,1)S(1)} %collective-permute-done.refs_1_.refs_9_.x0.x), channel_id=1, source_target_pairs={{0,4},{1,5},{2,6},{3,7},{4,0},{5,1},{6,2},{7,3},{8,12},{9,13},{10,... | collective-permute-start | bytes 1179656 | tf_op jit(solution)/shard_map/ppermute | solution.py:48
  29.6 9.2 %collective-permute-start.11 = (bf16[96,1536]{1,0:T(8,128)(2,1)S(1)}, bf16[96,1536]{1,0:T(8,128)(2,1)S(1)}, u32[]{:S(2)}, u32[]{:S(2)}) collective-permute-start(bf16[96,1536]{1,0:T(8,128)(2,1)S(1)} %pad_maximum_fusion.2), channel_id=1, source_target_pairs={{0,0},{1,4},{2,1},{3,5},{4,2},{5,6},{6,3},{7,7},{8,8},{9,12},{10,9... | collective-permute-start | bytes 884744 | tf_op jit(solution)/shard_map/ppermute | solution.py:48
  30.4 11.6 %collective-permute-start.12 = (bf16[96,1536]{1,0:T(8,128)(2,1)S(1)}, bf16[96,1536]{1,0:T(8,128)(2,1)S(1)}, u32[]{:S(2)}, u32[]{:S(2)}) collective-permute-start(bf16[96,1536]{1,0:T(8,128)(2,1)S(1)} %pad_maximum_fusion.2), channel_id=1, source_target_pairs={{0,2},{1,6},{2,3},{3,7},{4,0},{5,4},{6,1},{7,5},{8,10},{9,14},{10,... | collective-permute-start | bytes 884744 | tf_op jit(solution)/shard_map/ppermute | solution.py:48
  37.1 29.9 %collective-permute-start.19 = (bf16[4,2,96,192]{3,2,1,0:T(8,128)(2,1)S(1)}, bf16[4,2,96,192]{3,2,1,0:T(8,128)(2,1)S(1)}, u32[]{:S(2)}, u32[]{:S(2)}) collective-permute-start(bf16[4,2,96,192]{3,2,1,0:T(8,128)(2,1)S(1)} %pad_maximum_fusion.refs_5_), channel_id=1, source_target_pairs={{0,4},{1,5},{2,6},{3,7},{4,0},{5,1},{6,2},{7,3},{8,12},{9,13},{10,... | collective-permute-start | bytes 884744 | tf_op jit(solution)/shard_map/ppermute | solution.py:48
  38.8 6.8 %collective-permute-start.3 = (bf16[256,768]{1,0:T(8,128)(2,1)S(1)}, bf16[256,768]{1,0:T(8,128)(2,1)S(1)}, u32[]{:S(2)}, u32[]{:S(2)}) collective-permute-start(bf16[256,768]{1,0:T(8,128)(2,1)S(1)} %collective-permute-done.1.refs_2_.refs_10_.x1), channel_id=1, source_target_pairs={{0,4},{1,5},{2,6},{3,7},{4,0},{5,1},{6,2},{7,3},{8,12},{9,13},{10,... | collective-permute-start | bytes 1179656 | tf_op jit(solution)/shard_map/ppermute | solution.py:48
  42.1 9.9 %collective-permute-start.13 = (bf16[2,96,768]{2,1,0:T(8,128)(2,1)S(1)}, bf16[2,96,768]{2,1,0:T(8,128)(2,1)S(1)}, u32[]{:S(2)}, u32[]{:S(2)}) collective-permute-start(bf16[2,96,768]{2,1,0:T(8,128)(2,1)S(1)} %pad_maximum_fusion.3.refs_17_), channel_id=1, source_target_pairs={{0,8},{1,9},{2,10},{3,11},{4,12},{5,13},{6,14},{7,15},{8,0},{9,1},... | collective-permute-start | bytes 884744 | tf_op jit(solution)/shard_map/ppermute | solution.py:48
  42.7 21.4 %collective-permute-start.14 = (bf16[2,96,768]{2,1,0:T(8,128)(2,1)S(1)}, bf16[2,96,768]{2,1,0:T(8,128)(2,1)S(1)}, u32[]{:S(2)}, u32[]{:S(2)}) collective-permute-start(bf16[2,96,768]{2,1,0:T(8,128)(2,1)S(1)} %pad_maximum_fusion.3.refs_17_), channel_id=1, source_target_pairs={{0,16},{1,17},{2,18},{3,19},{4,20},{5,21},{6,22},{7,23},{8,24},{9,... | collective-permute-start | bytes 884744 | tf_op jit(solution)/shard_map/ppermute | solution.py:48
  44.4 19.8 %collective-permute-start.15 = (bf16[2,96,768]{2,1,0:T(8,128)(2,1)S(1)}, bf16[2,96,768]{2,1,0:T(8,128)(2,1)S(1)}, u32[]{:S(2)}, u32[]{:S(2)}) collective-permute-start(bf16[2,96,768]{2,1,0:T(8,128)(2,1)S(1)} %pad_maximum_fusion.3.refs_17_), channel_id=1, source_target_pairs={{0,24},{1,25},{2,26},{3,27},{4,28},{5,29},{6,30},{7,31},{8,16},{9,... | collective-permute-start | bytes 884744 | tf_op jit(solution)/shard_map/ppermute | solution.py:48
  45.6 18.5 %collective-permute-start.10 = (bf16[256,768]{1,0:T(8,128)(2,1)S(1)}, bf16[256,768]{1,0:T(8,128)(2,1)S(1)}, u32[]{:S(2)}, u32[]{:S(2)}) collective-permute-start(bf16[256,768]{1,0:T(8,128)(2,1)S(1)} %copy-done.35), channel_id=1, source_target_pairs={{0,0},{1,1},{2,4},{3,5},{4,2},{5,3},{6,6},{7,7},{8,8},{9,9},{10,12... | collective-permute-start | bytes 1179656 | tf_op jit(solution)/shard_map/ppermute | solution.py:48
  50.6 31.7 %copy-start.32 = (f32[768]{0:T(1024)S(1)}, f32[768]{0:T(1024)}, u32[]{:S(2)}) copy-start(f32[768]{0:T(1024)} %param.21) | copy-start | bytes 9220
  50.6 31.7 %copy-start.33 = (f32[768]{0:T(1024)S(1)}, f32[768]{0:T(1024)}, u32[]{:S(2)}) copy-start(f32[768]{0:T(1024)} %param.20) | copy-start | bytes 9220
  50.6 31.7 %copy-start.34 = (f32[768]{0:T(1024)S(1)}, f32[768]{0:T(1024)}, u32[]{:S(2)}) copy-start(f32[768]{0:T(1024)} %param.22) | copy-start | bytes 9220
  52.0 18.9 %collective-permute-start.18 = (bf16[4,2,96,192]{3,2,1,0:T(8,128)(2,1)S(1)}, bf16[4,2,96,192]{3,2,1,0:T(8,128)(2,1)S(1)}, u32[]{:S(2)}, u32[]{:S(2)}) collective-permute-start(bf16[4,2,96,192]{3,2,1,0:T(8,128)(2,1)S(1)} %pad_maximum_fusion.refs_5_), channel_id=1, source_target_pairs={{0,1},{1,0},{2,3},{3,2},{4,5},{5,4},{6,7},{7,6},{8,9},{9,8},{10,11... | collective-permute-start | bytes 884744 | tf_op jit(solution)/shard_map/ppermute | solution.py:48
  64.1 26.7 %copy-start = (bf16[1024,192]{1,0:T(8,128)(2,1)}, bf16[1024,192]{1,0:T(8,128)(2,1)S(1)}, u32[]{:S(2)}) copy-start(bf16[1024,192]{1,0:T(8,128)(2,1)S(1)} %get-tuple-element.80.refs_1_.refs_7_) | copy-start | bytes 1179652
  64.1 18.1 %collective-permute-start.16 = (bf16[1024,192]{1,0:T(8,128)(2,1)S(1)}, bf16[1024,192]{1,0:T(8,128)(2,1)S(1)}, u32[]{:S(2)}, u32[]{:S(2)}) collective-permute-start(bf16[1024,192]{1,0:T(8,128)(2,1)S(1)} %get-tuple-element.80.refs_1_.refs_7_), channel_id=1, source_target_pairs={{0,1},{1,0},{2,3},{3,2},{4,5},{5,4},{6,7},{7,6},{8,9},{9,8},{10,11... | collective-permute-start | bytes 1179656 | tf_op jit(solution)/shard_map/ppermute | solution.py:48
  64.2 9.2 %collective-permute-start.21 = (bf16[2,96,768]{2,1,0:T(8,128)(2,1)S(1)}, bf16[2,96,768]{2,1,0:T(8,128)(2,1)S(1)}, u32[]{:S(2)}, u32[]{:S(2)}) collective-permute-start(bf16[2,96,768]{2,1,0:T(8,128)(2,1)S(1)} %pad_maximum_fusion.4.refs_1_), channel_id=1, source_target_pairs={{0,8},{1,9},{2,10},{3,11},{4,12},{5,13},{6,14},{7,15},{8,0},{9,1},... | collective-permute-start | bytes 884744 | tf_op jit(solution)/shard_map/ppermute | solution.py:48
  65.7 14.5 %collective-permute-start.22 = (bf16[2,96,768]{2,1,0:T(8,128)(2,1)S(1)}, bf16[2,96,768]{2,1,0:T(8,128)(2,1)S(1)}, u32[]{:S(2)}, u32[]{:S(2)}) collective-permute-start(bf16[2,96,768]{2,1,0:T(8,128)(2,1)S(1)} %pad_maximum_fusion.4.refs_1_), channel_id=1, source_target_pairs={{0,16},{1,17},{2,18},{3,19},{4,20},{5,21},{6,22},{7,23},{8,24},{9,... | collective-permute-start | bytes 884744 | tf_op jit(solution)/shard_map/ppermute | solution.py:48
  67.0 14.3 %collective-permute-start.23 = (bf16[2,96,768]{2,1,0:T(8,128)(2,1)S(1)}, bf16[2,96,768]{2,1,0:T(8,128)(2,1)S(1)}, u32[]{:S(2)}, u32[]{:S(2)}) collective-permute-start(bf16[2,96,768]{2,1,0:T(8,128)(2,1)S(1)} %pad_maximum_fusion.4.refs_1_), channel_id=1, source_target_pairs={{0,24},{1,25},{2,26},{3,27},{4,28},{5,29},{6,30},{7,31},{8,16},{9,... | collective-permute-start | bytes 884744 | tf_op jit(solution)/shard_map/ppermute | solution.py:48
  71.0 11.2 %collective-permute-start.20 = (bf16[4,2,96,192]{3,2,1,0:T(8,128)(2,1)S(1)}, bf16[4,2,96,192]{3,2,1,0:T(8,128)(2,1)S(1)}, u32[]{:S(2)}, u32[]{:S(2)}) collective-permute-start(bf16[4,2,96,192]{3,2,1,0:T(8,128)(2,1)S(1)} %collective-permute-done.18.refs_6_), channel_id=1, source_target_pairs={{0,4},{1,5},{2,6},{3,7},{4,0},{5,1},{6,2},{7,3},{8,12},{9,13},{10,... | collective-permute-start | bytes 884744 | tf_op jit(solution)/shard_map/ppermute | solution.py:48
  73.5 10.2 %collective-permute-start.17 = (bf16[1024,192]{1,0:T(8,128)(2,1)S(1)}, bf16[1024,192]{1,0:T(8,128)(2,1)S(1)}, u32[]{:S(2)}, u32[]{:S(2)}) collective-permute-start(bf16[1024,192]{1,0:T(8,128)(2,1)S(1)} %get-tuple-element.80.refs_1_.refs_7_), channel_id=1, source_target_pairs={{0,4},{1,5},{2,6},{3,7},{4,0},{5,1},{6,2},{7,3},{8,12},{9,13},{10,... | collective-permute-start | bytes 1179656 | tf_op jit(solution)/shard_map/ppermute | solution.py:48
  82.2 1.9 collective-permute-start.24
  82.4 11.5 %collective-permute-start.26 = (bf16[256,768]{1,0:T(8,128)(2,1)S(1)}, bf16[256,768]{1,0:T(8,128)(2,1)S(1)}, u32[]{:S(2)}, u32[]{:S(2)}) collective-permute-start(bf16[256,768]{1,0:T(8,128)(2,1)S(1)} %collective-permute-done.10.refs_5_.refs_2_.g), channel_id=1, source_target_pairs={{0,4},{1,5},{2,6},{3,7},{4,0},{5,1},{6,2},{7,3},{8,12},{9,13},{10,... | collective-permute-start | bytes 1179656 | tf_op jit(solution)/shard_map/ppermute | solution.py:48
  82.8 11.1 %collective-permute-start.25 = (bf16[256,768]{1,0:T(8,128)(2,1)S(1)}, bf16[256,768]{1,0:T(8,128)(2,1)S(1)}, u32[]{:S(2)}, u32[]{:S(2)}) collective-permute-start(bf16[256,768]{1,0:T(8,128)(2,1)S(1)} %collective-permute-done.10.refs_5_.refs_2_.g), channel_id=1, source_target_pairs={{0,1},{1,0},{2,3},{3,2},{4,5},{5,4},{6,7},{7,6},{8,9},{9,8},{10,11... | collective-permute-start | bytes 1179656 | tf_op jit(solution)/shard_map/ppermute | solution.py:48
  94.0 1.7 collective-permute-start.27
  99.3 2.6 %collective-permute-start.29 = (bf16[2,256,768]{2,1,0:T(8,128)(2,1)S(1)}, bf16[2,256,768]{2,1,0:T(8,128)(2,1)S(1)}, u32[]{:S(2)}, u32[]{:S(2)}) collective-permute-start(bf16[2,256,768]{2,1,0:T(8,128)(2,1)S(1)} %get-tuple-element.94), channel_id=1, source_target_pairs={{0,4},{1,5},{2,6},{3,7},{4,0},{5,1},{6,2},{7,3},{8,12},{9,13},{10,... | collective-permute-start | bytes 2359304 | tf_op jit(solution)/shard_map/ppermute | solution.py:48
  101.5 25.8 %collective-permute-start.28 = (bf16[2,256,768]{2,1,0:T(8,128)(2,1)S(1)}, bf16[2,256,768]{2,1,0:T(8,128)(2,1)S(1)}, u32[]{:S(2)}, u32[]{:S(2)}) collective-permute-start(bf16[2,256,768]{2,1,0:T(8,128)(2,1)S(1)} %get-tuple-element.92), channel_id=1, source_target_pairs={{0,4},{1,5},{2,6},{3,7},{4,0},{5,1},{6,2},{7,3},{8,12},{9,13},{10,... | collective-permute-start | bytes 2359304 | tf_op jit(solution)/shard_map/ppermute | solution.py:48
  102.0 11.2 %collective-permute-start.30 = (bf16[256,768]{1,0:T(8,128)(2,1)S(1)}, bf16[256,768]{1,0:T(8,128)(2,1)S(1)}, u32[]{:S(2)}, u32[]{:S(2)}) collective-permute-start(bf16[256,768]{1,0:T(8,128)(2,1)S(1)} %fusion.2), channel_id=1, source_target_pairs={{0,1},{1,0},{2,3},{3,2},{4,5},{5,4},{6,7},{7,6},{8,9},{9,8},{10,11... | collective-permute-start | bytes 1179656 | tf_op jit(solution)/shard_map/ppermute | solution.py:48
  106.4 15.2 %collective-permute-start.35 = (bf16[192,1536]{1,0:T(8,128)(2,1)S(1)}, bf16[192,1536]{1,0:T(8,128)(2,1)S(1)}, u32[]{:S(2)}, u32[]{:S(2)}) collective-permute-start(bf16[192,1536]{1,0:T(8,128)(2,1)S(1)} %get-tuple-element.108), channel_id=1, source_target_pairs={{0,8},{1,9},{2,10},{3,11},{4,12},{5,13},{6,14},{7,15},{8,0},{9,1},... | collective-permute-start | bytes 1769480 | tf_op jit(solution)/shard_map/ppermute | solution.py:48
  107.1 14.8 %collective-permute-start.36 = (bf16[192,1536]{1,0:T(8,128)(2,1)S(1)}, bf16[192,1536]{1,0:T(8,128)(2,1)S(1)}, u32[]{:S(2)}, u32[]{:S(2)}) collective-permute-start(bf16[192,1536]{1,0:T(8,128)(2,1)S(1)} %get-tuple-element.109), channel_id=1, source_target_pairs={{0,16},{1,17},{2,18},{3,19},{4,20},{5,21},{6,22},{7,23},{8,24},{9,... | collective-permute-start | bytes 1769480 | tf_op jit(solution)/shard_map/ppermute | solution.py:48
  115.4 14.2 %copy-start.5 = (bf16[256,768]{1,0:T(8,128)(2,1)}, bf16[256,768]{1,0:T(8,128)(2,1)S(1)}, u32[]{:S(2)}) copy-start(bf16[256,768]{1,0:T(8,128)(2,1)S(1)} %get-tuple-element.101.gh0.refs_3_) | copy-start | bytes 1179652
  115.4 10.3 %collective-permute-start.31 = (bf16[256,768]{1,0:T(8,128)(2,1)S(1)}, bf16[256,768]{1,0:T(8,128)(2,1)S(1)}, u32[]{:S(2)}, u32[]{:S(2)}) collective-permute-start(bf16[256,768]{1,0:T(8,128)(2,1)S(1)} %get-tuple-element.101.gh0.refs_3_), channel_id=1, source_target_pairs={{0,1},{1,0},{2,3},{3,2},{4,5},{5,4},{6,7},{7,6},{8,9},{9,8},{10,11... | collective-permute-start | bytes 1179656 | tf_op jit(solution)/shard_map/ppermute | solution.py:48
  116.2 13.4 %collective-permute-start.34 = (bf16[256,768]{1,0:T(8,128)(2,1)S(1)}, bf16[256,768]{1,0:T(8,128)(2,1)S(1)}, u32[]{:S(2)}, u32[]{:S(2)}) collective-permute-start(bf16[256,768]{1,0:T(8,128)(2,1)S(1)} %get-tuple-element.101.gh0.refs_3_), channel_id=1, source_target_pairs={{0,4},{1,5},{2,6},{3,7},{4,0},{5,1},{6,2},{7,3},{8,12},{9,13},{10,... | collective-permute-start | bytes 1179656 | tf_op jit(solution)/shard_map/ppermute | solution.py:48
  125.8 3.8 %collective-permute-start.37 = (bf16[256,768]{1,0:T(8,128)(2,1)S(1)}, bf16[256,768]{1,0:T(8,128)(2,1)S(1)}, u32[]{:S(2)}, u32[]{:S(2)}) collective-permute-start(bf16[256,768]{1,0:T(8,128)(2,1)S(1)} %collective-permute-done.31.gh1.refs_4_), channel_id=1, source_target_pairs={{0,4},{1,5},{2,6},{3,7},{4,0},{5,1},{6,2},{7,3},{8,12},{9,13},{10,... | collective-permute-start | bytes 1179656 | tf_op jit(solution)/shard_map/ppermute | solution.py:48
  125.8 22.8 %collective-permute-start.39 = (bf16[192,1536]{1,0:T(8,128)(2,1)S(1)}, bf16[192,1536]{1,0:T(8,128)(2,1)}, u32[]{:S(2)}, u32[]{:S(2)}) collective-permute-start(bf16[192,1536]{1,0:T(8,128)(2,1)S(1)} %get-tuple-element.99), channel_id=1, source_target_pairs={{0,24},{1,25},{2,26},{3,27},{4,28},{5,29},{6,30},{7,31},{8,16},{9,... | collective-permute-start | bytes 1769480 | tf_op jit(solution)/shard_map/ppermute | solution.py:48
  127.6 16.0 %collective-permute-start.32 = (bf16[256,768]{1,0:T(8,128)(2,1)S(1)}, bf16[256,768]{1,0:T(8,128)(2,1)S(1)}, u32[]{:S(2)}, u32[]{:S(2)}) collective-permute-start(bf16[256,768]{1,0:T(8,128)(2,1)S(1)} %get-tuple-element.102), channel_id=1, source_target_pairs={{0,0},{1,1},{2,4},{3,5},{4,2},{5,3},{6,6},{7,7},{8,8},{9,9},{10,12... | collective-permute-start | bytes 1179656 | tf_op jit(solution)/shard_map/ppermute | solution.py:48
  128.5 15.1 %collective-permute-start.33 = (bf16[256,768]{1,0:T(8,128)(2,1)S(1)}, bf16[256,768]{1,0:T(8,128)(2,1)S(1)}, u32[]{:S(2)}, u32[]{:S(2)}) collective-permute-start(bf16[256,768]{1,0:T(8,128)(2,1)S(1)} %get-tuple-element.104), channel_id=1, source_target_pairs={{0,1},{1,0},{2,5},{3,4},{4,3},{5,2},{6,7},{7,6},{8,9},{9,8},{10,13... | collective-permute-start | bytes 1179656 | tf_op jit(solution)/shard_map/ppermute | solution.py:48
  145.1 5.7 %collective-permute-start.38 = (bf16[2,256,768]{2,1,0:T(8,128)(2,1)}, bf16[2,256,768]{2,1,0:T(8,128)(2,1)S(1)}, u32[]{:S(2)}, u32[]{:S(2)}) collective-permute-start(bf16[2,256,768]{2,1,0:T(8,128)(2,1)} %get-tuple-element.115), channel_id=1, source_target_pairs={{0,4},{1,5},{2,6},{3,7},{4,0},{5,1},{6,2},{7,3},{8,12},{9,13},{10,... | collective-permute-start | bytes 2359304 | tf_op jit(solution)/shard_map/ppermute | solution.py:48
  150.8 15.8 %collective-permute-start.40 = (bf16[256,768]{1,0:T(8,128)(2,1)S(1)}, bf16[256,768]{1,0:T(8,128)(2,1)S(1)}, u32[]{:S(2)}, u32[]{:S(2)}) collective-permute-start(bf16[256,768]{1,0:T(8,128)(2,1)S(1)} %fusion), channel_id=1, source_target_pairs={{0,1},{1,0},{2,3},{3,2},{4,5},{5,4},{6,7},{7,6},{8,9},{9,8},{10,11... | collective-permute-start | bytes 1179656 | tf_op jit(solution)/shard_map/ppermute | solution.py:48
  154.1 1.7 collective-permute-start.42
  155.8 4.2 %collective-permute-start.43 = (f32[16,768]{1,0:T(8,128)S(1)}, f32[16,768]{1,0:T(8,128)S(1)}, u32[]{:S(2)}, u32[]{:S(2)}) collective-permute-start(f32[16,768]{1,0:T(8,128)S(1)} %add.103), channel_id=1, source_target_pairs={{0,8},{1,9},{2,10},{3,11},{4,12},{5,13},{6,14},{7,15},{8,0},{9,1},... | collective-permute-start | bytes 147464 | tf_op jit(solution)/shard_map/ppermute | solution.py:48
  156.5 12.5 %collective-permute-start.52 = (bf16[96,1536]{1,0:T(8,128)(2,1)S(1)}, bf16[96,1536]{1,0:T(8,128)(2,1)S(1)}, u32[]{:S(2)}, u32[]{:S(2)}) collective-permute-start(bf16[96,1536]{1,0:T(8,128)(2,1)S(1)} %get-tuple-element.163), channel_id=1, source_target_pairs={{0,0},{1,2},{2,4},{3,6},{4,1},{5,3},{6,5},{7,7},{8,8},{9,10},{10,1... | collective-permute-start | bytes 884744 | tf_op jit(solution)/shard_map/ppermute | solution.py:48
  157.2 16.1 %collective-permute-start.53 = (bf16[96,1536]{1,0:T(8,128)(2,1)S(1)}, bf16[96,1536]{1,0:T(8,128)(2,1)S(1)}, u32[]{:S(2)}, u32[]{:S(2)}) collective-permute-start(bf16[96,1536]{1,0:T(8,128)(2,1)S(1)} %get-tuple-element.164), channel_id=1, source_target_pairs={{0,4},{1,6},{2,0},{3,2},{4,5},{5,7},{6,1},{7,3},{8,12},{9,14},{10,... | collective-permute-start | bytes 884744 | tf_op jit(solution)/shard_map/ppermute | solution.py:48
  159.9 4.3 %collective-permute-start.44 = (f32[16,768]{1,0:T(8,128)S(1)}, f32[16,768]{1,0:T(8,128)S(1)}, u32[]{:S(2)}, u32[]{:S(2)}) collective-permute-start(f32[16,768]{1,0:T(8,128)S(1)} %add.104), channel_id=1, source_target_pairs={{0,16},{1,17},{2,18},{3,19},{4,20},{5,21},{6,22},{7,23},{8,24},{9,... | collective-permute-start | bytes 147464 | tf_op jit(solution)/shard_map/ppermute | solution.py:48
  164.3 17.0 %collective-permute-start.47 = (bf16[192,768]{1,0:T(8,128)(2,1)S(1)}, bf16[192,768]{1,0:T(8,128)(2,1)S(1)}, u32[]{:S(2)}, u32[]{:S(2)}) collective-permute-start(bf16[192,768]{1,0:T(8,128)(2,1)S(1)} %get-tuple-element.132), channel_id=1, source_target_pairs={{0,8},{1,9},{2,10},{3,11},{4,12},{5,13},{6,14},{7,15},{8,0},{9,1},... | collective-permute-start | bytes 884744 | tf_op jit(solution)/shard_map/ppermute | solution.py:48
  165.3 16.0 %collective-permute-start.48 = (bf16[192,768]{1,0:T(8,128)(2,1)S(1)}, bf16[192,768]{1,0:T(8,128)(2,1)S(1)}, u32[]{:S(2)}, u32[]{:S(2)}) collective-permute-start(bf16[192,768]{1,0:T(8,128)(2,1)S(1)} %get-tuple-element.133), channel_id=1, source_target_pairs={{0,16},{1,17},{2,18},{3,19},{4,20},{5,21},{6,22},{7,23},{8,24},{9,... | collective-permute-start | bytes 884744 | tf_op jit(solution)/shard_map/ppermute | solution.py:48
  166.6 14.7 %collective-permute-start.49 = (bf16[192,768]{1,0:T(8,128)(2,1)S(1)}, bf16[192,768]{1,0:T(8,128)(2,1)S(1)}, u32[]{:S(2)}, u32[]{:S(2)}) collective-permute-start(bf16[192,768]{1,0:T(8,128)(2,1)S(1)} %get-tuple-element.134), channel_id=1, source_target_pairs={{0,24},{1,25},{2,26},{3,27},{4,28},{5,29},{6,30},{7,31},{8,16},{9,... | collective-permute-start | bytes 884744 | tf_op jit(solution)/shard_map/ppermute | solution.py:48
  169.0 12.2 %collective-permute-start.41 = (bf16[256,768]{1,0:T(8,128)(2,1)S(1)}, bf16[256,768]{1,0:T(8,128)(2,1)S(1)}, u32[]{:S(2)}, u32[]{:S(2)}) collective-permute-start(bf16[256,768]{1,0:T(8,128)(2,1)S(1)} %shard_map.254), channel_id=1, source_target_pairs={{0,0},{1,1},{2,4},{3,5},{4,2},{5,3},{6,6},{7,7},{8,8},{9,9},{10,12... | collective-permute-start | bytes 1179656 | tf_op jit(solution)/shard_map/ppermute | solution.py:48
  173.3 4.3 %collective-permute-start.45 = (f32[16,768]{1,0:T(8,128)S(1)}, f32[16,768]{1,0:T(8,128)S(1)}, u32[]{:S(2)}, u32[]{:S(2)}) collective-permute-start(f32[16,768]{1,0:T(8,128)S(1)} %add.105), channel_id=1, source_target_pairs={{0,1},{1,0},{2,3},{3,2},{4,5},{5,4},{6,7},{7,6},{8,9},{9,8},{10,11... | collective-permute-start | bytes 147464 | tf_op jit(solution)/shard_map/ppermute | solution.py:48
  177.7 10.4 %collective-permute-start.46 = (f32[16,768]{1,0:T(8,128)S(1)}, f32[16,768]{1,0:T(8,128)S(1)}, u32[]{:S(2)}, u32[]{:S(2)}) collective-permute-start(f32[16,768]{1,0:T(8,128)S(1)} %add.106), channel_id=1, source_target_pairs={{0,2},{1,3},{2,0},{3,1},{4,6},{5,7},{6,4},{7,5},{8,10},{9,11},{10,... | collective-permute-start | bytes 147464 | tf_op jit(solution)/shard_map/ppermute | solution.py:48
  181.6 8.7 %collective-permute-start.50 = (bf16[96,768]{0,1:T(8,128)(2,1)S(1)}, bf16[96,768]{0,1:T(8,128)(2,1)S(1)}, u32[]{:S(2)}, u32[]{:S(2)}) collective-permute-start(bf16[96,768]{0,1:T(8,128)(2,1)S(1)} %bitcast.67), channel_id=1, source_target_pairs={{0,0},{1,2},{2,4},{3,6},{4,1},{5,3},{6,5},{7,7},{8,8},{9,10},{10,1... | collective-permute-start | bytes 442376 | tf_op jit(solution)/shard_map/ppermute | solution.py:48
  182.5 14.1 %collective-permute-start.51 = (bf16[96,768]{0,1:T(8,128)(2,1)S(1)}, bf16[96,768]{0,1:T(8,128)(2,1)S(1)}, u32[]{:S(2)}, u32[]{:S(2)}) collective-permute-start(bf16[96,768]{0,1:T(8,128)(2,1)S(1)} %bitcast.68), channel_id=1, source_target_pairs={{0,4},{1,6},{2,0},{3,2},{4,5},{5,7},{6,1},{7,3},{8,12},{9,14},{10,... | collective-permute-start | bytes 442376 | tf_op jit(solution)/shard_map/ppermute | solution.py:48
  (26 other events, 143.0 us)
